TPU v7x, 32 devices: a whole 2x2x4 slice. The times are simulated.
32 devices in a mesh: groups: 2 (over x), epoch: 16 (over z, y, core).
Axes of the slice: x: 2, y: 2, z: 4, core: 2. Of those that a mesh axis runs over, the one named last changes fastest.
Arguments:
- science: bfloat16 [32, 256, 384], P(('groups', 'epoch')), parts along dimension 0, may hold values from -6 to 6
- template: bfloat16 [512, 384], P(('groups', 'epoch')), parts along dimension 0, may hold values from -6 to 6
- kernels: bfloat16 [16, 21, 21], replicated, may hold values from -0.25 to 0.25
- coef: float32 [32, 8, 16], P(('groups', 'epoch')), parts along dimension 0, may hold values from -1.5 to 1.5
- grid_index: int32 [32, 2, 3], P(('groups', 'epoch')), parts along dimension 0, may hold values from 0 to 7
- clip_mask: int32 [32, 256, 384], P('groups', 'epoch'), parts along dimension 0, may hold values 0 or 1
- inv_var: bfloat16 [32, 256, 384], P('groups', 'epoch'), parts along dimension 0, may hold values from 0.25 to 4
Outputs:
- significance: float32 [512, 384], P(('groups', 'epoch')), parts along dimension 0
There are 2 independent parts, one for each index of `groups`. A program takes and returns all parts, laid end to end along the dimension named above; an argument that names none is the same for every part. Nothing has to cross between parts.
All inputs are finite; a program needn't handle non-finite values. No bound on the sum of `clip_mask` on one device may be relied on, other than what follows from the above.
Results may differ from a plain program's by a relative error of at most 0.0039.
Values may be sent and summed in bfloat16 or wider, within the bound.
No kernel may reach another device: no remote copies, remote signals or barrier semaphores. Data moves between devices by JAX's collectives and lax.ppermute only.
A program may use at most 128 MiB of HBM per device.

v0:
```python
import functools

import jax
import jax.numpy as jnp
from jax import lax
from jax.experimental import pallas as pl
from jax.experimental.pallas import tpu as pltpu
from jax.sharding import PartitionSpec as P

CELL = 128
ITERS = 3
LANES = 128
SUB = 8
TILE = 16
VMEM_LIMIT = 16 * 1024 * 1024


def up(value, unit):
    return -(-value // unit) * unit


def tree_sum(items):
    items = list(items)
    while len(items) > 1:
        items = [
            items[i] + items[i + 1] if i + 1 < len(items) else items[i]
            for i in range(0, len(items), 2)
        ]
    return items[0]


def pack_kernel(rows, science, coef, grid_index, out, spread):
    height, width = science.shape[1:]
    columns = width // CELL
    basis = coef.shape[2]
    spread[...] = jnp.zeros(spread.shape, jnp.float32)
    spread[:, :basis] = coef[0]
    tail = out.shape[1] - columns * rows
    for cell_row in range(grid_index.shape[1]):
        picked = [
            spread[pl.ds(grid_index[0, cell_row, c], 1), :] for c in range(columns)
        ]
        block = jnp.concatenate(
            picked + [jnp.zeros((tail - columns, LANES), jnp.float32)], axis=0
        )
        first = block.astype(jnp.bfloat16).astype(jnp.float32)
        rest = block - first
        second = rest.astype(jnp.bfloat16).astype(jnp.float32)
        third = rest - second
        block = first + pltpu.roll(second, basis, 1) + pltpu.roll(third, 2 * basis, 1)
        block = block.astype(jnp.bfloat16)
        for d in range(cell_row * CELL // rows, (cell_row + 1) * CELL // rows):
            out[d, columns * rows :, :] = block
    for d in range(height // rows):
        for c in range(columns):
            out[d, c * rows : (c + 1) * rows, :] = science[
                0, d * rows : (d + 1) * rows, c * CELL : (c + 1) * CELL
            ]


def pack(science, coef, grid_index, rows):
    height, width = science.shape[1:]
    columns = width // CELL
    return pl.pallas_call(
        functools.partial(pack_kernel, rows),
        out_shape=jax.ShapeDtypeStruct(
            (height // rows, columns * rows + TILE, LANES), jnp.bfloat16
        ),
        in_specs=[
            pl.BlockSpec(memory_space=pltpu.VMEM),
            pl.BlockSpec(memory_space=pltpu.VMEM),
            pl.BlockSpec(memory_space=pltpu.SMEM),
        ],
        scratch_shapes=[pltpu.VMEM((up(coef.shape[1], SUB), LANES), jnp.float32)],
        compiler_params=pltpu.CompilerParams(vmem_limit_bytes=VMEM_LIMIT),
        cost_estimate=pl.CostEstimate(flops=0, bytes_accessed=500_000, transcendentals=0),
    )(science, coef, grid_index)


def basis_kernel(slot, kernels, own, pair, other, out, image, taps, turned, left, right):
    count, side, _ = kernels.shape
    half = side // 2
    rows, width = own.shape
    span = image.shape[1]
    odd = lax.rem(lax.axis_index("epoch"), 2) == 1
    image[...] = jnp.zeros(image.shape, jnp.float32)
    below = pair[...].astype(jnp.float32)
    above = other[...].astype(jnp.float32)
    low = jnp.where(odd, below, above)
    high = jnp.where(odd, above, below)
    image[:half, :width] = low[rows - half :, :]
    image[half : half + rows, :width] = own[...].astype(jnp.float32)
    image[half + rows : 2 * half + rows, :width] = high[:half, :]
    image[...] = pltpu.roll(image[...], (span + half + 1 - slot) % span, 1)
    taps[...] = jnp.zeros(taps.shape, jnp.float32)
    taps[:, :side, :side] = kernels[...].astype(jnp.float32)
    flip = (
        lax.broadcasted_iota(jnp.int32, (LANES, LANES), 0)
        + lax.broadcasted_iota(jnp.int32, (LANES, LANES), 1)
        == slot - 1
    )
    flat = taps[...].reshape(count * taps.shape[1], LANES).astype(jnp.bfloat16)
    turned[...] = jnp.dot(
        flat, flip.astype(jnp.bfloat16), preferred_element_type=jnp.float32
    ).reshape(turned.shape)
    per = LANES // slot
    lines = [turned[:, u, :] for u in range(side)]
    left[...] = jnp.zeros(left.shape, jnp.bfloat16)
    for phase in range(min(per, rows)):
        chunks = {}
        for u in range(side):
            chunk, place = divmod(u + phase, per)
            line = lines[u] if place == 0 else pltpu.roll(lines[u], place * slot, 1)
            chunks[chunk] = line if chunk not in chunks else chunks[chunk] + line
        for y in range(phase, rows, per):
            for chunk, value in chunks.items():
                at = (y // per + chunk) * LANES
                left[y * count : (y + 1) * count, at : at + LANES] = value.astype(jnp.bfloat16)
    for row in range(rows + 2 * half):
        line = jnp.broadcast_to(image[row : row + 1, :], (slot, span))
        moved = pltpu.roll(line, 0, 1, stride=1, stride_axis=0)
        right[row * slot : (row + 1) * slot, :] = moved[:, :width].astype(jnp.bfloat16)
    out[...] = jnp.dot(
        left[...], right[...], preferred_element_type=jnp.float32
    ).astype(jnp.bfloat16)


def basis_rows(kernels, own, pair, other):
    count, side, _ = kernels.shape
    rows, width = own.shape
    slot = up(side, 32)
    lines = rows + side - 1
    span = up(width + side, LANES)
    depth = up(lines * slot, LANES)
    return pl.pallas_call(
        functools.partial(basis_kernel, slot),
        out_shape=jax.ShapeDtypeStruct((rows * count, width), jnp.bfloat16),
        scratch_shapes=[
            pltpu.VMEM((up(lines, SUB), span), jnp.float32),
            pltpu.VMEM((count, up(side, SUB), LANES), jnp.float32),
            pltpu.VMEM((count, up(side, SUB), LANES), jnp.float32),
            pltpu.VMEM((rows * count, depth), jnp.bfloat16),
            pltpu.VMEM((depth, width), jnp.bfloat16),
        ],
        compiler_params=pltpu.CompilerParams(vmem_limit_bytes=VMEM_LIMIT),
        cost_estimate=pl.CostEstimate(
            flops=2 * rows * count * depth * width, bytes_accessed=600_000, transcendentals=0
        ),
    )(kernels, own, pair, other)


def stack_kernel(count, blocks, basis, clip_mask, inv_var, out, model):
    epochs, rows, width = clip_mask.shape
    columns = width // CELL
    parts = rows // SUB
    depth = SUB * count
    lane = lax.broadcasted_iota(jnp.int32, (SUB, LANES), 1)
    line = lax.broadcasted_iota(jnp.int32, (SUB, LANES), 0)
    diagonal = (lane >= line * count) & (lane < (line + 1) * count)
    spread = []
    for e in range(epochs):
        tail = blocks[e, columns * rows :, :].astype(jnp.float32)[:SUB]
        terms = []
        for term in range(3):
            value = tail if term == 0 else pltpu.roll(tail, LANES - term * count, 1)
            value = jnp.where(lane < count, value, 0.0)
            step = count
            while step < LANES:
                value = value + pltpu.roll(value, step, 1)
                step *= 2
            terms.append(value)
        spread.append(terms)
    for c in range(columns):
        at = slice(c * CELL, (c + 1) * CELL)
        weights = jnp.concatenate(
            [
                jnp.concatenate(
                    [
                        jnp.where(
                            diagonal,
                            jnp.broadcast_to(spread[e][term][c : c + 1], (SUB, LANES)),
                            0.0,
                        )
                        for e in range(epochs)
                    ],
                    axis=0,
                ).astype(jnp.bfloat16)
                for term in range(3)
            ],
            axis=1,
        )
        planes = jnp.concatenate(
            [basis[p * depth : (p + 1) * depth, at] for p in range(parts)], axis=1
        )
        model[...] = jnp.dot(
            weights, jnp.concatenate([planes] * 3, axis=0), preferred_element_type=jnp.float32
        )
        for p in range(parts):
            top = slice(p * SUB, (p + 1) * SUB)
            values, weight_iv, base = [], [], []
            for e in range(epochs):
                science = blocks[e, c * rows : (c + 1) * rows, :].astype(jnp.float32)[top]
                difference = science - model[e * SUB : (e + 1) * SUB, p * CELL : (p + 1) * CELL]
                values.append(difference.astype(jnp.bfloat16).astype(jnp.float32))
                iv = inv_var[e, :, at].astype(jnp.float32)[top]
                weight_iv.append(iv)
                base.append(clip_mask[e, top, at].astype(jnp.float32) * iv)
            num = tree_sum(b * v for b, v in zip(base, values))
            den = tree_sum(base)
            mean = num / (1.0 + den)
            for sweep in range(ITERS):
                weight = []
                for e in range(epochs):
                    resid = values[e] - mean
                    weight.append(base[e] / (1.0 + weight_iv[e] * resid * resid))
                num = tree_sum(w * v for w, v in zip(weight, values))
                den = tree_sum(weight)
                mean = num / (1.0 + den)
            out[top, at] = num / jnp.sqrt(1.0 + den)


def stack(count, blocks, basis, clip_mask, inv_var):
    epochs, rows, width = clip_mask.shape
    return pl.pallas_call(
        functools.partial(stack_kernel, count),
        out_shape=jax.ShapeDtypeStruct((rows, width), jnp.float32),
        scratch_shapes=[pltpu.VMEM((epochs * SUB, rows // SUB * CELL), jnp.float32)],
        compiler_params=pltpu.CompilerParams(vmem_limit_bytes=VMEM_LIMIT),
        cost_estimate=pl.CostEstimate(
            flops=100 * epochs * rows * width, bytes_accessed=10**6, transcendentals=0
        ),
    )(blocks, basis, clip_mask, inv_var)


def local(science, template, kernels, coef, grid_index, clip_mask, inv_var):
    rows = template.shape[0]
    count = lax.axis_size("epoch")
    blocks = pack(science, coef, grid_index, rows)
    blocks = lax.all_to_all(blocks, "epoch", split_axis=0, concat_axis=0, tiled=True)
    pair = lax.ppermute(template, "epoch", [(i, i ^ 1) for i in range(count)])
    swap = [(i, i + 1) for i in range(1, count - 1, 2)]
    other = lax.ppermute(template, "epoch", swap + [(b, a) for a, b in swap])
    basis = basis_rows(kernels, template, pair, other)
    return stack(kernels.shape[0], blocks, basis, clip_mask, inv_var)


def solution(mesh):
    return jax.shard_map(
        local,
        mesh=mesh,
        in_specs=(
            P(("groups", "epoch"), None, None),
            P(("groups", "epoch"), None),
            P(),
            P(("groups", "epoch"), None, None),
            P(("groups", "epoch"), None, None),
            P("groups", "epoch", None),
            P("groups", "epoch", None),
        ),
        out_specs=P(("groups", "epoch"), None),
        check_vma=False,
    )
```

profile of v0, /device:TPU:0, one launch (start us, length us, event | category | flops | bytes accessed | tf_op | source)
XLA Modules:
  0.0 22.8 jit_solution(6686782550253737666)
XLA Ops:
  0.0 0.0 copy-start.1
  0.0 0.9 %copy-done.1 = bf16[1,256,384]{2,1,0:T(8,128)(2,1)S(1)} copy-done((bf16[1,256,384]{2,1,0:T(8,128)(2,1)S(1)}, bf16[1,256,384]{2,1,0:T(8,128)(2,1)}, u32[]{:S(2)}) %copy-start.1) | copy-done | bytes 196632
  0.9 0.0 copy-start.3
  0.9 0.7 %copy-done.3 = f32[1,8,16]{2,1,0:T(8,128)S(1)} copy-done((f32[1,8,16]{2,1,0:T(8,128)S(1)}, f32[1,8,16]{2,1,0:T(8,128)}, u32[]{:S(2)}) %copy-start.3) | copy-done | bytes 536
  1.6 0.0 copy-start.4
  1.6 0.7 %copy-done.4 = s32[1,2,3]{2,1,0:T(2,128)S(1)} copy-done((s32[1,2,3]{2,1,0:T(2,128)S(1)}, s32[1,2,3]{2,1,0:T(2,128)}, u32[]{:S(2)}) %copy-start.4) | copy-done | bytes 48
  2.3 1.4 %shard_map.73 = bf16[16,64,128]{2,1,0:T(8,128)(2,1)} custom-call(bf16[1,256,384]{2,1,0:T(8,128)(2,1)S(1)} %copy-done.1, f32[1,8,16]{2,1,0:T(8,128)S(1)} %copy-done.3, s32[1,2,3]{2,1,0:T(2,128)S(1)} %copy-done.4), custom_call_target="tpu_custom_call" | custom-call | bytes 500000 | tf_op jit(solution)/shard_map/pallas_call | solution.py:64
  3.6 0.0 copy-start.5
  3.7 0.0 copy-start.6
  3.7 7.5 %all-to-all-start = ((bf16[16,64,128]{2,1,0:T(8,128)(2,1)}), bf16[16,64,128]{2,1,0:T(8,128)(2,1)S(1)}, u32[]{:S(2)}, u32[]{:S(2)}) async-start(bf16[16,64,128]{2,1,0:T(8,128)(2,1)} %shard_map.73), calls=%async_computation | async-start | bytes 524288 | tf_op jit(solution)/shard_map/all_to_all | solution.py:239
  11.2 0.0 copy-done.5
  11.2 0.5 %collective-permute-start = (bf16[16,384]{1,0:T(8,128)(2,1)S(1)}, bf16[16,384]{1,0:T(8,128)(2,1)S(1)}, u32[]{:S(2)}, u32[]{:S(2)}) collective-permute-start(bf16[16,384]{1,0:T(8,128)(2,1)S(1)} %copy-done.5), channel_id=1, source_target_pairs={{0,1},{1,0},{2,3},{3,2},{4,5},{5,4},{6,7},{7,6},{8,9},{9,8},{10,11... | collective-permute-start | bytes 36872 | tf_op jit(solution)/shard_map/ppermute | solution.py:240
  11.7 0.7 %collective-permute-start.1 = (bf16[16,384]{1,0:T(8,128)(2,1)S(1)}, bf16[16,384]{1,0:T(8,128)(2,1)S(1)}, u32[]{:S(2)}, u32[]{:S(2)}) collective-permute-start(bf16[16,384]{1,0:T(8,128)(2,1)S(1)} %copy-done.5), channel_id=1, source_target_pairs={{1,2},{3,4},{5,6},{7,8},{9,10},{11,12},{13,14},{2,1},{4,3},{6,5},{... | collective-permute-start | bytes 36872 | tf_op jit(solution)/shard_map/ppermute | solution.py:242
  12.3 0.0 copy-done.6
  12.4 0.0 copy-start
  12.4 0.0 copy-start.2
  12.4 0.1 collective-permute-done.pair
  12.5 0.0 collective-permute-done.1.other
  12.5 0.9 %shard_map.74.basis = bf16[256,384]{1,0:T(8,128)(2,1)S(1)} custom-call(bf16[16,21,21]{2,1,0:T(8,128)(2,1)S(1)} %copy.8.kernels, bf16[16,384]{1,0:T(8,128)(2,1)S(1)} %copy-done.5, bf16[16,384]{1,0:T(8,128)(2,1)S(1)} %collective-permute-done.pair, bf16[16,384]{1,0:T(8,128)(2,1)S(1)} %collective-permute-done.1.other), custom_call_target="tpu_custom_call" | custom-call | flops 226492416 | bytes 600000 | tf_op jit(solution)/shard_map/pallas_call | solution.py:135
  13.4 7.8 %all-to-all-done.blocks = bf16[16,64,128]{2,1,0:T(8,128)(2,1)S(1)} async-done(((bf16[16,64,128]{2,1,0:T(8,128)(2,1)}), bf16[16,64,128]{2,1,0:T(8,128)(2,1)S(1)}, u32[]{:S(2)}, u32[]{:S(2)}) %all-to-all-start) | async-done | bytes 262176 | tf_op jit(solution)/shard_map/all_to_all | solution.py:239
  21.2 0.0 copy-done
  21.2 0.0 copy-done.2
  21.2 1.5 %shard_map.75 = f32[16,384]{1,0:T(8,128)} custom-call(bf16[16,64,128]{2,1,0:T(8,128)(2,1)S(1)} %all-to-all-done.blocks, bf16[256,384]{1,0:T(8,128)(2,1)S(1)} %shard_map.74.basis, s32[16,16,384]{2,1,0:T(8,128)S(1)} %copy-done, bf16[16,16,384]{2,1,0:T(8,128)(2,1)S(1)} %copy-done.2), custom_call_target="tpu_custom_call" | custom-call | flops 9830400 | bytes 1000000 | tf_op jit(solution)/shard_map/pallas_call | solution.py:224
  (1 shorter events, 0.0 us)
Async XLA Ops:
  0.0 0.9 %copy-start.1 = (bf16[1,256,384]{2,1,0:T(8,128)(2,1)S(1)}, bf16[1,256,384]{2,1,0:T(8,128)(2,1)}, u32[]{:S(2)}) copy-start(bf16[1,256,384]{2,1,0:T(8,128)(2,1)} %science.1) | copy-start | bytes 589828
  0.9 0.7 %copy-start.3 = (f32[1,8,16]{2,1,0:T(8,128)S(1)}, f32[1,8,16]{2,1,0:T(8,128)}, u32[]{:S(2)}) copy-start(f32[1,8,16]{2,1,0:T(8,128)} %coef.1) | copy-start | bytes 1540
  1.6 0.7 %copy-start.4 = (s32[1,2,3]{2,1,0:T(2,128)S(1)}, s32[1,2,3]{2,1,0:T(2,128)}, u32[]{:S(2)}) copy-start(s32[1,2,3]{2,1,0:T(2,128)} %grid_index.1) | copy-start | bytes 76
  3.6 7.5 %copy-start.5 = (bf16[16,384]{1,0:T(8,128)(2,1)S(1)}, bf16[16,384]{1,0:T(8,128)(2,1)}, u32[]{:S(2)}) copy-start(bf16[16,384]{1,0:T(8,128)(2,1)} %own.1) | copy-start | bytes 36868
  3.7 8.7 %copy-start.6 = (bf16[16,21,21]{2,0,1:T(8,128)(2,1)S(1)}, bf16[16,21,21]{2,0,1:T(8,128)(2,1)}, u32[]{:S(2)}) copy-start(bf16[16,21,21]{2,0,1:T(8,128)(2,1)} %param.9) | copy-start | bytes 42340
  3.7 17.6 %all-to-all-start = ((bf16[16,64,128]{2,1,0:T(8,128)(2,1)}), bf16[16,64,128]{2,1,0:T(8,128)(2,1)S(1)}, u32[]{:S(2)}, u32[]{:S(2)}) async-start(bf16[16,64,128]{2,1,0:T(8,128)(2,1)} %shard_map.73), calls=%async_computation | async-start | bytes 524288 | tf_op jit(solution)/shard_map/all_to_all | solution.py:239
  11.2 1.3 %collective-permute-start = (bf16[16,384]{1,0:T(8,128)(2,1)S(1)}, bf16[16,384]{1,0:T(8,128)(2,1)S(1)}, u32[]{:S(2)}, u32[]{:S(2)}) collective-permute-start(bf16[16,384]{1,0:T(8,128)(2,1)S(1)} %copy-done.5), channel_id=1, source_target_pairs={{0,1},{1,0},{2,3},{3,2},{4,5},{5,4},{6,7},{7,6},{8,9},{9,8},{10,11... | collective-permute-start | bytes 36872 | tf_op jit(solution)/shard_map/ppermute | solution.py:240
  11.7 0.8 %collective-permute-start.1 = (bf16[16,384]{1,0:T(8,128)(2,1)S(1)}, bf16[16,384]{1,0:T(8,128)(2,1)S(1)}, u32[]{:S(2)}, u32[]{:S(2)}) collective-permute-start(bf16[16,384]{1,0:T(8,128)(2,1)S(1)} %copy-done.5), channel_id=1, source_target_pairs={{1,2},{3,4},{5,6},{7,8},{9,10},{11,12},{13,14},{2,1},{4,3},{6,5},{... | collective-permute-start | bytes 36872 | tf_op jit(solution)/shard_map/ppermute | solution.py:242
  12.4 8.9 %copy-start = (s32[16,16,384]{2,1,0:T(8,128)S(1)}, s32[16,16,384]{2,1,0:T(8,128)}, u32[]{:S(2)}) copy-start(s32[16,16,384]{2,1,0:T(8,128)} %clip_mask.1) | copy-start | bytes 1179652
  12.4 8.9 %copy-start.2 = (bf16[16,16,384]{2,1,0:T(8,128)(2,1)S(1)}, bf16[16,16,384]{2,1,0:T(8,128)(2,1)}, u32[]{:S(2)}) copy-start(bf16[16,16,384]{2,1,0:T(8,128)(2,1)} %inv_var.1) | copy-start | bytes 589828
where the time goes:
time: 23.1 us; the launch traced here: 22.8 us
  starting transfers between devices  8.64 us (37%)
  waiting for transfers between devices  7.9 us (34%)
  Pallas kernels  3.83 us (17%)
  local copies, waits for them, and re-layouts  2.34 us (10%)
    all_to_all x1, waiting for transfers between devices, local(): lax.all_to_all(blocks, 'epoch', split_axis=0, concat_axis=0, tiled=True)  7.79 us
    all_to_all x1, starting transfers between devices, local(): lax.all_to_all(blocks, 'epoch', split_axis=0, concat_axis=0, tiled=True)  7.52 us
    unnamed x15, local copies, waits for them, and re-layouts  2.34 us
    pallas_call x1, Pallas kernels, stack(): pl.pallas_call(functools.partial(stack_kernel, count), out_shape=jax.Shap...  1.54 us
    pallas_call x1, Pallas kernels, pack(): pl.pallas_call(functools.partial(pack_kernel, rows), out_shape=jax.ShapeD...  1.35 us
    pallas_call x1, Pallas kernels, basis_rows(): pl.pallas_call(functools.partial(basis_kernel, slot), out_shape=jax.Shape...  0.93 us
    ppermute x1, starting transfers between devices, local(): other = lax.ppermute(template, 'epoch', swap + [(b, a) for a, b in swap])  0.65 us
    ppermute x1, starting transfers between devices, local(): pair = lax.ppermute(template, 'epoch', [(i, i ^ 1) for i in range(count)])  0.47 us
  transfers between devices with their start and end apart: 3, of which 2 were waited for; matrix products, arithmetic and copies ran while one was open for 0% of the time, Pallas kernels for 4%

commit v1 on v0

v1 whole, which is shorter than its diff:
```python
import functools

import jax
import jax.numpy as jnp
from jax import lax
from jax.experimental import pallas as pl
from jax.experimental.pallas import tpu as pltpu
from jax.sharding import PartitionSpec as P

CELL = 128
ITERS = 3
LANES = 128
SUB = 8
TILE = 16
VMEM_LIMIT = 16 * 1024 * 1024


def up(value, unit):
    return -(-value // unit) * unit


def tree_sum(items):
    items = list(items)
    while len(items) > 1:
        items = [
            items[i] + items[i + 1] if i + 1 < len(items) else items[i]
            for i in range(0, len(items), 2)
        ]
    return items[0]


def pack_kernel(fast, science, template, coef, grid_index, *refs):
    blocks = refs[:fast]
    spread, cells, sems, small = refs[fast:]
    rows, width = template.shape
    columns = width // CELL
    slow = science.shape[0]
    basis = coef.shape[1]
    here = lax.rem(lax.axis_index("epoch"), fast)
    cell_copy = pltpu.make_async_copy(grid_index, cells, small.at[0])
    coef_copy = pltpu.make_async_copy(coef, spread, small.at[1])
    cell_copy.start()
    coef_copy.start()
    moves = []
    for c in range(columns):
        at = slice(c * CELL, (c + 1) * CELL)
        for k in range(fast):
            moves.append(
                pltpu.make_async_copy(
                    science.at[:, here ^ k, :, at],
                    blocks[k].at[c * slow : (c + 1) * slow],
                    sems.at[k, c],
                )
            )
        moves.append(
            pltpu.make_async_copy(
                template.at[:, at], blocks[1].at[blocks[1].shape[0] - columns + c], small.at[2 + c]
            )
        )
    for move in moves:
        move.start()
    cell_copy.wait()
    coef_copy.wait()
    picked = [
        spread[pl.ds(cells[r, c], 1), :] for r in range(cells.shape[0]) for c in range(columns)
    ]
    size = up(len(picked), rows)
    if size > len(picked):
        picked.append(jnp.zeros((size - len(picked), basis), jnp.float32))
    table = jnp.concatenate(picked, axis=0)
    table = jnp.concatenate([table, jnp.zeros((size, LANES - basis), jnp.float32)], axis=1)
    first = table.astype(jnp.bfloat16).astype(jnp.float32)
    rest = table - first
    second = rest.astype(jnp.bfloat16).astype(jnp.float32)
    third = rest - second
    table = first + pltpu.roll(second, basis, 1) + pltpu.roll(third, 2 * basis, 1)
    table = table.astype(jnp.bfloat16)
    for k in range(fast):
        for g in range(size // rows):
            blocks[k][columns * slow + g] = table[g * rows : (g + 1) * rows]
    for move in moves:
        move.wait()


def pack(science, template, coef, grid_index, fast):
    rows, width = template.shape
    slow = science.shape[1] // rows // fast
    columns = width // CELL
    groups = slow * columns + up(grid_index.shape[1] * columns, rows) // rows
    shapes = [
        jax.ShapeDtypeStruct(
            (groups + (columns if k == 1 else 0), rows, LANES), jnp.bfloat16
        )
        for k in range(fast)
    ]
    return pl.pallas_call(
        functools.partial(pack_kernel, fast),
        out_shape=shapes,
        in_specs=[pl.BlockSpec(memory_space=pltpu.HBM)] * 4,
        out_specs=[pl.BlockSpec(memory_space=pltpu.VMEM)] * fast,
        scratch_shapes=[
            pltpu.VMEM(coef.shape[1:], jnp.float32),
            pltpu.SMEM(grid_index.shape[1:], jnp.int32),
            pltpu.SemaphoreType.DMA((fast, columns)),
            pltpu.SemaphoreType.DMA((2 + columns,)),
        ],
        compiler_params=pltpu.CompilerParams(vmem_limit_bytes=VMEM_LIMIT),
        cost_estimate=pl.CostEstimate(flops=0, bytes_accessed=500_000, transcendentals=0),
    )(science.reshape(slow, fast, rows, width), template, coef[0], grid_index[0])


def route_kernel(fast, slow, columns, *refs):
    held, sent, tails = refs[:fast], refs[fast : fast + slow], refs[fast + slow]
    rows = held[0].shape[1]
    me = lax.axis_index("epoch")
    across, here = lax.div(me, fast), lax.rem(me, fast)
    span = tails.shape[1] // rows
    for j in range(fast):
        for g in range(span):
            tails[j, g * rows : (g + 1) * rows] = held[j][columns * slow + g].astype(jnp.float32)
    for k in range(slow):
        to = across ^ k
        for j in range(fast):
            for c in range(columns):
                sent[k][j * columns + c] = held[j][c * slow + to]
        cell_row = lax.div((to * fast + here) * rows, CELL)
        picked = [
            tails[j, pl.ds(cell_row * columns + c, 1), :]
            for j in range(fast)
            for c in range(columns)
        ]
        size = up(len(picked), rows)
        if size > len(picked):
            picked.append(jnp.zeros((size - len(picked), LANES), jnp.float32))
        table = jnp.concatenate(picked, axis=0).astype(jnp.bfloat16)
        for g in range(size // rows):
            sent[k][fast * columns + g] = table[g * rows : (g + 1) * rows]


def route(held, slow, columns):
    fast = len(held)
    rows = held[0].shape[1]
    groups = fast * columns + up(fast * columns, rows) // rows
    tail = (held[0].shape[0] - slow * columns) * rows
    return pl.pallas_call(
        functools.partial(route_kernel, fast, slow, columns),
        out_shape=[jax.ShapeDtypeStruct((groups, rows, LANES), jnp.bfloat16)] * slow,
        scratch_shapes=[pltpu.VMEM((fast, tail, LANES), jnp.float32)],
        compiler_params=pltpu.CompilerParams(vmem_limit_bytes=VMEM_LIMIT),
        cost_estimate=pl.CostEstimate(flops=0, bytes_accessed=500_000, transcendentals=0),
    )(*held)


def basis_kernel(slot, kernels, own, pair, other, out, image, left, right):
    side, count, _ = kernels.shape
    half = side // 2
    rows, width = own.shape
    span = image.shape[1]
    odd = lax.rem(lax.axis_index("epoch"), 2) == 1
    image[...] = jnp.zeros(image.shape, jnp.float32)
    columns = width // CELL
    near = [pair[pair.shape[0] - columns + c].astype(jnp.float32) for c in range(columns)]
    near = jnp.concatenate(near, axis=1)
    far = other[...].astype(jnp.float32)
    low = jnp.where(odd, near, far)
    high = jnp.where(odd, far, near)
    image[:half, :width] = low[rows - half :, :]
    image[half : half + rows, :width] = own[...].astype(jnp.float32)
    image[half + rows : 2 * half + rows, :width] = high[:half, :]
    image[...] = pltpu.roll(image[...], (span + half + 1 - slot) % span, 1)
    flip = (
        lax.broadcasted_iota(jnp.int32, (side, LANES), 0)
        + lax.broadcasted_iota(jnp.int32, (side, LANES), 1)
        == slot - 1
    ).astype(jnp.float32).astype(jnp.bfloat16)
    per = LANES // slot
    lines = [
        jnp.dot(kernels[u], flip, preferred_element_type=jnp.float32) for u in range(side)
    ]
    left[...] = jnp.zeros(left.shape, jnp.bfloat16)
    for phase in range(min(per, rows)):
        chunks = {}
        for u in range(side):
            chunk, place = divmod(u + phase, per)
            line = lines[u] if place == 0 else pltpu.roll(lines[u], place * slot, 1)
            chunks[chunk] = line if chunk not in chunks else chunks[chunk] + line
        for y in range(phase, rows, per):
            for chunk, value in chunks.items():
                at = (y // per + chunk) * LANES
                left[y * count : (y + 1) * count, at : at + LANES] = value.astype(jnp.bfloat16)
    for row in range(rows + 2 * half):
        line = jnp.broadcast_to(image[row : row + 1, :], (slot, span))
        moved = pltpu.roll(line, 0, 1, stride=1, stride_axis=0)
        right[row * slot : (row + 1) * slot, :] = moved[:, :width].astype(jnp.bfloat16)
    out[...] = jnp.dot(
        left[...], right[...], preferred_element_type=jnp.float32
    ).astype(jnp.bfloat16)


def basis_rows(kernels, own, pair, other):
    count, side, _ = kernels.shape
    rows, width = own.shape
    slot = up(side, 32)
    lines = rows + side - 1
    span = up(width + side, LANES)
    depth = up(lines * slot, LANES)
    return pl.pallas_call(
        functools.partial(basis_kernel, slot),
        out_shape=jax.ShapeDtypeStruct((rows * count, width), jnp.bfloat16),
        scratch_shapes=[
            pltpu.VMEM((up(lines, SUB), span), jnp.float32),
            pltpu.VMEM((rows * count, depth), jnp.bfloat16),
            pltpu.VMEM((depth, width), jnp.bfloat16),
        ],
        compiler_params=pltpu.CompilerParams(vmem_limit_bytes=VMEM_LIMIT),
        cost_estimate=pl.CostEstimate(
            flops=2 * rows * count * depth * width, bytes_accessed=600_000, transcendentals=0
        ),
    )(kernels.transpose(1, 0, 2), own, pair, other)


def stack_kernel(count, fast, *refs):
    slow = len(refs) - 5
    blocks = refs[:slow]
    basis, clip_mask, inv_var, out, model = refs[slow:]
    epochs, rows, width = clip_mask.shape
    columns = width // CELL
    parts = rows // SUB
    depth = SUB * count
    lane = lax.broadcasted_iota(jnp.int32, (SUB, LANES), 1)
    line = lax.broadcasted_iota(jnp.int32, (SUB, LANES), 0)
    diagonal = (lane >= line * count) & (lane < (line + 1) * count)
    me = lax.axis_index("epoch")
    across, here = lax.div(me, fast), lax.rem(me, fast)
    order, spread = [], []
    for k in range(slow):
        tail = jnp.concatenate(
            [blocks[k][g].astype(jnp.float32) for g in range(fast * columns, blocks[k].shape[0])],
            axis=0,
        )
        own_lane = lax.broadcasted_iota(jnp.int32, tail.shape, 1) < count
        terms = []
        for term in range(3):
            value = tail if term == 0 else pltpu.roll(tail, LANES - term * count, 1)
            value = jnp.where(own_lane, value, 0.0)
            step = count
            while step < LANES:
                value = value + pltpu.roll(value, step, 1)
                step *= 2
            terms.append(value)
        for j in range(fast):
            order.append((k, j, (across ^ k) * fast + (here ^ j)))
            spread.append([value[j * columns : (j + 1) * columns] for value in terms])
    for c in range(columns):
        at = slice(c * CELL, (c + 1) * CELL)
        weights = jnp.concatenate(
            [
                jnp.concatenate(
                    [
                        jnp.where(
                            diagonal,
                            jnp.broadcast_to(spread[e][term][c : c + 1], (SUB, LANES)),
                            0.0,
                        )
                        for e in range(epochs)
                    ],
                    axis=0,
                ).astype(jnp.bfloat16)
                for term in range(3)
            ],
            axis=1,
        )
        planes = jnp.concatenate(
            [basis[p * depth : (p + 1) * depth, at] for p in range(parts)], axis=1
        )
        model[...] = jnp.dot(
            weights, jnp.concatenate([planes] * 3, axis=0), preferred_element_type=jnp.float32
        )
        for p in range(parts):
            top = slice(p * SUB, (p + 1) * SUB)
            values, weight_iv, base = [], [], []
            for e in range(epochs):
                k, j, epoch = order[e]
                science = blocks[k][j * columns + c].astype(jnp.float32)[top]
                difference = science - model[e * SUB : (e + 1) * SUB, p * CELL : (p + 1) * CELL]
                values.append(difference.astype(jnp.bfloat16).astype(jnp.float32))
                iv = inv_var[epoch, :, at].astype(jnp.float32)[top]
                weight_iv.append(iv)
                base.append(clip_mask[epoch, top, at].astype(jnp.float32) * iv)
            num = tree_sum(b * v for b, v in zip(base, values))
            den = tree_sum(base)
            mean = num / (1.0 + den)
            for sweep in range(ITERS):
                weight = []
                for e in range(epochs):
                    resid = values[e] - mean
                    weight.append(base[e] / (1.0 + weight_iv[e] * resid * resid))
                num = tree_sum(w * v for w, v in zip(weight, values))
                den = tree_sum(weight)
                mean = num / (1.0 + den)
            out[top, at] = num / jnp.sqrt(1.0 + den)


def stack(count, fast, blocks, basis, clip_mask, inv_var):
    epochs, rows, width = clip_mask.shape
    return pl.pallas_call(
        functools.partial(stack_kernel, count, fast),
        out_shape=jax.ShapeDtypeStruct((rows, width), jnp.float32),
        scratch_shapes=[pltpu.VMEM((epochs * SUB, rows // SUB * CELL), jnp.float32)],
        compiler_params=pltpu.CompilerParams(vmem_limit_bytes=VMEM_LIMIT),
        cost_estimate=pl.CostEstimate(
            flops=100 * epochs * rows * width, bytes_accessed=10**6, transcendentals=0
        ),
    )(*blocks, basis, clip_mask, inv_var)


def exchange(block, step):
    return lax.ppermute(block, "epoch", [(i, i ^ step) for i in range(lax.axis_size("epoch"))])


def local(science, template, kernels, coef, grid_index, clip_mask, inv_var):
    count = lax.axis_size("epoch")
    fast = 2
    while 4 * fast * fast <= count:
        fast *= 2
    slow = count // fast
    columns = template.shape[1] // CELL
    sent = pack(science, template, coef, grid_index, fast)
    held = [sent[0]] + [exchange(sent[k], k) for k in range(1, fast)]
    swap = [(i, i + 1) for i in range(1, count - 1, 2)]
    other = lax.ppermute(template, "epoch", swap + [(b, a) for a, b in swap])
    sent = route(held, slow, columns)
    blocks = [sent[0]] + [exchange(sent[k], k * fast) for k in range(1, slow)]
    basis = basis_rows(kernels, template, held[1], other)
    return stack(kernels.shape[0], fast, blocks, basis, clip_mask, inv_var)


def solution(mesh):
    return jax.shard_map(
        local,
        mesh=mesh,
        in_specs=(
            P(("groups", "epoch"), None, None),
            P(("groups", "epoch"), None),
            P(),
            P(("groups", "epoch"), None, None),
            P(("groups", "epoch"), None, None),
            P("groups", "epoch", None),
            P("groups", "epoch", None),
        ),
        out_specs=P(("groups", "epoch"), None),
        check_vma=False,
    )
```

time: 23.1 us -> 22.2 us (0.961)
  Pallas kernels: 3.83 us -> 3.32 us
  starting transfers between devices: 8.64 us -> 8.28 us
    all_to_all x1 -> x0, waiting for transfers between devices: 7.79 us -> none  [local(): lax.all_to_all(blocks, 'epoch', split_axis=0, concat_axis=0, tiled=True)]
    ppermute x1 -> x6, waiting for transfers between devices: 0.11 us -> 7.88 us  [exchange(): lax.ppermute(block, 'epoch', [(i, i ^ step) for i in range(lax.axis_size(...]
    all_to_all x1 -> x0, starting transfers between devices: 7.52 us -> none  [local(): lax.all_to_all(blocks, 'epoch', split_axis=0, concat_axis=0, tiled=True)]
    ppermute x1 -> x6, starting transfers between devices: 0.47 us -> 7.63 us  [exchange(): lax.ppermute(block, 'epoch', [(i, i ^ step) for i in range(lax.axis_size(...]
    pallas_call x2 -> x3, Pallas kernels: 2.89 us -> 2.4 us  [the longest x1 1.53 us: stack(): pl.pallas_call(functools.partial(stack_kernel, count, fast), out_shape=ja...]
    unnamed x15 -> x16, local copies, waits for them, and re-layouts: 2.34 us -> 2.35 us
  transfers between devices with their start and end apart: 3 -> 7, of which waited for: 2 -> 4; matrix products, arithmetic and copies ran while one was open for 0% -> 0% of each run, Pallas kernels for 4% -> 4%
where the time goes in v1:
time: 22.2 us; the launch traced here: 21.9 us
  starting transfers between devices  8.28 us (37%)
  waiting for transfers between devices  7.88 us (35%)
  Pallas kernels  3.32 us (15%)
  local copies, waits for them, and re-layouts  2.35 us (11%)
    ppermute x6, waiting for transfers between devices, exchange(): lax.ppermute(block, 'epoch', [(i, i ^ step) for i in range(lax.axis_size(...  7.88 us
    ppermute x6, starting transfers between devices, exchange(): lax.ppermute(block, 'epoch', [(i, i ^ step) for i in range(lax.axis_size(...  7.63 us
    unnamed x16, local copies, waits for them, and re-layouts  2.35 us
    pallas_call x1, Pallas kernels, stack(): pl.pallas_call(functools.partial(stack_kernel, count, fast), out_shape=ja...  1.53 us
    pallas_call x1, Pallas kernels, basis_rows(): pl.pallas_call(functools.partial(basis_kernel, slot), out_shape=jax.Shape...  0.92 us
    pallas_call x1, Pallas kernels, pack(): pl.pallas_call(functools.partial(pack_kernel, fast), out_shape=shapes, in...  0.81 us
    ppermute x1, starting transfers between devices, local(): other = lax.ppermute(template, 'epoch', swap + [(b, a) for a, b in swap])  0.65 us
  transfers between devices with their start and end apart: 7, of which 4 were waited for; matrix products, arithmetic and copies ran while one was open for 0% of the time, Pallas kernels for 4%

profile of v1, /device:TPU:0, one launch (start us, length us, event | category | flops | bytes accessed | tf_op | source)
XLA Modules:
  0.0 21.9 jit_solution(8339737201762489577)
XLA Ops:
  0.0 0.0 copy-start.5
  0.0 0.0 copy-start.6
  0.0 0.7 %copy-done.5 = f32[1,8,16]{2,1,0:T(8,128)S(1)} copy-done((f32[1,8,16]{2,1,0:T(8,128)S(1)}, f32[1,8,16]{2,1,0:T(8,128)}, u32[]{:S(2)}) %copy-start.5) | copy-done | bytes 536
  0.7 0.0 copy-done.6
  0.7 0.0 copy-start.1
  0.7 0.9 %copy-done.1 = bf16[1,256,384]{2,1,0:T(8,128)(2,1)S(1)} copy-done((bf16[1,256,384]{2,1,0:T(8,128)(2,1)S(1)}, bf16[1,256,384]{2,1,0:T(8,128)(2,1)}, u32[]{:S(2)}) %copy-start.1) | copy-done | bytes 196632
  1.6 0.0 copy-start.3
  1.6 0.7 %copy-done.3 = bf16[16,384]{1,0:T(8,128)(2,1)S(1)} copy-done((bf16[16,384]{1,0:T(8,128)(2,1)S(1)}, bf16[16,384]{1,0:T(8,128)(2,1)}, u32[]{:S(2)}) %copy-start.3) | copy-done | bytes 12312
  2.3 0.8 %shard_map.73 = (bf16[13,16,128]{2,1,0:T(8,128)(2,1)S(1)}, bf16[16,16,128]{2,1,0:T(8,128)(2,1)S(1)}, bf16[13,16,128]{2,1,0:T(8,128)(2,1)S(1)}, bf16[13,16,128]{2,1,0:T(8,128)(2,1)S(1)}) custom-call(bf16[4,4,16,384]{3,2,1,0:T(8,128)(2,1)S(1)} %bitcast.4, bf16[16,384]{1,0:T(8,128)(2,1)S(1)} %copy-done.3, f32[8,16]{1,0:T(8,128)S(1)} %bitcast.5, s32[2,3]{1,0:T(2,128)S(1)} %bitcast.6), custom_call_target="tpu_custom_call" | custom-call | bytes 500000 | tf_op jit(solution)/shard_map/pallas_call | solution.py:96
  3.1 0.5 %collective-permute-start = (bf16[16,16,128]{2,1,0:T(8,128)(2,1)S(1)}, bf16[16,16,128]{2,1,0:T(8,128)(2,1)S(1)}, u32[]{:S(2)}, u32[]{:S(2)}) collective-permute-start(bf16[16,16,128]{2,1,0:T(8,128)(2,1)S(1)} %get-tuple-element.14), channel_id=1, source_target_pairs={{0,1},{1,0},{2,3},{3,2},{4,5},{5,4},{6,7},{7,6},{8,9},{9,8},{10,11... | collective-permute-start | bytes 196616 | tf_op jit(solution)/shard_map/ppermute | solution.py:318
  3.7 2.6 %collective-permute-start.1 = (bf16[13,16,128]{2,1,0:T(8,128)(2,1)S(1)}, bf16[13,16,128]{2,1,0:T(8,128)(2,1)S(1)}, u32[]{:S(2)}, u32[]{:S(2)}) collective-permute-start(bf16[13,16,128]{2,1,0:T(8,128)(2,1)S(1)} %get-tuple-element.15), channel_id=1, source_target_pairs={{0,2},{1,3},{2,0},{3,1},{4,6},{5,7},{6,4},{7,5},{8,10},{9,11},{10,... | collective-permute-start | bytes 159752 | tf_op jit(solution)/shard_map/ppermute | solution.py:318
  6.3 0.1 collective-permute-start.2
  6.3 2.4 %collective-permute-done.1.refs_2_ = bf16[13,16,128]{2,1,0:T(8,128)(2,1)S(1)} collective-permute-done((bf16[13,16,128]{2,1,0:T(8,128)(2,1)S(1)}, bf16[13,16,128]{2,1,0:T(8,128)(2,1)S(1)}, u32[]{:S(2)}, u32[]{:S(2)}) %collective-permute-start.1) | collective-permute-done | bytes 53280 | tf_op jit(solution)/shard_map/ppermute | solution.py:318
  8.7 1.4 %collective-permute-done.2.refs_3_ = bf16[13,16,128]{2,1,0:T(8,128)(2,1)S(1)} collective-permute-done((bf16[13,16,128]{2,1,0:T(8,128)(2,1)S(1)}, bf16[13,16,128]{2,1,0:T(8,128)(2,1)S(1)}, u32[]{:S(2)}, u32[]{:S(2)}) %collective-permute-start.2) | collective-permute-done | bytes 53280 | tf_op jit(solution)/shard_map/ppermute | solution.py:318
  10.0 0.0 collective-permute-done.refs_1_.pair
  10.0 0.0 copy-start.4
  10.1 0.0 copy-start.7
  10.1 0.1 shard_map.74
  10.1 1.6 %collective-permute-start.3 = (bf16[13,16,128]{2,1,0:T(8,128)(2,1)S(1)}, bf16[13,16,128]{2,1,0:T(8,128)(2,1)S(1)}, u32[]{:S(2)}, u32[]{:S(2)}) collective-permute-start(bf16[13,16,128]{2,1,0:T(8,128)(2,1)S(1)} %get-tuple-element.18), channel_id=1, source_target_pairs={{0,4},{1,5},{2,6},{3,7},{4,0},{5,1},{6,2},{7,3},{8,12},{9,13},{10,... | collective-permute-start | bytes 159752 | tf_op jit(solution)/shard_map/ppermute | solution.py:318
  11.8 2.6 %collective-permute-start.4 = (bf16[13,16,128]{2,1,0:T(8,128)(2,1)S(1)}, bf16[13,16,128]{2,1,0:T(8,128)(2,1)S(1)}, u32[]{:S(2)}, u32[]{:S(2)}) collective-permute-start(bf16[13,16,128]{2,1,0:T(8,128)(2,1)S(1)} %get-tuple-element.19), channel_id=1, source_target_pairs={{0,8},{1,9},{2,10},{3,11},{4,12},{5,13},{6,14},{7,15},{8,0},{9,1},... | collective-permute-start | bytes 159752 | tf_op jit(solution)/shard_map/ppermute | solution.py:318
  14.3 0.2 %collective-permute-start.5 = (bf16[13,16,128]{2,1,0:T(8,128)(2,1)S(1)}, bf16[13,16,128]{2,1,0:T(8,128)(2,1)S(1)}, u32[]{:S(2)}, u32[]{:S(2)}) collective-permute-start(bf16[13,16,128]{2,1,0:T(8,128)(2,1)S(1)} %get-tuple-element.20), channel_id=1, source_target_pairs={{0,12},{1,13},{2,14},{3,15},{4,8},{5,9},{6,10},{7,11},{8,4},{9,5},... | collective-permute-start | bytes 159752 | tf_op jit(solution)/shard_map/ppermute | solution.py:318
  14.6 0.0 copy-done.4
  14.6 0.7 %collective-permute-start.6 = (bf16[16,384]{1,0:T(8,128)(2,1)S(1)}, bf16[16,384]{1,0:T(8,128)(2,1)S(1)}, u32[]{:S(2)}, u32[]{:S(2)}) collective-permute-start(bf16[16,384]{1,0:T(8,128)(2,1)S(1)} %copy-done.4), channel_id=1, source_target_pairs={{1,2},{3,4},{5,6},{7,8},{9,10},{11,12},{13,14},{2,1},{4,3},{6,5},{... | collective-permute-start | bytes 36872 | tf_op jit(solution)/shard_map/ppermute | solution.py:331
  15.2 0.0 collective-permute-done.6.other
  15.2 0.0 copy-done.7
  15.2 0.0 copy-start
  15.3 0.0 copy-start.2
  15.3 0.9 %shard_map.75.refs_4_ = bf16[256,384]{1,0:T(8,128)(2,1)S(1)} custom-call(bf16[21,16,21]{2,1,0:T(8,128)(2,1)S(1)} %bitcast.7, bf16[16,384]{1,0:T(8,128)(2,1)S(1)} %copy-done.4, bf16[16,16,128]{2,1,0:T(8,128)(2,1)S(1)} %collective-permute-done.refs_1_.pair, bf16[16,384]{1,0:T(8,128)(2,1)S(1)} %collective-permute-done.6.other), custom_call_target="tpu_custom_call" | custom-call | flops 226492416 | bytes 600000 | tf_op jit(solution)/shard_map/pallas_call | solution.py:207
  16.2 0.0 collective-permute-done.3.refs_1_
  16.2 1.7 %collective-permute-done.4.refs_2_ = bf16[13,16,128]{2,1,0:T(8,128)(2,1)S(1)} collective-permute-done((bf16[13,16,128]{2,1,0:T(8,128)(2,1)S(1)}, bf16[13,16,128]{2,1,0:T(8,128)(2,1)S(1)}, u32[]{:S(2)}, u32[]{:S(2)}) %collective-permute-start.4) | collective-permute-done | bytes 53280 | tf_op jit(solution)/shard_map/ppermute | solution.py:318
  17.9 2.4 %collective-permute-done.5.refs_3_ = bf16[13,16,128]{2,1,0:T(8,128)(2,1)S(1)} collective-permute-done((bf16[13,16,128]{2,1,0:T(8,128)(2,1)S(1)}, bf16[13,16,128]{2,1,0:T(8,128)(2,1)S(1)}, u32[]{:S(2)}, u32[]{:S(2)}) %collective-permute-start.5) | collective-permute-done | bytes 53280 | tf_op jit(solution)/shard_map/ppermute | solution.py:318
  20.4 0.0 copy-done
  20.4 0.0 copy-done.2
  20.4 1.5 %shard_map.76 = f32[16,384]{1,0:T(8,128)} custom-call(bf16[13,16,128]{2,1,0:T(8,128)(2,1)S(1)} %get-tuple-element.17.refs_0_, bf16[13,16,128]{2,1,0:T(8,128)(2,1)S(1)} %collective-permute-done.3.refs_1_, bf16[13,16,128]{2,1,0:T(8,128)(2,1)S(1)} %collective-permute-done.4.refs_2_, bf16[13,16,128]{2,1,0:T(8,128)(2,1)S(1)} %collective-permute-done.5.refs_3_, ...), custom_call_target="tpu_custom_call" | custom-call | flops 9830400 | bytes 1000000 | tf_op jit(solution)/shard_map/pallas_call | solution.py:306
Async XLA Ops:
  0.0 0.7 %copy-start.5 = (f32[1,8,16]{2,1,0:T(8,128)S(1)}, f32[1,8,16]{2,1,0:T(8,128)}, u32[]{:S(2)}) copy-start(f32[1,8,16]{2,1,0:T(8,128)} %param.10) | copy-start | bytes 1540
  0.0 0.7 %copy-start.6 = (s32[1,2,3]{2,1,0:T(2,128)S(1)}, s32[1,2,3]{2,1,0:T(2,128)}, u32[]{:S(2)}) copy-start(s32[1,2,3]{2,1,0:T(2,128)} %param.11) | copy-start | bytes 76
  0.7 0.9 %copy-start.1 = (bf16[1,256,384]{2,1,0:T(8,128)(2,1)S(1)}, bf16[1,256,384]{2,1,0:T(8,128)(2,1)}, u32[]{:S(2)}) copy-start(bf16[1,256,384]{2,1,0:T(8,128)(2,1)} %param.7) | copy-start | bytes 589828
  1.6 0.7 %copy-start.3 = (bf16[16,384]{1,0:T(8,128)(2,1)S(1)}, bf16[16,384]{1,0:T(8,128)(2,1)}, u32[]{:S(2)}) copy-start(bf16[16,384]{1,0:T(8,128)(2,1)} %own.1) | copy-start | bytes 36868
  3.1 6.9 %collective-permute-start = (bf16[16,16,128]{2,1,0:T(8,128)(2,1)S(1)}, bf16[16,16,128]{2,1,0:T(8,128)(2,1)S(1)}, u32[]{:S(2)}, u32[]{:S(2)}) collective-permute-start(bf16[16,16,128]{2,1,0:T(8,128)(2,1)S(1)} %get-tuple-element.14), channel_id=1, source_target_pairs={{0,1},{1,0},{2,3},{3,2},{4,5},{5,4},{6,7},{7,6},{8,9},{9,8},{10,11... | collective-permute-start | bytes 196616 | tf_op jit(solution)/shard_map/ppermute | solution.py:318
  3.7 5.0 %collective-permute-start.1 = (bf16[13,16,128]{2,1,0:T(8,128)(2,1)S(1)}, bf16[13,16,128]{2,1,0:T(8,128)(2,1)S(1)}, u32[]{:S(2)}, u32[]{:S(2)}) collective-permute-start(bf16[13,16,128]{2,1,0:T(8,128)(2,1)S(1)} %get-tuple-element.15), channel_id=1, source_target_pairs={{0,2},{1,3},{2,0},{3,1},{4,6},{5,7},{6,4},{7,5},{8,10},{9,11},{10,... | collective-permute-start | bytes 159752 | tf_op jit(solution)/shard_map/ppermute | solution.py:318
  6.3 3.8 %collective-permute-start.2 = (bf16[13,16,128]{2,1,0:T(8,128)(2,1)S(1)}, bf16[13,16,128]{2,1,0:T(8,128)(2,1)S(1)}, u32[]{:S(2)}, u32[]{:S(2)}) collective-permute-start(bf16[13,16,128]{2,1,0:T(8,128)(2,1)S(1)} %get-tuple-element.16), channel_id=1, source_target_pairs={{0,3},{1,2},{2,1},{3,0},{4,7},{5,6},{6,5},{7,4},{8,11},{9,10},{10,... | collective-permute-start | bytes 159752 | tf_op jit(solution)/shard_map/ppermute | solution.py:318
  10.0 4.5 %copy-start.4 = (bf16[16,384]{1,0:T(8,128)(2,1)S(1)}, bf16[16,384]{1,0:T(8,128)(2,1)}, u32[]{:S(2)}) copy-start(bf16[16,384]{1,0:T(8,128)(2,1)} %own.1) | copy-start | bytes 36868
  10.1 5.2 %copy-start.7 = (bf16[16,21,21]{2,0,1:T(8,128)(2,1)S(1)}, bf16[16,21,21]{2,0,1:T(8,128)(2,1)}, u32[]{:S(2)}) copy-start(bf16[16,21,21]{2,0,1:T(8,128)(2,1)} %param.9) | copy-start | bytes 42340
  10.1 6.1 %collective-permute-start.3 = (bf16[13,16,128]{2,1,0:T(8,128)(2,1)S(1)}, bf16[13,16,128]{2,1,0:T(8,128)(2,1)S(1)}, u32[]{:S(2)}, u32[]{:S(2)}) collective-permute-start(bf16[13,16,128]{2,1,0:T(8,128)(2,1)S(1)} %get-tuple-element.18), channel_id=1, source_target_pairs={{0,4},{1,5},{2,6},{3,7},{4,0},{5,1},{6,2},{7,3},{8,12},{9,13},{10,... | collective-permute-start | bytes 159752 | tf_op jit(solution)/shard_map/ppermute | solution.py:318
  11.8 6.2 %collective-permute-start.4 = (bf16[13,16,128]{2,1,0:T(8,128)(2,1)S(1)}, bf16[13,16,128]{2,1,0:T(8,128)(2,1)S(1)}, u32[]{:S(2)}, u32[]{:S(2)}) collective-permute-start(bf16[13,16,128]{2,1,0:T(8,128)(2,1)S(1)} %get-tuple-element.19), channel_id=1, source_target_pairs={{0,8},{1,9},{2,10},{3,11},{4,12},{5,13},{6,14},{7,15},{8,0},{9,1},... | collective-permute-start | bytes 159752 | tf_op jit(solution)/shard_map/ppermute | solution.py:318
  14.3 6.0 %collective-permute-start.5 = (bf16[13,16,128]{2,1,0:T(8,128)(2,1)S(1)}, bf16[13,16,128]{2,1,0:T(8,128)(2,1)S(1)}, u32[]{:S(2)}, u32[]{:S(2)}) collective-permute-start(bf16[13,16,128]{2,1,0:T(8,128)(2,1)S(1)} %get-tuple-element.20), channel_id=1, source_target_pairs={{0,12},{1,13},{2,14},{3,15},{4,8},{5,9},{6,10},{7,11},{8,4},{9,5},... | collective-permute-start | bytes 159752 | tf_op jit(solution)/shard_map/ppermute | solution.py:318
  14.6 0.7 %collective-permute-start.6 = (bf16[16,384]{1,0:T(8,128)(2,1)S(1)}, bf16[16,384]{1,0:T(8,128)(2,1)S(1)}, u32[]{:S(2)}, u32[]{:S(2)}) collective-permute-start(bf16[16,384]{1,0:T(8,128)(2,1)S(1)} %copy-done.4), channel_id=1, source_target_pairs={{1,2},{3,4},{5,6},{7,8},{9,10},{11,12},{13,14},{2,1},{4,3},{6,5},{... | collective-permute-start | bytes 36872 | tf_op jit(solution)/shard_map/ppermute | solution.py:331
  15.2 5.1 %copy-start = (s32[16,16,384]{2,1,0:T(8,128)S(1)}, s32[16,16,384]{2,1,0:T(8,128)}, u32[]{:S(2)}) copy-start(s32[16,16,384]{2,1,0:T(8,128)} %refs_5_.1) | copy-start | bytes 1179652
  15.3 5.1 %copy-start.2 = (bf16[16,16,384]{2,1,0:T(8,128)(2,1)S(1)}, bf16[16,16,384]{2,1,0:T(8,128)(2,1)}, u32[]{:S(2)}) copy-start(bf16[16,16,384]{2,1,0:T(8,128)(2,1)} %refs_6_.1) | copy-start | bytes 589828

commit v2 on v1

--- a/solution.py
+++ b/solution.py
@@ -29,126 +29,126 @@
     return items[0]
 
 
-def pack_kernel(fast, science, template, coef, grid_index, *refs):
-    blocks = refs[:fast]
-    spread, cells, sems, small = refs[fast:]
-    rows, width = template.shape
-    columns = width // CELL
-    slow = science.shape[0]
-    basis = coef.shape[1]
-    here = lax.rem(lax.axis_index("epoch"), fast)
-    cell_copy = pltpu.make_async_copy(grid_index, cells, small.at[0])
-    coef_copy = pltpu.make_async_copy(coef, spread, small.at[1])
-    cell_copy.start()
-    coef_copy.start()
-    moves = []
-    for c in range(columns):
-        at = slice(c * CELL, (c + 1) * CELL)
-        for k in range(fast):
-            moves.append(
-                pltpu.make_async_copy(
-                    science.at[:, here ^ k, :, at],
-                    blocks[k].at[c * slow : (c + 1) * slow],
-                    sems.at[k, c],
-                )
-            )
-        moves.append(
-            pltpu.make_async_copy(
-                template.at[:, at], blocks[1].at[blocks[1].shape[0] - columns + c], small.at[2 + c]
-            )
-        )
-    for move in moves:
-        move.start()
-    cell_copy.wait()
-    coef_copy.wait()
-    picked = [
-        spread[pl.ds(cells[r, c], 1), :] for r in range(cells.shape[0]) for c in range(columns)
-    ]
-    size = up(len(picked), rows)
-    if size > len(picked):
-        picked.append(jnp.zeros((size - len(picked), basis), jnp.float32))
+def cell_rows(coef, grid_index):
+    levels, basis = coef.shape
+    level = lax.broadcasted_iota(jnp.int32, (levels, basis), 0)
+    picked = []
+    for r in range(grid_index.shape[0]):
+        for c in range(grid_index.shape[1]):
+            chosen = jnp.broadcast_to(grid_index[r : r + 1, c : c + 1], (levels, basis)) == level
+            picked.append(jnp.sum(jnp.where(chosen, coef[...], 0.0), axis=0, keepdims=True))
     table = jnp.concatenate(picked, axis=0)
-    table = jnp.concatenate([table, jnp.zeros((size, LANES - basis), jnp.float32)], axis=1)
+    table = jnp.concatenate(
+        [table, jnp.zeros((table.shape[0], LANES - basis), jnp.float32)], axis=1
+    )
     first = table.astype(jnp.bfloat16).astype(jnp.float32)
     rest = table - first
     second = rest.astype(jnp.bfloat16).astype(jnp.float32)
     third = rest - second
-    table = first + pltpu.roll(second, basis, 1) + pltpu.roll(third, 2 * basis, 1)
+    return first + pltpu.roll(second, basis, 1) + pltpu.roll(third, 2 * basis, 1)
+
+
+def fill_tail(block, at, tables):
+    rows = block.shape[1]
+    table = jnp.concatenate(tables, axis=0)
+    size = up(table.shape[0], rows)
+    if size > table.shape[0]:
+        table = jnp.concatenate(
+            [table, jnp.zeros((size - table.shape[0], LANES), jnp.float32)], axis=0
+        )
     table = table.astype(jnp.bfloat16)
-    for k in range(fast):
-        for g in range(size // rows):
-            blocks[k][columns * slow + g] = table[g * rows : (g + 1) * rows]
-    for move in moves:
-        move.wait()
-
-
-def pack(science, template, coef, grid_index, fast):
-    rows, width = template.shape
-    slow = science.shape[1] // rows // fast
+    for g in range(size // rows):
+        block[at + g] = table[g * rows : (g + 1) * rows]
+
+
+def stage_kernel(science, coef, grid_index, rows_out, table_out):
+    slow, middle, cores, _, _ = science.shape
+    core = lax.rem(lax.axis_index("epoch"), cores)
+    for z in range(slow):
+        for k in range(middle):
+            rows_out[z, k] = science[z, k, core]
+    table_out[...] = cell_rows(coef, grid_index)
+
+
+def stage(science, coef, grid_index):
+    slow, middle, _, rows, width = science.shape
+    cells = grid_index.shape[0] * grid_index.shape[1]
+    return pl.pallas_call(
+        stage_kernel,
+        out_shape=[
+            jax.ShapeDtypeStruct((slow, middle, rows, width), jnp.bfloat16),
+            jax.ShapeDtypeStruct((cells, LANES), jnp.float32),
+        ],
+        compiler_params=pltpu.CompilerParams(vmem_limit_bytes=VMEM_LIMIT),
+        cost_estimate=pl.CostEstimate(flops=0, bytes_accessed=1_000_000, transcendentals=0),
+    )(science, coef, grid_index)
+
+
+def pack_kernel(own, pair, own_table, pair_coef, pair_index, after, *blocks):
+    slow, middle, cores, rows, width = pair.shape
     columns = width // CELL
-    groups = slow * columns + up(grid_index.shape[1] * columns, rows) // rows
-    shapes = [
-        jax.ShapeDtypeStruct(
-            (groups + (columns if k == 1 else 0), rows, LANES), jnp.bfloat16
-        )
-        for k in range(fast)
-    ]
-    return pl.pallas_call(
-        functools.partial(pack_kernel, fast),
-        out_shape=shapes,
-        in_specs=[pl.BlockSpec(memory_space=pltpu.HBM)] * 4,
-        out_specs=[pl.BlockSpec(memory_space=pltpu.VMEM)] * fast,
-        scratch_shapes=[
-            pltpu.VMEM(coef.shape[1:], jnp.float32),
-            pltpu.SMEM(grid_index.shape[1:], jnp.int32),
-            pltpu.SemaphoreType.DMA((fast, columns)),
-            pltpu.SemaphoreType.DMA((2 + columns,)),
-        ],
+    me = lax.axis_index("epoch")
+    core, here = lax.rem(me, cores), lax.rem(lax.div(me, cores), middle)
+    tables = [own_table[...], cell_rows(pair_coef, pair_index)]
+    for k in range(middle):
+        to = here ^ k
+        for c in range(columns):
+            at = slice(c * CELL, (c + 1) * CELL)
+            for z in range(slow):
+                blocks[k][c * slow + z] = own[z, to, :, at]
+                blocks[k][(columns + c) * slow + z] = pair[z, to, core, :, at]
+        fill_tail(blocks[k], cores * columns * slow, tables)
+
+
+def pack(own, pair, own_table, pair_coef, pair_index, after):
+    slow, middle, cores, rows, width = pair.shape
+    columns = width // CELL
+    groups = cores * slow * columns + up(cores * own_table.shape[0], rows) // rows
+    return pl.pallas_call(
+        pack_kernel,
+        out_shape=[jax.ShapeDtypeStruct((groups, rows, LANES), jnp.bfloat16)] * middle,
         compiler_params=pltpu.CompilerParams(vmem_limit_bytes=VMEM_LIMIT),
         cost_estimate=pl.CostEstimate(flops=0, bytes_accessed=500_000, transcendentals=0),
-    )(science.reshape(slow, fast, rows, width), template, coef[0], grid_index[0])
-
-
-def route_kernel(fast, slow, columns, *refs):
-    held, sent, tails = refs[:fast], refs[fast : fast + slow], refs[fast + slow]
+    )(own, pair, own_table, pair_coef, pair_index, after)
+
+
+def route_kernel(middle, slow, columns, cells, *refs):
+    held, sent, tails = refs[:middle], refs[middle + 1 : middle + 1 + slow], refs[-1]
     rows = held[0].shape[1]
     me = lax.axis_index("epoch")
-    across, here = lax.div(me, fast), lax.rem(me, fast)
+    across, here = lax.div(me, 2 * middle), lax.rem(me, 2 * middle)
     span = tails.shape[1] // rows
-    for j in range(fast):
+    tail = 2 * columns * slow
+    for j in range(middle):
         for g in range(span):
-            tails[j, g * rows : (g + 1) * rows] = held[j][columns * slow + g].astype(jnp.float32)
+            tails[j, g * rows : (g + 1) * rows] = held[j][tail + g].astype(jnp.float32)
     for k in range(slow):
         to = across ^ k
-        for j in range(fast):
-            for c in range(columns):
-                sent[k][j * columns + c] = held[j][c * slow + to]
-        cell_row = lax.div((to * fast + here) * rows, CELL)
+        for j in range(middle):
+            for g in range(2 * columns):
+                sent[k][j * 2 * columns + g] = held[j][g * slow + to]
+        cell_row = lax.div((to * 2 * middle + here) * rows, CELL)
         picked = [
-            tails[j, pl.ds(cell_row * columns + c, 1), :]
-            for j in range(fast)
+            tails[j, pl.ds(q * cells + cell_row * columns + c, 1), :]
+            for j in range(middle)
+            for q in range(2)
             for c in range(columns)
         ]
-        size = up(len(picked), rows)
-        if size > len(picked):
-            picked.append(jnp.zeros((size - len(picked), LANES), jnp.float32))
-        table = jnp.concatenate(picked, axis=0).astype(jnp.bfloat16)
-        for g in range(size // rows):
-            sent[k][fast * columns + g] = table[g * rows : (g + 1) * rows]
-
-
-def route(held, slow, columns):
-    fast = len(held)
+        fill_tail(sent[k], 2 * middle * columns, picked)
+
+
+def route(held, after, slow, columns, cells):
+    middle = len(held)
     rows = held[0].shape[1]
-    groups = fast * columns + up(fast * columns, rows) // rows
-    tail = (held[0].shape[0] - slow * columns) * rows
-    return pl.pallas_call(
-        functools.partial(route_kernel, fast, slow, columns),
+    groups = 2 * middle * columns + up(2 * middle * columns, rows) // rows
+    tail = (held[0].shape[0] - 2 * slow * columns) * rows
+    return pl.pallas_call(
+        functools.partial(route_kernel, middle, slow, columns, cells),
         out_shape=[jax.ShapeDtypeStruct((groups, rows, LANES), jnp.bfloat16)] * slow,
-        scratch_shapes=[pltpu.VMEM((fast, tail, LANES), jnp.float32)],
+        scratch_shapes=[pltpu.VMEM((middle, tail, LANES), jnp.float32)],
         compiler_params=pltpu.CompilerParams(vmem_limit_bytes=VMEM_LIMIT),
         cost_estimate=pl.CostEstimate(flops=0, bytes_accessed=500_000, transcendentals=0),
-    )(*held)
+    )(*held, after)
 
 
 def basis_kernel(slot, kernels, own, pair, other, out, image, left, right):
@@ -158,9 +158,7 @@
     span = image.shape[1]
     odd = lax.rem(lax.axis_index("epoch"), 2) == 1
     image[...] = jnp.zeros(image.shape, jnp.float32)
-    columns = width // CELL
-    near = [pair[pair.shape[0] - columns + c].astype(jnp.float32) for c in range(columns)]
-    near = jnp.concatenate(near, axis=1)
+    near = pair[...].astype(jnp.float32)
     far = other[...].astype(jnp.float32)
     low = jnp.where(odd, near, far)
     high = jnp.where(odd, far, near)
@@ -219,7 +217,7 @@
     )(kernels.transpose(1, 0, 2), own, pair, other)
 
 
-def stack_kernel(count, fast, *refs):
+def stack_kernel(count, units, *refs):
     slow = len(refs) - 5
     blocks = refs[:slow]
     basis, clip_mask, inv_var, out, model = refs[slow:]
@@ -231,11 +229,10 @@
     line = lax.broadcasted_iota(jnp.int32, (SUB, LANES), 0)
     diagonal = (lane >= line * count) & (lane < (line + 1) * count)
     me = lax.axis_index("epoch")
-    across, here = lax.div(me, fast), lax.rem(me, fast)
     order, spread = [], []
     for k in range(slow):
         tail = jnp.concatenate(
-            [blocks[k][g].astype(jnp.float32) for g in range(fast * columns, blocks[k].shape[0])],
+            [blocks[k][g].astype(jnp.float32) for g in range(units * columns, blocks[k].shape[0])],
             axis=0,
         )
         own_lane = lax.broadcasted_iota(jnp.int32, tail.shape, 1) < count
@@ -248,8 +245,8 @@
                 value = value + pltpu.roll(value, step, 1)
                 step *= 2
             terms.append(value)
-        for j in range(fast):
-            order.append((k, j, (across ^ k) * fast + (here ^ j)))
+        for j in range(units):
+            order.append((k, j, me ^ (k * units + j)))
             spread.append([value[j * columns : (j + 1) * columns] for value in terms])
     for c in range(columns):
         at = slice(c * CELL, (c + 1) * CELL)
@@ -301,10 +298,10 @@
             out[top, at] = num / jnp.sqrt(1.0 + den)
 
 
-def stack(count, fast, blocks, basis, clip_mask, inv_var):
+def stack(count, units, blocks, basis, clip_mask, inv_var):
     epochs, rows, width = clip_mask.shape
     return pl.pallas_call(
-        functools.partial(stack_kernel, count, fast),
+        functools.partial(stack_kernel, count, units),
         out_shape=jax.ShapeDtypeStruct((rows, width), jnp.float32),
         scratch_shapes=[pltpu.VMEM((epochs * SUB, rows // SUB * CELL), jnp.float32)],
         compiler_params=pltpu.CompilerParams(vmem_limit_bytes=VMEM_LIMIT),
@@ -320,19 +317,27 @@
 
 def local(science, template, kernels, coef, grid_index, clip_mask, inv_var):
     count = lax.axis_size("epoch")
-    fast = 2
-    while 4 * fast * fast <= count:
-        fast *= 2
-    slow = count // fast
-    columns = template.shape[1] // CELL
-    sent = pack(science, template, coef, grid_index, fast)
-    held = [sent[0]] + [exchange(sent[k], k) for k in range(1, fast)]
-    swap = [(i, i + 1) for i in range(1, count - 1, 2)]
-    other = lax.ppermute(template, "epoch", swap + [(b, a) for a, b in swap])
-    sent = route(held, slow, columns)
-    blocks = [sent[0]] + [exchange(sent[k], k * fast) for k in range(1, slow)]
-    basis = basis_rows(kernels, template, held[1], other)
-    return stack(kernels.shape[0], fast, blocks, basis, clip_mask, inv_var)
+    rows, width = template.shape
+    columns = width // CELL
+    slow = 1
+    while slow * slow * 2 < count:
+        slow *= 2
+    middle = count // 2 // slow
+    units = 2 * middle
+    view = (slow, middle, 2, rows, width)
+    pair_science = exchange(science, 1).reshape(view)
+    pair_coef = exchange(coef, 1)[0]
+    pair_index = exchange(grid_index, 1)[0]
+    pair = exchange(template, 1)
+    own, table = stage(science.reshape(view), coef[0], grid_index[0])
+    sent = pack(own, pair_science, table, pair_coef, pair_index, pair)
+    held = [sent[0]] + [exchange(sent[k], 2 * k) for k in range(1, middle)]
+    up_down = [(i, i + 2) if i % 2 == 0 else (i + 2, i) for i in range(count - 2)]
+    other = lax.ppermute(pair, "epoch", up_down)
+    sent = route(held, other, slow, columns, grid_index.shape[1] * columns)
+    blocks = [sent[0]] + [exchange(sent[k], k * units) for k in range(1, slow)]
+    basis = basis_rows(kernels, template, pair, other)
+    return stack(kernels.shape[0], units, blocks, basis, clip_mask, inv_var)
 
 
 def solution(mesh):

time: 22.2 us -> 24.4 us (1.099)
  starting transfers between devices: 8.28 us -> 13.3 us
  waiting for transfers between devices: 7.88 us -> 6.36 us
  local copies, waits for them, and re-layouts: 2.35 us -> 1.63 us
  Pallas kernels: 3.32 us -> 2.89 us
    ppermute x6 -> x8, starting transfers between devices: 7.63 us -> 11.4 us  [exchange(): lax.ppermute(block, 'epoch', [(i, i ^ step) for i in range(lax.axis_size(...]
    ppermute x6 -> x8, waiting for transfers between devices: 7.88 us -> 4.97 us  [exchange(): lax.ppermute(block, 'epoch', [(i, i ^ step) for i in range(lax.axis_size(...]
    ppermute x1, waiting for transfers between devices: 0.01 us -> 1.39 us  [local(): other = lax.ppermute(pair, 'epoch', up_down)]
    ppermute x1, starting transfers between devices: 0.65 us -> 1.92 us  [local(): other = lax.ppermute(pair, 'epoch', up_down)]
    unnamed x16 -> x14, local copies, waits for them, and re-layouts: 2.35 us -> 1.63 us
    pallas_call x3 -> x4, Pallas kernels: 2.4 us -> 1.97 us  [the longest x1 1.53 us: stack(): pl.pallas_call(functools.partial(stack_kernel, count, units), out_shape=j...]
  transfers between devices with their start and end apart: 7 -> 9, of which waited for: 4 -> 3; matrix products, arithmetic and copies ran while one was open for 0% -> 0% of each run, Pallas kernels for 4% -> 5%
where the time goes in v2:
time: 24.4 us; the launch traced here: 24.3 us
  starting transfers between devices  13.3 us (55%)
  waiting for transfers between devices  6.36 us (26%)
  Pallas kernels  2.89 us (12%)
  local copies, waits for them, and re-layouts  1.63 us (7%)
    ppermute x8, starting transfers between devices, exchange(): lax.ppermute(block, 'epoch', [(i, i ^ step) for i in range(lax.axis_size(...  11.4 us
    ppermute x8, waiting for transfers between devices, exchange(): lax.ppermute(block, 'epoch', [(i, i ^ step) for i in range(lax.axis_size(...  4.97 us
    ppermute x1, starting transfers between devices, local(): other = lax.ppermute(pair, 'epoch', up_down)  1.92 us
    unnamed x14, local copies, waits for them, and re-layouts  1.63 us
    pallas_call x1, Pallas kernels, stack(): pl.pallas_call(functools.partial(stack_kernel, count, units), out_shape=j...  1.53 us
    ppermute x1, waiting for transfers between devices, local(): other = lax.ppermute(pair, 'epoch', up_down)  1.39 us
    pallas_call x1, Pallas kernels, basis_rows(): pl.pallas_call(functools.partial(basis_kernel, slot), out_shape=jax.Shape...  0.92 us
  transfers between devices with their start and end apart: 9, of which 3 were waited for; matrix products, arithmetic and copies ran while one was open for 0% of the time, Pallas kernels for 5%

profile of v2, /device:TPU:0, one launch (start us, length us, event | category | flops | bytes accessed | tf_op | source)
XLA Modules:
  0.0 24.3 jit_solution(12346044221782449704)
XLA Ops:
  0.0 0.0 copy-start.3
  0.0 0.5 %collective-permute-start = (bf16[1,256,384]{2,1,0:T(8,128)(2,1)}, bf16[1,256,384]{2,1,0:T(8,128)(2,1)S(1)}, u32[]{:S(2)}, u32[]{:S(2)}) collective-permute-start(bf16[1,256,384]{2,1,0:T(8,128)(2,1)} %param.7), channel_id=1, source_target_pairs={{0,1},{1,0},{2,3},{3,2},{4,5},{5,4},{6,7},{7,6},{8,9},{9,8},{10,11... | collective-permute-start | bytes 589832 | tf_op jit(solution)/shard_map/ppermute | solution.py:315
  0.5 0.1 collective-permute-start.3
  0.5 0.4 %collective-permute-start.1 = (f32[1,8,16]{2,1,0:T(8,128)}, f32[1,8,16]{2,1,0:T(8,128)S(1)}, u32[]{:S(2)}, u32[]{:S(2)}) collective-permute-start(f32[1,8,16]{2,1,0:T(8,128)} %param.10), channel_id=1, source_target_pairs={{0,1},{1,0},{2,3},{3,2},{4,5},{5,4},{6,7},{7,6},{8,9},{9,8},{10,11... | collective-permute-start | bytes 1544 | tf_op jit(solution)/shard_map/ppermute | solution.py:315
  1.0 0.1 collective-permute-start.2
  1.0 0.0 copy-start.4
  1.0 0.0 copy-done.3
  1.0 0.7 %copy-done.4 = s32[1,2,3]{2,1,0:T(2,128)S(1)} copy-done((s32[1,2,3]{2,1,0:T(2,128)S(1)}, s32[1,2,3]{2,1,0:T(2,128)}, u32[]{:S(2)}) %copy-start.4) | copy-done | bytes 48
  1.7 0.0 copy-start.1
  1.7 0.9 %copy-done.1 = bf16[1,256,384]{2,1,0:T(8,128)(2,1)S(1)} copy-done((bf16[1,256,384]{2,1,0:T(8,128)(2,1)S(1)}, bf16[1,256,384]{2,1,0:T(8,128)(2,1)}, u32[]{:S(2)}) %copy-start.1) | copy-done | bytes 196632
  2.6 0.2 shard_map.73
  2.8 0.0 collective-permute-done.2
  2.8 0.0 collective-permute-done.1
  2.8 0.0 collective-permute-done.3.after.pair
  2.8 0.0 collective-permute-done
  2.9 0.2 shard_map.74
  3.0 3.0 %collective-permute-start.4 = (bf16[25,16,128]{2,1,0:T(8,128)(2,1)S(1)}, bf16[25,16,128]{2,1,0:T(8,128)(2,1)S(1)}, u32[]{:S(2)}, u32[]{:S(2)}) collective-permute-start(bf16[25,16,128]{2,1,0:T(8,128)(2,1)S(1)} %get-tuple-element.16), channel_id=1, source_target_pairs={{0,2},{1,3},{2,0},{3,1},{4,6},{5,7},{6,4},{7,5},{8,10},{9,11},{10,... | collective-permute-start | bytes 307208 | tf_op jit(solution)/shard_map/ppermute | solution.py:315
  6.0 1.9 %collective-permute-start.5 = (bf16[16,384]{1,0:T(8,128)(2,1)S(1)}, bf16[16,384]{1,0:T(8,128)(2,1)S(1)}, u32[]{:S(2)}, u32[]{:S(2)}) collective-permute-start(bf16[16,384]{1,0:T(8,128)(2,1)S(1)} %collective-permute-done.3.after.pair), channel_id=1, source_target_pairs={{0,2},{3,1},{2,4},{5,3},{4,6},{7,5},{6,8},{9,7},{8,10},{11,9},{10,... | collective-permute-start | bytes 36872 | tf_op jit(solution)/shard_map/ppermute | solution.py:336
  8.0 1.4 %collective-permute-done.5.refs_2_.other = bf16[16,384]{1,0:T(8,128)(2,1)S(1)} collective-permute-done((bf16[16,384]{1,0:T(8,128)(2,1)S(1)}, bf16[16,384]{1,0:T(8,128)(2,1)S(1)}, u32[]{:S(2)}, u32[]{:S(2)}) %collective-permute-start.5) | collective-permute-done | bytes 12320 | tf_op jit(solution)/shard_map/ppermute | solution.py:336
  9.3 0.0 collective-permute-done.4.refs_1_
  9.4 0.0 copy-start.5
  9.4 0.0 copy-start.6
  9.4 0.1 shard_map.75
  9.4 4.8 %collective-permute-start.6 = (bf16[13,16,128]{2,1,0:T(8,128)(2,1)S(1)}, bf16[13,16,128]{2,1,0:T(8,128)(2,1)S(1)}, u32[]{:S(2)}, u32[]{:S(2)}) collective-permute-start(bf16[13,16,128]{2,1,0:T(8,128)(2,1)S(1)} %get-tuple-element.18), channel_id=1, source_target_pairs={{0,4},{1,5},{2,6},{3,7},{4,0},{5,1},{6,2},{7,3},{8,12},{9,13},{10,... | collective-permute-start | bytes 159752 | tf_op jit(solution)/shard_map/ppermute | solution.py:315
  14.2 2.6 %collective-permute-start.7 = (bf16[13,16,128]{2,1,0:T(8,128)(2,1)S(1)}, bf16[13,16,128]{2,1,0:T(8,128)(2,1)S(1)}, u32[]{:S(2)}, u32[]{:S(2)}) collective-permute-start(bf16[13,16,128]{2,1,0:T(8,128)(2,1)S(1)} %get-tuple-element.19), channel_id=1, source_target_pairs={{0,8},{1,9},{2,10},{3,11},{4,12},{5,13},{6,14},{7,15},{8,0},{9,1},... | collective-permute-start | bytes 159752 | tf_op jit(solution)/shard_map/ppermute | solution.py:315
  16.8 0.0 collective-permute-start.8
  16.8 0.0 copy-done.5
  16.8 0.0 copy-done.6
  16.8 0.0 copy-start
  16.8 0.0 copy-start.2
  16.8 0.9 %shard_map.76.refs_4_ = bf16[256,384]{1,0:T(8,128)(2,1)S(1)} custom-call(bf16[21,16,21]{2,1,0:T(8,128)(2,1)S(1)} %bitcast.13, bf16[16,384]{1,0:T(8,128)(2,1)S(1)} %copy-done.6, bf16[16,384]{1,0:T(8,128)(2,1)S(1)} %collective-permute-done.3.after.pair, bf16[16,384]{1,0:T(8,128)(2,1)S(1)} %collective-permute-done.5.refs_2_.other), custom_call_target="tpu_custom_call" | custom-call | flops 226492416 | bytes 600000 | tf_op jit(solution)/shard_map/pallas_call | solution.py:205
  17.8 0.0 collective-permute-done.6.refs_1_
  17.8 2.5 %collective-permute-done.7.refs_2_ = bf16[13,16,128]{2,1,0:T(8,128)(2,1)S(1)} collective-permute-done((bf16[13,16,128]{2,1,0:T(8,128)(2,1)S(1)}, bf16[13,16,128]{2,1,0:T(8,128)(2,1)S(1)}, u32[]{:S(2)}, u32[]{:S(2)}) %collective-permute-start.7) | collective-permute-done | bytes 53280 | tf_op jit(solution)/shard_map/ppermute | solution.py:315
  20.2 2.5 %collective-permute-done.8.refs_3_ = bf16[13,16,128]{2,1,0:T(8,128)(2,1)S(1)} collective-permute-done((bf16[13,16,128]{2,1,0:T(8,128)(2,1)S(1)}, bf16[13,16,128]{2,1,0:T(8,128)(2,1)S(1)}, u32[]{:S(2)}, u32[]{:S(2)}) %collective-permute-start.8) | collective-permute-done | bytes 53280 | tf_op jit(solution)/shard_map/ppermute | solution.py:315
  22.7 0.0 copy-done
  22.7 0.0 copy-done.2
  22.7 1.5 %shard_map.77 = f32[16,384]{1,0:T(8,128)} custom-call(bf16[13,16,128]{2,1,0:T(8,128)(2,1)S(1)} %get-tuple-element.17.refs_0_, bf16[13,16,128]{2,1,0:T(8,128)(2,1)S(1)} %collective-permute-done.6.refs_1_, bf16[13,16,128]{2,1,0:T(8,128)(2,1)S(1)} %collective-permute-done.7.refs_2_, bf16[13,16,128]{2,1,0:T(8,128)(2,1)S(1)} %collective-permute-done.8.refs_3_, ...), custom_call_target="tpu_custom_call" | custom-call | flops 9830400 | bytes 1000000 | tf_op jit(solution)/shard_map/pallas_call | solution.py:303
Async XLA Ops:
  0.0 1.0 %copy-start.3 = (f32[1,8,16]{2,1,0:T(8,128)S(1)}, f32[1,8,16]{2,1,0:T(8,128)}, u32[]{:S(2)}) copy-start(f32[1,8,16]{2,1,0:T(8,128)} %param.10) | copy-start | bytes 1540
  0.0 2.8 %collective-permute-start = (bf16[1,256,384]{2,1,0:T(8,128)(2,1)}, bf16[1,256,384]{2,1,0:T(8,128)(2,1)S(1)}, u32[]{:S(2)}, u32[]{:S(2)}) collective-permute-start(bf16[1,256,384]{2,1,0:T(8,128)(2,1)} %param.7), channel_id=1, source_target_pairs={{0,1},{1,0},{2,3},{3,2},{4,5},{5,4},{6,7},{7,6},{8,9},{9,8},{10,11... | collective-permute-start | bytes 589832 | tf_op jit(solution)/shard_map/ppermute | solution.py:315
  0.5 2.4 %collective-permute-start.3 = (bf16[16,384]{1,0:T(8,128)(2,1)}, bf16[16,384]{1,0:T(8,128)(2,1)S(1)}, u32[]{:S(2)}, u32[]{:S(2)}) collective-permute-start(bf16[16,384]{1,0:T(8,128)(2,1)} %own.1), channel_id=1, source_target_pairs={{0,1},{1,0},{2,3},{3,2},{4,5},{5,4},{6,7},{7,6},{8,9},{9,8},{10,11... | collective-permute-start | bytes 36872 | tf_op jit(solution)/shard_map/ppermute | solution.py:315
  0.5 2.3 %collective-permute-start.1 = (f32[1,8,16]{2,1,0:T(8,128)}, f32[1,8,16]{2,1,0:T(8,128)S(1)}, u32[]{:S(2)}, u32[]{:S(2)}) collective-permute-start(f32[1,8,16]{2,1,0:T(8,128)} %param.10), channel_id=1, source_target_pairs={{0,1},{1,0},{2,3},{3,2},{4,5},{5,4},{6,7},{7,6},{8,9},{9,8},{10,11... | collective-permute-start | bytes 1544 | tf_op jit(solution)/shard_map/ppermute | solution.py:315
  1.0 1.9 %collective-permute-start.2 = (s32[1,2,3]{2,1,0:T(2,128)}, s32[1,2,3]{2,1,0:T(2,128)S(1)}, u32[]{:S(2)}, u32[]{:S(2)}) collective-permute-start(s32[1,2,3]{2,1,0:T(2,128)} %param.11), channel_id=1, source_target_pairs={{0,1},{1,0},{2,3},{3,2},{4,5},{5,4},{6,7},{7,6},{8,9},{9,8},{10,11... | collective-permute-start | bytes 80 | tf_op jit(solution)/shard_map/ppermute | solution.py:315
  1.0 0.7 %copy-start.4 = (s32[1,2,3]{2,1,0:T(2,128)S(1)}, s32[1,2,3]{2,1,0:T(2,128)}, u32[]{:S(2)}) copy-start(s32[1,2,3]{2,1,0:T(2,128)} %param.11) | copy-start | bytes 76
  1.7 0.9 %copy-start.1 = (bf16[1,256,384]{2,1,0:T(8,128)(2,1)S(1)}, bf16[1,256,384]{2,1,0:T(8,128)(2,1)}, u32[]{:S(2)}) copy-start(bf16[1,256,384]{2,1,0:T(8,128)(2,1)} %param.7) | copy-start | bytes 589828
  3.0 6.3 %collective-permute-start.4 = (bf16[25,16,128]{2,1,0:T(8,128)(2,1)S(1)}, bf16[25,16,128]{2,1,0:T(8,128)(2,1)S(1)}, u32[]{:S(2)}, u32[]{:S(2)}) collective-permute-start(bf16[25,16,128]{2,1,0:T(8,128)(2,1)S(1)} %get-tuple-element.16), channel_id=1, source_target_pairs={{0,2},{1,3},{2,0},{3,1},{4,6},{5,7},{6,4},{7,5},{8,10},{9,11},{10,... | collective-permute-start | bytes 307208 | tf_op jit(solution)/shard_map/ppermute | solution.py:315
  6.0 3.3 %collective-permute-start.5 = (bf16[16,384]{1,0:T(8,128)(2,1)S(1)}, bf16[16,384]{1,0:T(8,128)(2,1)S(1)}, u32[]{:S(2)}, u32[]{:S(2)}) collective-permute-start(bf16[16,384]{1,0:T(8,128)(2,1)S(1)} %collective-permute-done.3.after.pair), channel_id=1, source_target_pairs={{0,2},{3,1},{2,4},{5,3},{4,6},{7,5},{6,8},{9,7},{8,10},{11,9},{10,... | collective-permute-start | bytes 36872 | tf_op jit(solution)/shard_map/ppermute | solution.py:336
  9.4 7.5 %copy-start.5 = (bf16[16,21,21]{2,0,1:T(8,128)(2,1)S(1)}, bf16[16,21,21]{2,0,1:T(8,128)(2,1)}, u32[]{:S(2)}) copy-start(bf16[16,21,21]{2,0,1:T(8,128)(2,1)} %param.9) | copy-start | bytes 42340
  9.4 7.5 %copy-start.6 = (bf16[16,384]{1,0:T(8,128)(2,1)S(1)}, bf16[16,384]{1,0:T(8,128)(2,1)}, u32[]{:S(2)}) copy-start(bf16[16,384]{1,0:T(8,128)(2,1)} %own.1) | copy-start | bytes 36868
  9.4 8.4 %collective-permute-start.6 = (bf16[13,16,128]{2,1,0:T(8,128)(2,1)S(1)}, bf16[13,16,128]{2,1,0:T(8,128)(2,1)S(1)}, u32[]{:S(2)}, u32[]{:S(2)}) collective-permute-start(bf16[13,16,128]{2,1,0:T(8,128)(2,1)S(1)} %get-tuple-element.18), channel_id=1, source_target_pairs={{0,4},{1,5},{2,6},{3,7},{4,0},{5,1},{6,2},{7,3},{8,12},{9,13},{10,... | collective-permute-start | bytes 159752 | tf_op jit(solution)/shard_map/ppermute | solution.py:315
  14.2 6.0 %collective-permute-start.7 = (bf16[13,16,128]{2,1,0:T(8,128)(2,1)S(1)}, bf16[13,16,128]{2,1,0:T(8,128)(2,1)S(1)}, u32[]{:S(2)}, u32[]{:S(2)}) collective-permute-start(bf16[13,16,128]{2,1,0:T(8,128)(2,1)S(1)} %get-tuple-element.19), channel_id=1, source_target_pairs={{0,8},{1,9},{2,10},{3,11},{4,12},{5,13},{6,14},{7,15},{8,0},{9,1},... | collective-permute-start | bytes 159752 | tf_op jit(solution)/shard_map/ppermute | solution.py:315
  16.8 5.9 %collective-permute-start.8 = (bf16[13,16,128]{2,1,0:T(8,128)(2,1)S(1)}, bf16[13,16,128]{2,1,0:T(8,128)(2,1)S(1)}, u32[]{:S(2)}, u32[]{:S(2)}) collective-permute-start(bf16[13,16,128]{2,1,0:T(8,128)(2,1)S(1)} %get-tuple-element.20), channel_id=1, source_target_pairs={{0,12},{1,13},{2,14},{3,15},{4,8},{5,9},{6,10},{7,11},{8,4},{9,5},... | collective-permute-start | bytes 159752 | tf_op jit(solution)/shard_map/ppermute | solution.py:315
  16.8 5.9 %copy-start = (s32[16,16,384]{2,1,0:T(8,128)S(1)}, s32[16,16,384]{2,1,0:T(8,128)}, u32[]{:S(2)}) copy-start(s32[16,16,384]{2,1,0:T(8,128)} %refs_5_.1) | copy-start | bytes 1179652
  16.8 5.9 %copy-start.2 = (bf16[16,16,384]{2,1,0:T(8,128)(2,1)S(1)}, bf16[16,16,384]{2,1,0:T(8,128)(2,1)}, u32[]{:S(2)}) copy-start(bf16[16,16,384]{2,1,0:T(8,128)(2,1)} %refs_6_.1) | copy-start | bytes 589828

commit v3 on v2

--- a/solution.py
+++ b/solution.py
@@ -13,6 +13,7 @@
 SUB = 8
 TILE = 16
 VMEM_LIMIT = 16 * 1024 * 1024
+ORDER = [7, 3, 1, 6, 5, 4, 2]
 
 
 def up(value, unit):
@@ -61,105 +62,93 @@
         block[at + g] = table[g * rows : (g + 1) * rows]
 
 
-def stage_kernel(science, coef, grid_index, rows_out, table_out):
-    slow, middle, cores, _, _ = science.shape
-    core = lax.rem(lax.axis_index("epoch"), cores)
-    for z in range(slow):
-        for k in range(middle):
-            rows_out[z, k] = science[z, k, core]
-    table_out[...] = cell_rows(coef, grid_index)
+def with_template(k):
+    return k & (k + 1) == 0 and k > 0
+
+
+def stage_kernel(science, coef, grid_index, out, table):
+    core = lax.rem(lax.axis_index("epoch"), 2)
+    for chip in range(science.shape[0]):
+        out[chip] = science[chip, core]
+    table[...] = cell_rows(coef, grid_index)
 
 
 def stage(science, coef, grid_index):
-    slow, middle, _, rows, width = science.shape
-    cells = grid_index.shape[0] * grid_index.shape[1]
+    chips, _, rows, width = science.shape
     return pl.pallas_call(
         stage_kernel,
         out_shape=[
-            jax.ShapeDtypeStruct((slow, middle, rows, width), jnp.bfloat16),
-            jax.ShapeDtypeStruct((cells, LANES), jnp.float32),
+            jax.ShapeDtypeStruct((chips, rows, width), jnp.bfloat16),
+            jax.ShapeDtypeStruct((grid_index.shape[0] * grid_index.shape[1], LANES), jnp.float32),
         ],
         compiler_params=pltpu.CompilerParams(vmem_limit_bytes=VMEM_LIMIT),
         cost_estimate=pl.CostEstimate(flops=0, bytes_accessed=1_000_000, transcendentals=0),
     )(science, coef, grid_index)
 
 
-def pack_kernel(own, pair, own_table, pair_coef, pair_index, after, *blocks):
-    slow, middle, cores, rows, width = pair.shape
+def pack_kernel(steps, own, pair, own_table, pair_coef, pair_index, template, *refs):
+    blocks, tables = refs[:-1], refs[-1]
+    rows, width = template.shape
     columns = width // CELL
     me = lax.axis_index("epoch")
-    core, here = lax.rem(me, cores), lax.rem(lax.div(me, cores), middle)
-    tables = [own_table[...], cell_rows(pair_coef, pair_index)]
-    for k in range(middle):
+    core, here = lax.rem(me, 2), lax.div(me, 2)
+    half = tables.shape[0] // 2
+    cells = own_table.shape[0]
+    tables[:cells] = own_table[...]
+    tables[half : half + cells] = cell_rows(pair_coef, pair_index)
+    for k, block in zip(steps, blocks):
         to = here ^ k
         for c in range(columns):
             at = slice(c * CELL, (c + 1) * CELL)
-            for z in range(slow):
-                blocks[k][c * slow + z] = own[z, to, :, at]
-                blocks[k][(columns + c) * slow + z] = pair[z, to, core, :, at]
-        fill_tail(blocks[k], cores * columns * slow, tables)
-
-
-def pack(own, pair, own_table, pair_coef, pair_index, after):
-    slow, middle, cores, rows, width = pair.shape
-    columns = width // CELL
-    groups = cores * slow * columns + up(cores * own_table.shape[0], rows) // rows
-    return pl.pallas_call(
-        pack_kernel,
-        out_shape=[jax.ShapeDtypeStruct((groups, rows, LANES), jnp.bfloat16)] * middle,
-        compiler_params=pltpu.CompilerParams(vmem_limit_bytes=VMEM_LIMIT),
-        cost_estimate=pl.CostEstimate(flops=0, bytes_accessed=500_000, transcendentals=0),
-    )(own, pair, own_table, pair_coef, pair_index, after)
-
-
-def route_kernel(middle, slow, columns, cells, *refs):
-    held, sent, tails = refs[:middle], refs[middle + 1 : middle + 1 + slow], refs[-1]
-    rows = held[0].shape[1]
-    me = lax.axis_index("epoch")
-    across, here = lax.div(me, 2 * middle), lax.rem(me, 2 * middle)
-    span = tails.shape[1] // rows
-    tail = 2 * columns * slow
-    for j in range(middle):
-        for g in range(span):
-            tails[j, g * rows : (g + 1) * rows] = held[j][tail + g].astype(jnp.float32)
-    for k in range(slow):
-        to = across ^ k
-        for j in range(middle):
-            for g in range(2 * columns):
-                sent[k][j * 2 * columns + g] = held[j][g * slow + to]
-        cell_row = lax.div((to * 2 * middle + here) * rows, CELL)
+            block[c] = own[to, :, at]
+            block[columns + c] = pair[to, core, :, at]
+            if with_template(k):
+                block[block.shape[0] - columns + c] = template[:, at]
+        cell_row = lax.div((to * 2 + core) * rows, CELL)
         picked = [
-            tails[j, pl.ds(q * cells + cell_row * columns + c, 1), :]
-            for j in range(middle)
+            tables[pl.ds(q * half + cell_row * columns + c, 1), :]
             for q in range(2)
             for c in range(columns)
         ]
-        fill_tail(sent[k], 2 * middle * columns, picked)
-
-
-def route(held, after, slow, columns, cells):
-    middle = len(held)
-    rows = held[0].shape[1]
-    groups = 2 * middle * columns + up(2 * middle * columns, rows) // rows
-    tail = (held[0].shape[0] - 2 * slow * columns) * rows
+        fill_tail(block, 2 * columns, picked)
+
+
+def pack(own, pair, own_table, pair_coef, pair_index, template, steps):
+    rows, width = template.shape
+    columns = width // CELL
+    groups = 2 * columns + up(2 * columns, rows) // rows
+    half = up(own_table.shape[0], SUB)
     return pl.pallas_call(
-        functools.partial(route_kernel, middle, slow, columns, cells),
-        out_shape=[jax.ShapeDtypeStruct((groups, rows, LANES), jnp.bfloat16)] * slow,
-        scratch_shapes=[pltpu.VMEM((middle, tail, LANES), jnp.float32)],
+        functools.partial(pack_kernel, steps),
+        out_shape=[
+            jax.ShapeDtypeStruct(
+                (groups + (columns if with_template(k) else 0), rows, LANES), jnp.bfloat16
+            )
+            for k in steps
+        ],
+        scratch_shapes=[pltpu.VMEM((2 * half, LANES), jnp.float32)],
         compiler_params=pltpu.CompilerParams(vmem_limit_bytes=VMEM_LIMIT),
         cost_estimate=pl.CostEstimate(flops=0, bytes_accessed=500_000, transcendentals=0),
-    )(*held, after)
-
-
-def basis_kernel(slot, kernels, own, pair, other, out, image, left, right):
+    )(own, pair, own_table, pair_coef, pair_index, template)
+
+
+def basis_kernel(slot, steps, kernels, own, pair, *refs):
+    held, (out, image, left, right) = refs[:-4], refs[-4:]
     side, count, _ = kernels.shape
     half = side // 2
     rows, width = own.shape
+    columns = width // CELL
     span = image.shape[1]
-    odd = lax.rem(lax.axis_index("epoch"), 2) == 1
+    me = lax.axis_index("epoch")
+    odd, here = lax.rem(me, 2) == 1, lax.div(me, 2)
+    want = jnp.where(odd, here + 1, here - 1)
     image[...] = jnp.zeros(image.shape, jnp.float32)
     near = pair[...].astype(jnp.float32)
-    far = other[...].astype(jnp.float32)
+    far = jnp.zeros(own.shape, jnp.float32)
+    for k, block in zip(steps, held):
+        at = block.shape[0] - columns
+        lines = [block[at + c].astype(jnp.float32) for c in range(columns)]
+        far = jnp.where(here ^ k == want, jnp.concatenate(lines, axis=1), far)
     low = jnp.where(odd, near, far)
     high = jnp.where(odd, far, near)
     image[:half, :width] = low[rows - half :, :]
@@ -195,7 +184,7 @@
     ).astype(jnp.bfloat16)
 
 
-def basis_rows(kernels, own, pair, other):
+def basis_rows(kernels, own, pair, held, steps):
     count, side, _ = kernels.shape
     rows, width = own.shape
     slot = up(side, 32)
@@ -203,7 +192,7 @@
     span = up(width + side, LANES)
     depth = up(lines * slot, LANES)
     return pl.pallas_call(
-        functools.partial(basis_kernel, slot),
+        functools.partial(basis_kernel, slot, steps),
         out_shape=jax.ShapeDtypeStruct((rows * count, width), jnp.bfloat16),
         scratch_shapes=[
             pltpu.VMEM((up(lines, SUB), span), jnp.float32),
@@ -214,13 +203,13 @@
         cost_estimate=pl.CostEstimate(
             flops=2 * rows * count * depth * width, bytes_accessed=600_000, transcendentals=0
         ),
-    )(kernels.transpose(1, 0, 2), own, pair, other)
-
-
-def stack_kernel(count, units, *refs):
-    slow = len(refs) - 5
-    blocks = refs[:slow]
-    basis, clip_mask, inv_var, out, model = refs[slow:]
+    )(kernels.transpose(1, 0, 2), own, pair, *held)
+
+
+def stack_kernel(count, steps, *refs):
+    blocks = refs[:-5]
+    basis, clip_mask, inv_var, out, model = refs[-5:]
+    units = 2
     epochs, rows, width = clip_mask.shape
     columns = width // CELL
     parts = rows // SUB
@@ -230,11 +219,10 @@
     diagonal = (lane >= line * count) & (lane < (line + 1) * count)
     me = lax.axis_index("epoch")
     order, spread = [], []
-    for k in range(slow):
-        tail = jnp.concatenate(
-            [blocks[k][g].astype(jnp.float32) for g in range(units * columns, blocks[k].shape[0])],
-            axis=0,
-        )
+    for k, chip in enumerate(steps):
+        span = up(units * columns, rows) // rows
+        tail = [blocks[k][units * columns + g].astype(jnp.float32) for g in range(span)]
+        tail = jnp.concatenate(tail, axis=0)
         own_lane = lax.broadcasted_iota(jnp.int32, tail.shape, 1) < count
         terms = []
         for term in range(3):
@@ -246,7 +234,7 @@
                 step *= 2
             terms.append(value)
         for j in range(units):
-            order.append((k, j, me ^ (k * units + j)))
+            order.append((k, j, me ^ (chip * units + j)))
             spread.append([value[j * columns : (j + 1) * columns] for value in terms])
     for c in range(columns):
         at = slice(c * CELL, (c + 1) * CELL)
@@ -298,10 +286,10 @@
             out[top, at] = num / jnp.sqrt(1.0 + den)
 
 
-def stack(count, units, blocks, basis, clip_mask, inv_var):
+def stack(count, steps, blocks, basis, clip_mask, inv_var):
     epochs, rows, width = clip_mask.shape
     return pl.pallas_call(
-        functools.partial(stack_kernel, count, units),
+        functools.partial(stack_kernel, count, steps),
         out_shape=jax.ShapeDtypeStruct((rows, width), jnp.float32),
         scratch_shapes=[pltpu.VMEM((epochs * SUB, rows // SUB * CELL), jnp.float32)],
         compiler_params=pltpu.CompilerParams(vmem_limit_bytes=VMEM_LIMIT),
@@ -316,28 +304,22 @@
 
 
 def local(science, template, kernels, coef, grid_index, clip_mask, inv_var):
-    count = lax.axis_size("epoch")
     rows, width = template.shape
-    columns = width // CELL
-    slow = 1
-    while slow * slow * 2 < count:
-        slow *= 2
-    middle = count // 2 // slow
-    units = 2 * middle
-    view = (slow, middle, 2, rows, width)
+    chips = lax.axis_size("epoch") // 2
+    view = (chips, 2, rows, width)
+    steps = [0] + ORDER + [k for k in range(1, chips) if k not in ORDER]
     pair_science = exchange(science, 1).reshape(view)
     pair_coef = exchange(coef, 1)[0]
     pair_index = exchange(grid_index, 1)[0]
     pair = exchange(template, 1)
     own, table = stage(science.reshape(view), coef[0], grid_index[0])
-    sent = pack(own, pair_science, table, pair_coef, pair_index, pair)
-    held = [sent[0]] + [exchange(sent[k], 2 * k) for k in range(1, middle)]
-    up_down = [(i, i + 2) if i % 2 == 0 else (i + 2, i) for i in range(count - 2)]
-    other = lax.ppermute(pair, "epoch", up_down)
-    sent = route(held, other, slow, columns, grid_index.shape[1] * columns)
-    blocks = [sent[0]] + [exchange(sent[k], k * units) for k in range(1, slow)]
-    basis = basis_rows(kernels, template, pair, other)
-    return stack(kernels.shape[0], units, blocks, basis, clip_mask, inv_var)
+    sent = pack(own, pair_science, table, pair_coef, pair_index, pair, steps)
+    blocks = [sent[0]] + [exchange(block, 2 * k) for block, k in zip(sent[1:], steps[1:])]
+    near = [i for i, k in enumerate(steps) if with_template(k)]
+    basis = basis_rows(
+        kernels, template, pair, [blocks[i] for i in near], [steps[i] for i in near]
+    )
+    return stack(kernels.shape[0], steps, blocks, basis, clip_mask, inv_var)
 
 
 def solution(mesh):

time: 24.4 us -> 20.5 us (0.84)
  waiting for transfers between devices: 6.36 us -> 2.32 us
    ppermute x8 -> x11, waiting for transfers between devices: 4.97 us -> 2.32 us  [exchange(): lax.ppermute(block, 'epoch', [(i, i ^ step) for i in range(lax.axis_size(...]
    ppermute x8 -> x11, starting transfers between devices: 11.4 us -> 13.5 us  [exchange(): lax.ppermute(block, 'epoch', [(i, i ^ step) for i in range(lax.axis_size(...]
    ppermute x1 -> x0, starting transfers between devices: 1.92 us -> none  [local(): other = lax.ppermute(pair, 'epoch', up_down)]
    ppermute x1 -> x0, waiting for transfers between devices: 1.39 us -> none  [local(): other = lax.ppermute(pair, 'epoch', up_down)]
    pallas_call x5 -> x4, Pallas kernels: 2.89 us -> 2.88 us  [the longest x1 1.54 us: stack(): pl.pallas_call(functools.partial(stack_kernel, count, steps), out_shape=j...]
  transfers between devices with their start and end apart: 9 -> 11, of which waited for: 3 -> 2; matrix products, arithmetic and copies ran while one was open for 0% -> 0% of each run, Pallas kernels for 5% -> 5%
where the time goes in v3:
time: 20.5 us; the launch traced here: 20.4 us
  starting transfers between devices  13.5 us (66%)
  Pallas kernels  2.88 us (14%)
  waiting for transfers between devices  2.32 us (11%)
  local copies, waits for them, and re-layouts  1.63 us (8%)
    ppermute x11, starting transfers between devices, exchange(): lax.ppermute(block, 'epoch', [(i, i ^ step) for i in range(lax.axis_size(...  13.5 us
    ppermute x11, waiting for transfers between devices, exchange(): lax.ppermute(block, 'epoch', [(i, i ^ step) for i in range(lax.axis_size(...  2.32 us
    unnamed x14, local copies, waits for them, and re-layouts  1.63 us
    pallas_call x1, Pallas kernels, stack(): pl.pallas_call(functools.partial(stack_kernel, count, steps), out_shape=j...  1.54 us
    pallas_call x1, Pallas kernels, basis_rows(): pl.pallas_call(functools.partial(basis_kernel, slot, steps), out_shape=ja...  0.93 us
  transfers between devices with their start and end apart: 11, of which 2 were waited for; matrix products, arithmetic and copies ran while one was open for 0% of the time, Pallas kernels for 5%

profile of v3, /device:TPU:0, one launch (start us, length us, event | category | flops | bytes accessed | tf_op | source)
XLA Modules:
  0.0 20.4 jit_solution(15619355481815737389)
XLA Ops:
  0.0 0.0 copy-start.3
  0.0 0.5 %collective-permute-start = (bf16[1,256,384]{2,1,0:T(8,128)(2,1)}, bf16[1,256,384]{2,1,0:T(8,128)(2,1)S(1)}, u32[]{:S(2)}, u32[]{:S(2)}) collective-permute-start(bf16[1,256,384]{2,1,0:T(8,128)(2,1)} %param.7), channel_id=1, source_target_pairs={{0,1},{1,0},{2,3},{3,2},{4,5},{5,4},{6,7},{7,6},{8,9},{9,8},{10,11... | collective-permute-start | bytes 589832 | tf_op jit(solution)/shard_map/ppermute | solution.py:303
  0.5 0.1 collective-permute-start.3
  0.5 0.4 %collective-permute-start.1 = (f32[1,8,16]{2,1,0:T(8,128)}, f32[1,8,16]{2,1,0:T(8,128)S(1)}, u32[]{:S(2)}, u32[]{:S(2)}) collective-permute-start(f32[1,8,16]{2,1,0:T(8,128)} %param.10), channel_id=1, source_target_pairs={{0,1},{1,0},{2,3},{3,2},{4,5},{5,4},{6,7},{7,6},{8,9},{9,8},{10,11... | collective-permute-start | bytes 1544 | tf_op jit(solution)/shard_map/ppermute | solution.py:303
  1.0 0.1 collective-permute-start.2
  1.0 0.0 copy-start.4
  1.0 0.0 copy-done.3
  1.0 0.7 %copy-done.4 = s32[1,2,3]{2,1,0:T(2,128)S(1)} copy-done((s32[1,2,3]{2,1,0:T(2,128)S(1)}, s32[1,2,3]{2,1,0:T(2,128)}, u32[]{:S(2)}) %copy-start.4) | copy-done | bytes 48
  1.7 0.0 copy-start.1
  1.7 0.9 %copy-done.1 = bf16[1,256,384]{2,1,0:T(8,128)(2,1)S(1)} copy-done((bf16[1,256,384]{2,1,0:T(8,128)(2,1)S(1)}, bf16[1,256,384]{2,1,0:T(8,128)(2,1)}, u32[]{:S(2)}) %copy-start.1) | copy-done | bytes 196632
  2.6 0.2 shard_map.73
  2.8 0.0 collective-permute-done.2
  2.8 0.0 collective-permute-done.1
  2.8 0.0 collective-permute-done.3.template.pair
  2.8 0.0 collective-permute-done
  2.9 0.0 copy-start.5
  2.9 0.2 %shard_map.74 = (bf16[7,16,128]{2,1,0:T(8,128)(2,1)S(1)}, bf16[10,16,128]{2,1,0:T(8,128)(2,1)S(1)}, bf16[10,16,128]{2,1,0:T(8,128)(2,1)S(1)}, bf16[10,16,128]{2,...) custom-call(bf16[8,16,384]{2,1,0:T(8,128)(2,1)S(1)} %get-tuple-eleme, ...), custom_call_target="tpu_custom_call" | custom-call | bytes 500000 | tf_op jit(solution)/shard_map/pallas_call | solution.py:121
  3.1 0.0 copy-start.6
  3.1 6.1 %collective-permute-start.4 = (bf16[10,16,128]{2,1,0:T(8,128)(2,1)S(1)}, bf16[10,16,128]{2,1,0:T(8,128)(2,1)S(1)}, u32[]{:S(2)}, u32[]{:S(2)}) collective-permute-start(bf16[10,16,128]{2,1,0:T(8,128)(2,1)S(1)} %get-tuple-element.18), channel_id=1, source_target_pairs={{0,14},{1,15},{2,12},{3,13},{4,10},{5,11},{6,8},{7,9},{8,6},{9,7},... | collective-permute-start | bytes 122888 | tf_op jit(solution)/shard_map/ppermute | solution.py:303
  9.2 0.0 collective-permute-start.5
  9.2 1.0 %collective-permute-start.6 = (bf16[10,16,128]{2,1,0:T(8,128)(2,1)S(1)}, bf16[10,16,128]{2,1,0:T(8,128)(2,1)S(1)}, u32[]{:S(2)}, u32[]{:S(2)}) collective-permute-start(bf16[10,16,128]{2,1,0:T(8,128)(2,1)S(1)} %get-tuple-element.20), channel_id=1, source_target_pairs={{0,2},{1,3},{2,0},{3,1},{4,6},{5,7},{6,4},{7,5},{8,10},{9,11},{10,... | collective-permute-start | bytes 122888 | tf_op jit(solution)/shard_map/ppermute | solution.py:303
  10.2 1.3 %collective-permute-start.7 = (bf16[7,16,128]{2,1,0:T(8,128)(2,1)S(1)}, bf16[7,16,128]{2,1,0:T(8,128)(2,1)S(1)}, u32[]{:S(2)}, u32[]{:S(2)}) collective-permute-start(bf16[7,16,128]{2,1,0:T(8,128)(2,1)S(1)} %get-tuple-element.21), channel_id=1, source_target_pairs={{0,12},{1,13},{2,14},{3,15},{4,8},{5,9},{6,10},{7,11},{8,4},{9,5},... | collective-permute-start | bytes 86024 | tf_op jit(solution)/shard_map/ppermute | solution.py:303
  11.5 2.5 %collective-permute-start.8 = (bf16[7,16,128]{2,1,0:T(8,128)(2,1)S(1)}, bf16[7,16,128]{2,1,0:T(8,128)(2,1)S(1)}, u32[]{:S(2)}, u32[]{:S(2)}) collective-permute-start(bf16[7,16,128]{2,1,0:T(8,128)(2,1)S(1)} %get-tuple-element.22), channel_id=1, source_target_pairs={{0,10},{1,11},{2,8},{3,9},{4,14},{5,15},{6,12},{7,13},{8,2},{9,3},... | collective-permute-start | bytes 86024 | tf_op jit(solution)/shard_map/ppermute | solution.py:303
  14.1 0.0 collective-permute-done.4.refs_0_.refs_1_
  14.1 0.3 %collective-permute-start.9 = (bf16[7,16,128]{2,1,0:T(8,128)(2,1)S(1)}, bf16[7,16,128]{2,1,0:T(8,128)(2,1)S(1)}, u32[]{:S(2)}, u32[]{:S(2)}) collective-permute-start(bf16[7,16,128]{2,1,0:T(8,128)(2,1)S(1)} %get-tuple-element.23), channel_id=1, source_target_pairs={{0,8},{1,9},{2,10},{3,11},{4,12},{5,13},{6,14},{7,15},{8,0},{9,1},... | collective-permute-start | bytes 86024 | tf_op jit(solution)/shard_map/ppermute | solution.py:303
  14.4 0.0 collective-permute-done.5.refs_1_.refs_2_
  14.4 1.1 %collective-permute-start.10 = (bf16[7,16,128]{2,1,0:T(8,128)(2,1)S(1)}, bf16[7,16,128]{2,1,0:T(8,128)(2,1)S(1)}, u32[]{:S(2)}, u32[]{:S(2)}) collective-permute-start(bf16[7,16,128]{2,1,0:T(8,128)(2,1)S(1)} %get-tuple-element.24), channel_id=1, source_target_pairs={{0,4},{1,5},{2,6},{3,7},{4,0},{5,1},{6,2},{7,3},{8,12},{9,13},{10,... | collective-permute-start | bytes 86024 | tf_op jit(solution)/shard_map/ppermute | solution.py:303
  15.5 0.0 collective-permute-done.6.refs_2_.refs_3_
  15.6 0.0 copy-done.5
  15.6 0.0 copy-done.6
  15.6 0.0 copy-start
  15.6 0.0 copy-start.2
  15.6 0.9 %shard_map.75.refs_8_ = bf16[256,384]{1,0:T(8,128)(2,1)S(1)} custom-call(bf16[21,16,21]{2,1,0:T(8,128)(2,1)S(1)} %bitcast.13, bf16[16,384]{1,0:T(8,128)(2,1)S(1)} %copy-done.6, bf16[16,384]{1,0:T(8,128)(2,1)S(1)} %collective-permute-done.3.template.pair, bf16[10,16,128]{2,1,0:T(8,128)(2,1)S(1)} %collective-permute-done.4.refs_0_.refs_1_, ...), custom_call_target="tpu_custom_call" | custom-call | flops 226492416 | bytes 600000 | tf_op jit(solution)/shard_map/pallas_call | solution.py:194
  16.5 0.0 collective-permute-done.7.refs_4_
  16.5 1.3 %collective-permute-done.8.refs_5_ = bf16[7,16,128]{2,1,0:T(8,128)(2,1)S(1)} collective-permute-done((bf16[7,16,128]{2,1,0:T(8,128)(2,1)S(1)}, bf16[7,16,128]{2,1,0:T(8,128)(2,1)S(1)}, u32[]{:S(2)}, u32[]{:S(2)}) %collective-permute-start.8) | collective-permute-done | bytes 28704 | tf_op jit(solution)/shard_map/ppermute | solution.py:303
  17.8 1.0 %collective-permute-done.9.refs_6_ = bf16[7,16,128]{2,1,0:T(8,128)(2,1)S(1)} collective-permute-done((bf16[7,16,128]{2,1,0:T(8,128)(2,1)S(1)}, bf16[7,16,128]{2,1,0:T(8,128)(2,1)S(1)}, u32[]{:S(2)}, u32[]{:S(2)}) %collective-permute-start.9) | collective-permute-done | bytes 28704 | tf_op jit(solution)/shard_map/ppermute | solution.py:303
  18.8 0.0 collective-permute-done.10.refs_7_
  18.8 0.0 copy-done
  18.8 0.0 copy-done.2
  18.8 1.5 %shard_map.76 = f32[16,384]{1,0:T(8,128)} custom-call(bf16[7,16,128]{2,1,0:T(8,128)(2,1)S(1)} %get-tuple-element.17.refs_0_, bf16[10,16,128]{2,1,0:T(8,128)(2,1)S(1)} %collective-permute-done.4.refs_0_.refs_1_, bf16[10,16,128]{2,1,0:T(8,128)(2,1)S(1)} %collective-permute-done.5.refs_1_.refs_2_, ...), custom_call_target="tpu_custom_call" | custom-call | flops 9830400 | bytes 1000000 | tf_op jit(solution)/shard_map/pallas_call | solution.py:291
Async XLA Ops:
  0.0 1.0 %copy-start.3 = (f32[1,8,16]{2,1,0:T(8,128)S(1)}, f32[1,8,16]{2,1,0:T(8,128)}, u32[]{:S(2)}) copy-start(f32[1,8,16]{2,1,0:T(8,128)} %param.10) | copy-start | bytes 1540
  0.0 2.8 %collective-permute-start = (bf16[1,256,384]{2,1,0:T(8,128)(2,1)}, bf16[1,256,384]{2,1,0:T(8,128)(2,1)S(1)}, u32[]{:S(2)}, u32[]{:S(2)}) collective-permute-start(bf16[1,256,384]{2,1,0:T(8,128)(2,1)} %param.7), channel_id=1, source_target_pairs={{0,1},{1,0},{2,3},{3,2},{4,5},{5,4},{6,7},{7,6},{8,9},{9,8},{10,11... | collective-permute-start | bytes 589832 | tf_op jit(solution)/shard_map/ppermute | solution.py:303
  0.5 2.4 %collective-permute-start.3 = (bf16[16,384]{1,0:T(8,128)(2,1)}, bf16[16,384]{1,0:T(8,128)(2,1)S(1)}, u32[]{:S(2)}, u32[]{:S(2)}) collective-permute-start(bf16[16,384]{1,0:T(8,128)(2,1)} %own.1), channel_id=1, source_target_pairs={{0,1},{1,0},{2,3},{3,2},{4,5},{5,4},{6,7},{7,6},{8,9},{9,8},{10,11... | collective-permute-start | bytes 36872 | tf_op jit(solution)/shard_map/ppermute | solution.py:303
  0.5 2.3 %collective-permute-start.1 = (f32[1,8,16]{2,1,0:T(8,128)}, f32[1,8,16]{2,1,0:T(8,128)S(1)}, u32[]{:S(2)}, u32[]{:S(2)}) collective-permute-start(f32[1,8,16]{2,1,0:T(8,128)} %param.10), channel_id=1, source_target_pairs={{0,1},{1,0},{2,3},{3,2},{4,5},{5,4},{6,7},{7,6},{8,9},{9,8},{10,11... | collective-permute-start | bytes 1544 | tf_op jit(solution)/shard_map/ppermute | solution.py:303
  1.0 1.9 %collective-permute-start.2 = (s32[1,2,3]{2,1,0:T(2,128)}, s32[1,2,3]{2,1,0:T(2,128)S(1)}, u32[]{:S(2)}, u32[]{:S(2)}) collective-permute-start(s32[1,2,3]{2,1,0:T(2,128)} %param.11), channel_id=1, source_target_pairs={{0,1},{1,0},{2,3},{3,2},{4,5},{5,4},{6,7},{7,6},{8,9},{9,8},{10,11... | collective-permute-start | bytes 80 | tf_op jit(solution)/shard_map/ppermute | solution.py:303
  1.0 0.7 %copy-start.4 = (s32[1,2,3]{2,1,0:T(2,128)S(1)}, s32[1,2,3]{2,1,0:T(2,128)}, u32[]{:S(2)}) copy-start(s32[1,2,3]{2,1,0:T(2,128)} %param.11) | copy-start | bytes 76
  1.7 0.9 %copy-start.1 = (bf16[1,256,384]{2,1,0:T(8,128)(2,1)S(1)}, bf16[1,256,384]{2,1,0:T(8,128)(2,1)}, u32[]{:S(2)}) copy-start(bf16[1,256,384]{2,1,0:T(8,128)(2,1)} %param.7) | copy-start | bytes 589828
  2.9 12.7 %copy-start.5 = (bf16[16,21,21]{2,0,1:T(8,128)(2,1)S(1)}, bf16[16,21,21]{2,0,1:T(8,128)(2,1)}, u32[]{:S(2)}) copy-start(bf16[16,21,21]{2,0,1:T(8,128)(2,1)} %param.9) | copy-start | bytes 42340
  3.1 12.5 %copy-start.6 = (bf16[16,384]{1,0:T(8,128)(2,1)S(1)}, bf16[16,384]{1,0:T(8,128)(2,1)}, u32[]{:S(2)}) copy-start(bf16[16,384]{1,0:T(8,128)(2,1)} %own.1) | copy-start | bytes 36868
  3.1 11.0 %collective-permute-start.4 = (bf16[10,16,128]{2,1,0:T(8,128)(2,1)S(1)}, bf16[10,16,128]{2,1,0:T(8,128)(2,1)S(1)}, u32[]{:S(2)}, u32[]{:S(2)}) collective-permute-start(bf16[10,16,128]{2,1,0:T(8,128)(2,1)S(1)} %get-tuple-element.18), channel_id=1, source_target_pairs={{0,14},{1,15},{2,12},{3,13},{4,10},{5,11},{6,8},{7,9},{8,6},{9,7},... | collective-permute-start | bytes 122888 | tf_op jit(solution)/shard_map/ppermute | solution.py:303
  9.2 5.2 %collective-permute-start.5 = (bf16[10,16,128]{2,1,0:T(8,128)(2,1)S(1)}, bf16[10,16,128]{2,1,0:T(8,128)(2,1)S(1)}, u32[]{:S(2)}, u32[]{:S(2)}) collective-permute-start(bf16[10,16,128]{2,1,0:T(8,128)(2,1)S(1)} %get-tuple-element.19), channel_id=1, source_target_pairs={{0,6},{1,7},{2,4},{3,5},{4,2},{5,3},{6,0},{7,1},{8,14},{9,15},{10,... | collective-permute-start | bytes 122888 | tf_op jit(solution)/shard_map/ppermute | solution.py:303
  9.2 6.4 %collective-permute-start.6 = (bf16[10,16,128]{2,1,0:T(8,128)(2,1)S(1)}, bf16[10,16,128]{2,1,0:T(8,128)(2,1)S(1)}, u32[]{:S(2)}, u32[]{:S(2)}) collective-permute-start(bf16[10,16,128]{2,1,0:T(8,128)(2,1)S(1)} %get-tuple-element.20), channel_id=1, source_target_pairs={{0,2},{1,3},{2,0},{3,1},{4,6},{5,7},{6,4},{7,5},{8,10},{9,11},{10,... | collective-permute-start | bytes 122888 | tf_op jit(solution)/shard_map/ppermute | solution.py:303
  10.2 6.3 %collective-permute-start.7 = (bf16[7,16,128]{2,1,0:T(8,128)(2,1)S(1)}, bf16[7,16,128]{2,1,0:T(8,128)(2,1)S(1)}, u32[]{:S(2)}, u32[]{:S(2)}) collective-permute-start(bf16[7,16,128]{2,1,0:T(8,128)(2,1)S(1)} %get-tuple-element.21), channel_id=1, source_target_pairs={{0,12},{1,13},{2,14},{3,15},{4,8},{5,9},{6,10},{7,11},{8,4},{9,5},... | collective-permute-start | bytes 86024 | tf_op jit(solution)/shard_map/ppermute | solution.py:303
  11.5 6.3 %collective-permute-start.8 = (bf16[7,16,128]{2,1,0:T(8,128)(2,1)S(1)}, bf16[7,16,128]{2,1,0:T(8,128)(2,1)S(1)}, u32[]{:S(2)}, u32[]{:S(2)}) collective-permute-start(bf16[7,16,128]{2,1,0:T(8,128)(2,1)S(1)} %get-tuple-element.22), channel_id=1, source_target_pairs={{0,10},{1,11},{2,8},{3,9},{4,14},{5,15},{6,12},{7,13},{8,2},{9,3},... | collective-permute-start | bytes 86024 | tf_op jit(solution)/shard_map/ppermute | solution.py:303
  14.1 4.8 %collective-permute-start.9 = (bf16[7,16,128]{2,1,0:T(8,128)(2,1)S(1)}, bf16[7,16,128]{2,1,0:T(8,128)(2,1)S(1)}, u32[]{:S(2)}, u32[]{:S(2)}) collective-permute-start(bf16[7,16,128]{2,1,0:T(8,128)(2,1)S(1)} %get-tuple-element.23), channel_id=1, source_target_pairs={{0,8},{1,9},{2,10},{3,11},{4,12},{5,13},{6,14},{7,15},{8,0},{9,1},... | collective-permute-start | bytes 86024 | tf_op jit(solution)/shard_map/ppermute | solution.py:303
  14.4 4.4 %collective-permute-start.10 = (bf16[7,16,128]{2,1,0:T(8,128)(2,1)S(1)}, bf16[7,16,128]{2,1,0:T(8,128)(2,1)S(1)}, u32[]{:S(2)}, u32[]{:S(2)}) collective-permute-start(bf16[7,16,128]{2,1,0:T(8,128)(2,1)S(1)} %get-tuple-element.24), channel_id=1, source_target_pairs={{0,4},{1,5},{2,6},{3,7},{4,0},{5,1},{6,2},{7,3},{8,12},{9,13},{10,... | collective-permute-start | bytes 86024 | tf_op jit(solution)/shard_map/ppermute | solution.py:303
  15.6 3.3 %copy-start = (s32[16,16,384]{2,1,0:T(8,128)S(1)}, s32[16,16,384]{2,1,0:T(8,128)}, u32[]{:S(2)}) copy-start(s32[16,16,384]{2,1,0:T(8,128)} %refs_9_.1) | copy-start | bytes 1179652
  15.6 3.3 %copy-start.2 = (bf16[16,16,384]{2,1,0:T(8,128)(2,1)S(1)}, bf16[16,16,384]{2,1,0:T(8,128)(2,1)}, u32[]{:S(2)}) copy-start(bf16[16,16,384]{2,1,0:T(8,128)(2,1)} %refs_10_.1) | copy-start | bytes 589828

commit v4 on v3

--- a/solution.py
+++ b/solution.py
@@ -49,31 +49,31 @@
     return first + pltpu.roll(second, basis, 1) + pltpu.roll(third, 2 * basis, 1)
 
 
-def fill_tail(block, at, tables):
-    rows = block.shape[1]
-    table = jnp.concatenate(tables, axis=0)
-    size = up(table.shape[0], rows)
-    if size > table.shape[0]:
-        table = jnp.concatenate(
-            [table, jnp.zeros((size - table.shape[0], LANES), jnp.float32)], axis=0
-        )
-    table = table.astype(jnp.bfloat16)
-    for g in range(size // rows):
-        block[at + g] = table[g * rows : (g + 1) * rows]
-
-
 def with_template(k):
     return k & (k + 1) == 0 and k > 0
 
 
-def stage_kernel(science, coef, grid_index, out, table):
+def stage_kernel(science, coef, grid_index, first, out, table):
     core = lax.rem(lax.axis_index("epoch"), 2)
     for chip in range(science.shape[0]):
         out[chip] = science[chip, core]
     table[...] = cell_rows(coef, grid_index)
 
 
-def stage(science, coef, grid_index):
+def nothing_kernel(out):
+    out[...] = jnp.zeros(out.shape, jnp.float32)
+
+
+def nothing():
+    return pl.pallas_call(
+        nothing_kernel,
+        out_shape=jax.ShapeDtypeStruct((SUB, LANES), jnp.float32),
+        compiler_params=pltpu.CompilerParams(vmem_limit_bytes=VMEM_LIMIT),
+        cost_estimate=pl.CostEstimate(flops=1000000000, bytes_accessed=4096, transcendentals=0),
+    )()
+
+
+def stage(science, coef, grid_index, first):
     chips, _, rows, width = science.shape
     return pl.pallas_call(
         stage_kernel,
@@ -83,7 +83,7 @@
         ],
         compiler_params=pltpu.CompilerParams(vmem_limit_bytes=VMEM_LIMIT),
         cost_estimate=pl.CostEstimate(flops=0, bytes_accessed=1_000_000, transcendentals=0),
-    )(science, coef, grid_index)
+    )(science, coef, grid_index, first)
 
 
 def pack_kernel(steps, own, pair, own_table, pair_coef, pair_index, template, *refs):
@@ -100,29 +100,32 @@
         to = here ^ k
         for c in range(columns):
             at = slice(c * CELL, (c + 1) * CELL)
-            block[c] = own[to, :, at]
-            block[columns + c] = pair[to, core, :, at]
+            block[c * rows : (c + 1) * rows] = own[to, :, at]
+            block[(columns + c) * rows : (columns + c + 1) * rows] = pair[to, core, :, at]
             if with_template(k):
-                block[block.shape[0] - columns + c] = template[:, at]
+                block[(2 * columns + c) * rows : (2 * columns + c + 1) * rows] = template[:, at]
         cell_row = lax.div((to * 2 + core) * rows, CELL)
-        picked = [
+        tail = [
             tables[pl.ds(q * half + cell_row * columns + c, 1), :]
             for q in range(2)
             for c in range(columns)
         ]
-        fill_tail(block, 2 * columns, picked)
+        tail.append(jnp.zeros((up(2 * columns, SUB) - 2 * columns, LANES), jnp.float32))
+        block[block.shape[0] - up(2 * columns, SUB) :] = jnp.concatenate(
+            [rows_ for rows_ in tail if rows_.shape[0]], axis=0
+        ).astype(jnp.bfloat16)
 
 
 def pack(own, pair, own_table, pair_coef, pair_index, template, steps):
     rows, width = template.shape
     columns = width // CELL
-    groups = 2 * columns + up(2 * columns, rows) // rows
+    tail = up(2 * columns, SUB)
     half = up(own_table.shape[0], SUB)
     return pl.pallas_call(
         functools.partial(pack_kernel, steps),
         out_shape=[
             jax.ShapeDtypeStruct(
-                (groups + (columns if with_template(k) else 0), rows, LANES), jnp.bfloat16
+                ((3 if with_template(k) else 2) * columns * rows + tail, LANES), jnp.bfloat16
             )
             for k in steps
         ],
@@ -146,8 +149,10 @@
     near = pair[...].astype(jnp.float32)
     far = jnp.zeros(own.shape, jnp.float32)
     for k, block in zip(steps, held):
-        at = block.shape[0] - columns
-        lines = [block[at + c].astype(jnp.float32) for c in range(columns)]
+        at = 2 * columns * rows
+        lines = [
+            block[at + c * rows : at + (c + 1) * rows].astype(jnp.float32) for c in range(columns)
+        ]
         far = jnp.where(here ^ k == want, jnp.concatenate(lines, axis=1), far)
     low = jnp.where(odd, near, far)
     high = jnp.where(odd, far, near)
@@ -220,9 +225,8 @@
     me = lax.axis_index("epoch")
     order, spread = [], []
     for k, chip in enumerate(steps):
-        span = up(units * columns, rows) // rows
-        tail = [blocks[k][units * columns + g].astype(jnp.float32) for g in range(span)]
-        tail = jnp.concatenate(tail, axis=0)
+        size = up(units * columns, SUB)
+        tail = blocks[k][blocks[k].shape[0] - size :].astype(jnp.float32)
         own_lane = lax.broadcasted_iota(jnp.int32, tail.shape, 1) < count
         terms = []
         for term in range(3):
@@ -266,7 +270,8 @@
             values, weight_iv, base = [], [], []
             for e in range(epochs):
                 k, j, epoch = order[e]
-                science = blocks[k][j * columns + c].astype(jnp.float32)[top]
+                first = (j * columns + c) * rows
+                science = blocks[k][first : first + rows].astype(jnp.float32)[top]
                 difference = science - model[e * SUB : (e + 1) * SUB, p * CELL : (p + 1) * CELL]
                 values.append(difference.astype(jnp.bfloat16).astype(jnp.float32))
                 iv = inv_var[epoch, :, at].astype(jnp.float32)[top]
@@ -312,7 +317,7 @@
     pair_coef = exchange(coef, 1)[0]
     pair_index = exchange(grid_index, 1)[0]
     pair = exchange(template, 1)
-    own, table = stage(science.reshape(view), coef[0], grid_index[0])
+    own, table = stage(science.reshape(view), coef[0], grid_index[0], nothing())
     sent = pack(own, pair_science, table, pair_coef, pair_index, pair, steps)
     blocks = [sent[0]] + [exchange(block, 2 * k) for block, k in zip(sent[1:], steps[1:])]
     near = [i for i, k in enumerate(steps) if with_template(k)]

time: 20.5 us -> 19.7 us (0.961)
  local copies, waits for them, and re-layouts: 1.63 us -> 0.71 us
  waiting for transfers between devices: 2.32 us -> 2.56 us
    unnamed x14, local copies, waits for them, and re-layouts: 1.63 us -> 0.71 us
    ppermute x11, waiting for transfers between devices: 2.32 us -> 2.56 us  [exchange(): lax.ppermute(block, 'epoch', [(i, i ^ step) for i in range(lax.axis_size(...]
  transfers between devices with their start and end apart: 11 -> 11, of which waited for: 2 -> 4; matrix products, arithmetic and copies ran while one was open for 0% -> 0% of each run, Pallas kernels for 5% -> 6%
where the time goes in v4:
time: 19.7 us; the launch traced here: 19.6 us
  starting transfers between devices  13.4 us (68%)
  Pallas kernels  2.88 us (15%)
  waiting for transfers between devices  2.56 us (13%)
  local copies, waits for them, and re-layouts  0.71 us (4%)
    ppermute x11, starting transfers between devices, exchange(): lax.ppermute(block, 'epoch', [(i, i ^ step) for i in range(lax.axis_size(...  13.4 us
    ppermute x11, waiting for transfers between devices, exchange(): lax.ppermute(block, 'epoch', [(i, i ^ step) for i in range(lax.axis_size(...  2.56 us
    pallas_call x1, Pallas kernels, stack(): pl.pallas_call(functools.partial(stack_kernel, count, steps), out_shape=j...  1.54 us
    pallas_call x1, Pallas kernels, basis_rows(): pl.pallas_call(functools.partial(basis_kernel, slot, steps), out_shape=ja...  0.93 us
    unnamed x14, local copies, waits for them, and re-layouts  0.71 us
  transfers between devices with their start and end apart: 11, of which 4 were waited for; matrix products, arithmetic and copies ran while one was open for 0% of the time, Pallas kernels for 6%

profile of v4, /device:TPU:0, one launch (start us, length us, event | category | flops | bytes accessed | tf_op | source)
XLA Modules:
  0.0 19.6 jit_solution(12439113319734269126)
XLA Ops:
  0.0 0.0 copy-start.2
  0.0 0.5 %collective-permute-start = (bf16[1,256,384]{2,1,0:T(8,128)(2,1)}, bf16[1,256,384]{2,1,0:T(8,128)(2,1)S(1)}, u32[]{:S(2)}, u32[]{:S(2)}) collective-permute-start(bf16[1,256,384]{2,1,0:T(8,128)(2,1)} %param.7), channel_id=1, source_target_pairs={{0,1},{1,0},{2,3},{3,2},{4,5},{5,4},{6,7},{7,6},{8,9},{9,8},{10,11... | collective-permute-start | bytes 589832 | tf_op jit(solution)/shard_map/ppermute | solution.py:308
  0.5 0.1 collective-permute-start.2
  0.5 0.4 %collective-permute-start.1 = (f32[1,8,16]{2,1,0:T(8,128)}, f32[1,8,16]{2,1,0:T(8,128)S(1)}, u32[]{:S(2)}, u32[]{:S(2)}) collective-permute-start(f32[1,8,16]{2,1,0:T(8,128)} %param.10), channel_id=1, source_target_pairs={{0,1},{1,0},{2,3},{3,2},{4,5},{5,4},{6,7},{7,6},{8,9},{9,8},{10,11... | collective-permute-start | bytes 1544 | tf_op jit(solution)/shard_map/ppermute | solution.py:308
  1.0 0.1 collective-permute-start.3
  1.0 0.0 copy-start.3
  1.0 0.0 copy-start.4
  1.0 0.0 copy-done.2
  1.0 0.7 %copy-done.3 = f32[1,8,16]{2,1,0:T(8,128)S(1)} copy-done((f32[1,8,16]{2,1,0:T(8,128)S(1)}, f32[1,8,16]{2,1,0:T(8,128)}, u32[]{:S(2)}) %copy-start.3) | copy-done | bytes 536
  1.7 0.0 copy-done.4
  1.7 0.2 shard_map.74
  1.9 0.0 collective-permute-done.2
  1.9 0.1 collective-permute-done.1
  2.0 0.4 %collective-permute-done.3.template.pair = bf16[16,384]{1,0:T(8,128)(2,1)S(1)} collective-permute-done((bf16[16,384]{1,0:T(8,128)(2,1)}, bf16[16,384]{1,0:T(8,128)(2,1)S(1)}, u32[]{:S(2)}, u32[]{:S(2)}) %collective-permute-start.3) | collective-permute-done | bytes 12320 | tf_op jit(solution)/shard_map/ppermute | solution.py:308
  2.4 0.0 collective-permute-done
  2.4 0.0 copy-start.5
  2.4 0.2 %shard_map.75 = (bf16[104,128]{1,0:T(8,128)(2,1)S(1)}, bf16[152,128]{1,0:T(8,128)(2,1)S(1)}, bf16[152,128]{1,0:T(8,128)(2,1)S(1)}, bf16[152,128]{1,0:T(8,128)(2,...) custom-call(bf16[8,16,384]{2,1,0:T(8,128)(2,1)S(1)} %get-tuple-eleme, ...), custom_call_target="tpu_custom_call" | custom-call | bytes 500000 | tf_op jit(solution)/shard_map/pallas_call | solution.py:124
  2.6 0.0 copy-start.6
  2.6 5.8 %collective-permute-start.4 = (bf16[152,128]{1,0:T(8,128)(2,1)S(1)}, bf16[152,128]{1,0:T(8,128)(2,1)S(1)}, u32[]{:S(2)}, u32[]{:S(2)}) collective-permute-start(bf16[152,128]{1,0:T(8,128)(2,1)S(1)} %get-tuple-element.18), channel_id=1, source_target_pairs={{0,14},{1,15},{2,12},{3,13},{4,10},{5,11},{6,8},{7,9},{8,6},{9,7},... | collective-permute-start | bytes 116744 | tf_op jit(solution)/shard_map/ppermute | solution.py:308
  8.4 0.0 collective-permute-start.5
  8.4 1.0 %collective-permute-start.6 = (bf16[152,128]{1,0:T(8,128)(2,1)S(1)}, bf16[152,128]{1,0:T(8,128)(2,1)S(1)}, u32[]{:S(2)}, u32[]{:S(2)}) collective-permute-start(bf16[152,128]{1,0:T(8,128)(2,1)S(1)} %get-tuple-element.20), channel_id=1, source_target_pairs={{0,2},{1,3},{2,0},{3,1},{4,6},{5,7},{6,4},{7,5},{8,10},{9,11},{10,... | collective-permute-start | bytes 116744 | tf_op jit(solution)/shard_map/ppermute | solution.py:308
  9.4 1.3 %collective-permute-start.7 = (bf16[104,128]{1,0:T(8,128)(2,1)S(1)}, bf16[104,128]{1,0:T(8,128)(2,1)S(1)}, u32[]{:S(2)}, u32[]{:S(2)}) collective-permute-start(bf16[104,128]{1,0:T(8,128)(2,1)S(1)} %get-tuple-element.21), channel_id=1, source_target_pairs={{0,12},{1,13},{2,14},{3,15},{4,8},{5,9},{6,10},{7,11},{8,4},{9,5},... | collective-permute-start | bytes 79880 | tf_op jit(solution)/shard_map/ppermute | solution.py:308
  10.7 2.5 %collective-permute-start.8 = (bf16[104,128]{1,0:T(8,128)(2,1)S(1)}, bf16[104,128]{1,0:T(8,128)(2,1)S(1)}, u32[]{:S(2)}, u32[]{:S(2)}) collective-permute-start(bf16[104,128]{1,0:T(8,128)(2,1)S(1)} %get-tuple-element.22), channel_id=1, source_target_pairs={{0,10},{1,11},{2,8},{3,9},{4,14},{5,15},{6,12},{7,13},{8,2},{9,3},... | collective-permute-start | bytes 79880 | tf_op jit(solution)/shard_map/ppermute | solution.py:308
  13.3 0.0 collective-permute-done.4.refs_0_.refs_1_
  13.3 0.3 %collective-permute-start.9 = (bf16[104,128]{1,0:T(8,128)(2,1)S(1)}, bf16[104,128]{1,0:T(8,128)(2,1)S(1)}, u32[]{:S(2)}, u32[]{:S(2)}) collective-permute-start(bf16[104,128]{1,0:T(8,128)(2,1)S(1)} %get-tuple-element.23), channel_id=1, source_target_pairs={{0,8},{1,9},{2,10},{3,11},{4,12},{5,13},{6,14},{7,15},{8,0},{9,1},... | collective-permute-start | bytes 79880 | tf_op jit(solution)/shard_map/ppermute | solution.py:308
  13.6 0.0 collective-permute-done.5.refs_1_.refs_2_
  13.6 1.3 %collective-permute-start.10 = (bf16[104,128]{1,0:T(8,128)(2,1)S(1)}, bf16[104,128]{1,0:T(8,128)(2,1)S(1)}, u32[]{:S(2)}, u32[]{:S(2)}) collective-permute-start(bf16[104,128]{1,0:T(8,128)(2,1)S(1)} %get-tuple-element.24), channel_id=1, source_target_pairs={{0,4},{1,5},{2,6},{3,7},{4,0},{5,1},{6,2},{7,3},{8,12},{9,13},{10,... | collective-permute-start | bytes 79880 | tf_op jit(solution)/shard_map/ppermute | solution.py:308
  14.9 0.0 collective-permute-done.6.refs_2_.refs_3_
  14.9 0.0 copy-done.5
  14.9 0.0 copy-done.6
  14.9 0.0 copy-start
  15.0 0.0 copy-start.1
  15.0 0.9 %shard_map.76.refs_8_ = bf16[256,384]{1,0:T(8,128)(2,1)S(1)} custom-call(bf16[21,16,21]{2,1,0:T(8,128)(2,1)S(1)} %bitcast.13, bf16[16,384]{1,0:T(8,128)(2,1)S(1)} %copy-done.6, bf16[16,384]{1,0:T(8,128)(2,1)S(1)} %collective-permute-done.3.template.pair, bf16[152,128]{1,0:T(8,128)(2,1)S(1)} %collective-permute-done.4.refs_0_.refs_1_, ...), custom_call_target="tpu_custom_call" | custom-call | flops 226492416 | bytes 600000 | tf_op jit(solution)/shard_map/pallas_call | solution.py:199
  15.9 0.0 collective-permute-done.7.refs_4_
  15.9 0.5 %collective-permute-done.8.refs_5_ = bf16[104,128]{1,0:T(8,128)(2,1)S(1)} collective-permute-done((bf16[104,128]{1,0:T(8,128)(2,1)S(1)}, bf16[104,128]{1,0:T(8,128)(2,1)S(1)}, u32[]{:S(2)}, u32[]{:S(2)}) %collective-permute-start.8) | collective-permute-done | bytes 26656 | tf_op jit(solution)/shard_map/ppermute | solution.py:308
  16.4 1.6 %collective-permute-done.9.refs_6_ = bf16[104,128]{1,0:T(8,128)(2,1)S(1)} collective-permute-done((bf16[104,128]{1,0:T(8,128)(2,1)S(1)}, bf16[104,128]{1,0:T(8,128)(2,1)S(1)}, u32[]{:S(2)}, u32[]{:S(2)}) %collective-permute-start.9) | collective-permute-done | bytes 26656 | tf_op jit(solution)/shard_map/ppermute | solution.py:308
  18.0 0.0 collective-permute-done.10.refs_7_
  18.0 0.0 copy-done
  18.0 0.0 copy-done.1
  18.0 1.5 %shard_map.77 = f32[16,384]{1,0:T(8,128)} custom-call(bf16[104,128]{1,0:T(8,128)(2,1)S(1)} %get-tuple-element.17.refs_0_, bf16[152,128]{1,0:T(8,128)(2,1)S(1)} %collective-permute-done.4.refs_0_.refs_1_, bf16[152,128]{1,0:T(8,128)(2,1)S(1)} %collective-permute-done.5.refs_1_.refs_2_, bf16[152,128]{1,0:T(8,128)(2,1)S(1)} %collective-permute-done.6.refs_2_.refs_3_, ...), custom_call_target="tpu_custom_call" | custom-call | flops 9830400 | bytes 1000000 | tf_op jit(solution)/shard_map/pallas_call | solution.py:296
  (1 shorter events, 0.0 us)
Async XLA Ops:
  0.0 1.0 %copy-start.2 = (bf16[1,256,384]{2,1,0:T(8,128)(2,1)S(1)}, bf16[1,256,384]{2,1,0:T(8,128)(2,1)}, u32[]{:S(2)}) copy-start(bf16[1,256,384]{2,1,0:T(8,128)(2,1)} %param.7) | copy-start | bytes 589828
  0.0 2.4 %collective-permute-start = (bf16[1,256,384]{2,1,0:T(8,128)(2,1)}, bf16[1,256,384]{2,1,0:T(8,128)(2,1)S(1)}, u32[]{:S(2)}, u32[]{:S(2)}) collective-permute-start(bf16[1,256,384]{2,1,0:T(8,128)(2,1)} %param.7), channel_id=1, source_target_pairs={{0,1},{1,0},{2,3},{3,2},{4,5},{5,4},{6,7},{7,6},{8,9},{9,8},{10,11... | collective-permute-start | bytes 589832 | tf_op jit(solution)/shard_map/ppermute | solution.py:308
  0.5 1.5 %collective-permute-start.2 = (s32[1,2,3]{2,1,0:T(2,128)}, s32[1,2,3]{2,1,0:T(2,128)S(1)}, u32[]{:S(2)}, u32[]{:S(2)}) collective-permute-start(s32[1,2,3]{2,1,0:T(2,128)} %param.11), channel_id=1, source_target_pairs={{0,1},{1,0},{2,3},{3,2},{4,5},{5,4},{6,7},{7,6},{8,9},{9,8},{10,11... | collective-permute-start | bytes 80 | tf_op jit(solution)/shard_map/ppermute | solution.py:308
  0.5 1.5 %collective-permute-start.1 = (f32[1,8,16]{2,1,0:T(8,128)}, f32[1,8,16]{2,1,0:T(8,128)S(1)}, u32[]{:S(2)}, u32[]{:S(2)}) collective-permute-start(f32[1,8,16]{2,1,0:T(8,128)} %param.10), channel_id=1, source_target_pairs={{0,1},{1,0},{2,3},{3,2},{4,5},{5,4},{6,7},{7,6},{8,9},{9,8},{10,11... | collective-permute-start | bytes 1544 | tf_op jit(solution)/shard_map/ppermute | solution.py:308
  1.0 1.4 %collective-permute-start.3 = (bf16[16,384]{1,0:T(8,128)(2,1)}, bf16[16,384]{1,0:T(8,128)(2,1)S(1)}, u32[]{:S(2)}, u32[]{:S(2)}) collective-permute-start(bf16[16,384]{1,0:T(8,128)(2,1)} %own.1), channel_id=1, source_target_pairs={{0,1},{1,0},{2,3},{3,2},{4,5},{5,4},{6,7},{7,6},{8,9},{9,8},{10,11... | collective-permute-start | bytes 36872 | tf_op jit(solution)/shard_map/ppermute | solution.py:308
  1.0 0.7 %copy-start.3 = (f32[1,8,16]{2,1,0:T(8,128)S(1)}, f32[1,8,16]{2,1,0:T(8,128)}, u32[]{:S(2)}) copy-start(f32[1,8,16]{2,1,0:T(8,128)} %param.10) | copy-start | bytes 1540
  1.0 0.7 %copy-start.4 = (s32[1,2,3]{2,1,0:T(2,128)S(1)}, s32[1,2,3]{2,1,0:T(2,128)}, u32[]{:S(2)}) copy-start(s32[1,2,3]{2,1,0:T(2,128)} %param.11) | copy-start | bytes 76
  2.4 12.6 %copy-start.5 = (bf16[16,21,21]{2,0,1:T(8,128)(2,1)S(1)}, bf16[16,21,21]{2,0,1:T(8,128)(2,1)}, u32[]{:S(2)}) copy-start(bf16[16,21,21]{2,0,1:T(8,128)(2,1)} %param.9) | copy-start | bytes 42340
  2.6 12.4 %copy-start.6 = (bf16[16,384]{1,0:T(8,128)(2,1)S(1)}, bf16[16,384]{1,0:T(8,128)(2,1)}, u32[]{:S(2)}) copy-start(bf16[16,384]{1,0:T(8,128)(2,1)} %own.1) | copy-start | bytes 36868
  2.6 10.7 %collective-permute-start.4 = (bf16[152,128]{1,0:T(8,128)(2,1)S(1)}, bf16[152,128]{1,0:T(8,128)(2,1)S(1)}, u32[]{:S(2)}, u32[]{:S(2)}) collective-permute-start(bf16[152,128]{1,0:T(8,128)(2,1)S(1)} %get-tuple-element.18), channel_id=1, source_target_pairs={{0,14},{1,15},{2,12},{3,13},{4,10},{5,11},{6,8},{7,9},{8,6},{9,7},... | collective-permute-start | bytes 116744 | tf_op jit(solution)/shard_map/ppermute | solution.py:308
  8.4 5.2 %collective-permute-start.5 = (bf16[152,128]{1,0:T(8,128)(2,1)S(1)}, bf16[152,128]{1,0:T(8,128)(2,1)S(1)}, u32[]{:S(2)}, u32[]{:S(2)}) collective-permute-start(bf16[152,128]{1,0:T(8,128)(2,1)S(1)} %get-tuple-element.19), channel_id=1, source_target_pairs={{0,6},{1,7},{2,4},{3,5},{4,2},{5,3},{6,0},{7,1},{8,14},{9,15},{10,... | collective-permute-start | bytes 116744 | tf_op jit(solution)/shard_map/ppermute | solution.py:308
  8.4 6.6 %collective-permute-start.6 = (bf16[152,128]{1,0:T(8,128)(2,1)S(1)}, bf16[152,128]{1,0:T(8,128)(2,1)S(1)}, u32[]{:S(2)}, u32[]{:S(2)}) collective-permute-start(bf16[152,128]{1,0:T(8,128)(2,1)S(1)} %get-tuple-element.20), channel_id=1, source_target_pairs={{0,2},{1,3},{2,0},{3,1},{4,6},{5,7},{6,4},{7,5},{8,10},{9,11},{10,... | collective-permute-start | bytes 116744 | tf_op jit(solution)/shard_map/ppermute | solution.py:308
  9.4 6.5 %collective-permute-start.7 = (bf16[104,128]{1,0:T(8,128)(2,1)S(1)}, bf16[104,128]{1,0:T(8,128)(2,1)S(1)}, u32[]{:S(2)}, u32[]{:S(2)}) collective-permute-start(bf16[104,128]{1,0:T(8,128)(2,1)S(1)} %get-tuple-element.21), channel_id=1, source_target_pairs={{0,12},{1,13},{2,14},{3,15},{4,8},{5,9},{6,10},{7,11},{8,4},{9,5},... | collective-permute-start | bytes 79880 | tf_op jit(solution)/shard_map/ppermute | solution.py:308
  10.7 5.7 %collective-permute-start.8 = (bf16[104,128]{1,0:T(8,128)(2,1)S(1)}, bf16[104,128]{1,0:T(8,128)(2,1)S(1)}, u32[]{:S(2)}, u32[]{:S(2)}) collective-permute-start(bf16[104,128]{1,0:T(8,128)(2,1)S(1)} %get-tuple-element.22), channel_id=1, source_target_pairs={{0,10},{1,11},{2,8},{3,9},{4,14},{5,15},{6,12},{7,13},{8,2},{9,3},... | collective-permute-start | bytes 79880 | tf_op jit(solution)/shard_map/ppermute | solution.py:308
  13.3 4.7 %collective-permute-start.9 = (bf16[104,128]{1,0:T(8,128)(2,1)S(1)}, bf16[104,128]{1,0:T(8,128)(2,1)S(1)}, u32[]{:S(2)}, u32[]{:S(2)}) collective-permute-start(bf16[104,128]{1,0:T(8,128)(2,1)S(1)} %get-tuple-element.23), channel_id=1, source_target_pairs={{0,8},{1,9},{2,10},{3,11},{4,12},{5,13},{6,14},{7,15},{8,0},{9,1},... | collective-permute-start | bytes 79880 | tf_op jit(solution)/shard_map/ppermute | solution.py:308
  13.6 4.4 %collective-permute-start.10 = (bf16[104,128]{1,0:T(8,128)(2,1)S(1)}, bf16[104,128]{1,0:T(8,128)(2,1)S(1)}, u32[]{:S(2)}, u32[]{:S(2)}) collective-permute-start(bf16[104,128]{1,0:T(8,128)(2,1)S(1)} %get-tuple-element.24), channel_id=1, source_target_pairs={{0,4},{1,5},{2,6},{3,7},{4,0},{5,1},{6,2},{7,3},{8,12},{9,13},{10,... | collective-permute-start | bytes 79880 | tf_op jit(solution)/shard_map/ppermute | solution.py:308
  14.9 3.1 %copy-start = (s32[16,16,384]{2,1,0:T(8,128)S(1)}, s32[16,16,384]{2,1,0:T(8,128)}, u32[]{:S(2)}) copy-start(s32[16,16,384]{2,1,0:T(8,128)} %refs_9_.1) | copy-start | bytes 1179652
  15.0 3.1 %copy-start.1 = (bf16[16,16,384]{2,1,0:T(8,128)(2,1)S(1)}, bf16[16,16,384]{2,1,0:T(8,128)(2,1)}, u32[]{:S(2)}) copy-start(bf16[16,16,384]{2,1,0:T(8,128)(2,1)} %refs_10_.1) | copy-start | bytes 589828

commit v5 on v4

--- a/solution.py
+++ b/solution.py
@@ -13,7 +13,6 @@
 SUB = 8
 TILE = 16
 VMEM_LIMIT = 16 * 1024 * 1024
-ORDER = [7, 3, 1, 6, 5, 4, 2]
 
 
 def up(value, unit):
@@ -53,10 +52,21 @@
     return k & (k + 1) == 0 and k > 0
 
 
-def stage_kernel(science, coef, grid_index, first, out, table):
-    core = lax.rem(lax.axis_index("epoch"), 2)
-    for chip in range(science.shape[0]):
-        out[chip] = science[chip, core]
+def handled(step, core):
+    return step if isinstance(step, int) else jnp.where(core == 0, step[0], step[1])
+
+
+def block_rows(step, rows, columns):
+    cores = 1 if isinstance(step, int) else 2
+    first = cores * 2 * columns * rows
+    size = up(2 * columns, SUB)
+    tail = first + (columns * rows if with_template(step if cores == 1 else step[0]) else 0)
+    return first, tail, tail + size
+
+
+def stage_kernel(science, template, coef, grid_index, first, out, edge, table):
+    out[...] = science[...]
+    edge[...] = template[...]
     table[...] = cell_rows(coef, grid_index)
 
 
@@ -73,22 +83,25 @@
     )()
 
 
-def stage(science, coef, grid_index, first):
+def stage(science, template, coef, grid_index, first):
     chips, _, rows, width = science.shape
     return pl.pallas_call(
         stage_kernel,
         out_shape=[
-            jax.ShapeDtypeStruct((chips, rows, width), jnp.bfloat16),
+            jax.ShapeDtypeStruct(science.shape, jnp.bfloat16),
+            jax.ShapeDtypeStruct(template.shape, jnp.bfloat16),
             jax.ShapeDtypeStruct((grid_index.shape[0] * grid_index.shape[1], LANES), jnp.float32),
         ],
         compiler_params=pltpu.CompilerParams(vmem_limit_bytes=VMEM_LIMIT),
         cost_estimate=pl.CostEstimate(flops=0, bytes_accessed=1_000_000, transcendentals=0),
-    )(science, coef, grid_index, first)
-
-
-def pack_kernel(steps, own, pair, own_table, pair_coef, pair_index, template, *refs):
+    )(science, template, coef, grid_index, first)
+
+
+def pack_kernel(
+    steps, own, pair, own_table, pair_coef, pair_index, own_template, pair_template, *refs
+):
     blocks, tables = refs[:-1], refs[-1]
-    rows, width = template.shape
+    rows, width = own_template.shape
     columns = width // CELL
     me = lax.axis_index("epoch")
     core, here = lax.rem(me, 2), lax.div(me, 2)
@@ -96,43 +109,80 @@
     cells = own_table.shape[0]
     tables[:cells] = own_table[...]
     tables[half : half + cells] = cell_rows(pair_coef, pair_index)
-    for k, block in zip(steps, blocks):
-        to = here ^ k
-        for c in range(columns):
-            at = slice(c * CELL, (c + 1) * CELL)
-            block[c * rows : (c + 1) * rows] = own[to, :, at]
-            block[(columns + c) * rows : (columns + c + 1) * rows] = pair[to, core, :, at]
-            if with_template(k):
-                block[(2 * columns + c) * rows : (2 * columns + c + 1) * rows] = template[:, at]
-        cell_row = lax.div((to * 2 + core) * rows, CELL)
-        tail = [
+    for step, block in zip(steps, blocks):
+        to = here ^ handled(step, core)
+        edge, tail, _ = block_rows(step, rows, columns)
+        first = 0
+        for target in [core] if isinstance(step, int) else range(2):
+            for source in (own, pair):
+                for c in range(columns):
+                    block[first : first + rows] = source[
+                        to, target, :, c * CELL : (c + 1) * CELL
+                    ]
+                    first += rows
+        if edge < tail:
+            mine, other = own_template[...], pair_template[...]
+            near = other.astype(jnp.float32)
+            if not isinstance(step, int):
+                near = jnp.where(here < to, near, mine.astype(jnp.float32))
+            for c in range(columns):
+                at = slice(c * CELL, (c + 1) * CELL)
+                block[edge + c * rows : edge + (c + 1) * rows] = near[:, at].astype(jnp.bfloat16)
+        cell_row = lax.div(to * 2 * rows, CELL)
+        picked = [
             tables[pl.ds(q * half + cell_row * columns + c, 1), :]
             for q in range(2)
             for c in range(columns)
         ]
-        tail.append(jnp.zeros((up(2 * columns, SUB) - 2 * columns, LANES), jnp.float32))
-        block[block.shape[0] - up(2 * columns, SUB) :] = jnp.concatenate(
-            [rows_ for rows_ in tail if rows_.shape[0]], axis=0
-        ).astype(jnp.bfloat16)
-
-
-def pack(own, pair, own_table, pair_coef, pair_index, template, steps):
-    rows, width = template.shape
+        spare = up(2 * columns, SUB) - 2 * columns
+        if spare:
+            picked.append(jnp.zeros((spare, LANES), jnp.float32))
+        block[tail:] = jnp.concatenate(picked, axis=0).astype(jnp.bfloat16)
+
+
+def pack(steps, own, pair, own_table, pair_coef, pair_index, own_template, pair_template):
+    rows, width = own_template.shape
     columns = width // CELL
-    tail = up(2 * columns, SUB)
+    assert CELL % (2 * rows) == 0
     half = up(own_table.shape[0], SUB)
     return pl.pallas_call(
         functools.partial(pack_kernel, steps),
         out_shape=[
-            jax.ShapeDtypeStruct(
-                ((3 if with_template(k) else 2) * columns * rows + tail, LANES), jnp.bfloat16
-            )
-            for k in steps
+            jax.ShapeDtypeStruct((block_rows(step, rows, columns)[2], LANES), jnp.bfloat16)
+            for step in steps
         ],
         scratch_shapes=[pltpu.VMEM((2 * half, LANES), jnp.float32)],
         compiler_params=pltpu.CompilerParams(vmem_limit_bytes=VMEM_LIMIT),
         cost_estimate=pl.CostEstimate(flops=0, bytes_accessed=500_000, transcendentals=0),
-    )(own, pair, own_table, pair_coef, pair_index, template)
+    )(own, pair, own_table, pair_coef, pair_index, own_template, pair_template)
+
+
+def edge_kernel(first, block, out):
+    rows, width = out.shape
+    for c in range(width // CELL):
+        out[:, c * CELL : (c + 1) * CELL] = block[first + c * rows : first + (c + 1) * rows]
+
+
+def edge_rows(block, first, rows, width):
+    return pl.pallas_call(
+        functools.partial(edge_kernel, first),
+        out_shape=jax.ShapeDtypeStruct((rows, width), jnp.bfloat16),
+        compiler_params=pltpu.CompilerParams(vmem_limit_bytes=VMEM_LIMIT),
+        cost_estimate=pl.CostEstimate(flops=1000000000, bytes_accessed=60_000, transcendentals=0),
+    )(block)
+
+
+def pass_kernel(block, after, out):
+    out[...] = block[...]
+
+
+def pass_on(block, after):
+    return pl.pallas_call(
+        pass_kernel,
+        out_shape=jax.ShapeDtypeStruct(block.shape, block.dtype),
+        compiler_params=pltpu.CompilerParams(vmem_limit_bytes=VMEM_LIMIT),
+        cost_estimate=pl.CostEstimate(flops=0, bytes_accessed=100_000, transcendentals=0),
+    )(block, after)
 
 
 def basis_kernel(slot, steps, kernels, own, pair, *refs):
@@ -148,12 +198,20 @@
     image[...] = jnp.zeros(image.shape, jnp.float32)
     near = pair[...].astype(jnp.float32)
     far = jnp.zeros(own.shape, jnp.float32)
-    for k, block in zip(steps, held):
-        at = 2 * columns * rows
-        lines = [
-            block[at + c * rows : at + (c + 1) * rows].astype(jnp.float32) for c in range(columns)
-        ]
-        far = jnp.where(here ^ k == want, jnp.concatenate(lines, axis=1), far)
+    held = list(held)
+    for step in steps:
+        at = block_rows(step, rows, columns)[0]
+        found = []
+        for _ in range(1 if isinstance(step, int) else 2):
+            block = held.pop(0)
+            if isinstance(step, int):
+                found.append(block[...].astype(jnp.float32))
+                continue
+            lines = [block[at + c * rows : at + (c + 1) * rows] for c in range(columns)]
+            found.append(jnp.concatenate([line.astype(jnp.float32) for line in lines], axis=1))
+        line = found[0] if len(found) == 1 else jnp.where(odd, found[1], found[0])
+        k = step if isinstance(step, int) else step[0]
+        far = jnp.where(here ^ k == want, line, far)
     low = jnp.where(odd, near, far)
     high = jnp.where(odd, far, near)
     image[:half, :width] = low[rows - half :, :]
@@ -211,69 +269,85 @@
     )(kernels.transpose(1, 0, 2), own, pair, *held)
 
 
-def stack_kernel(count, steps, *refs):
-    blocks = refs[:-5]
-    basis, clip_mask, inv_var, out, model = refs[-5:]
-    units = 2
-    epochs, rows, width = clip_mask.shape
-    columns = width // CELL
+def unit_terms(count, steps, blocks, rows, columns):
+    me = lax.axis_index("epoch")
+    core, here = lax.rem(me, 2), lax.div(me, 2)
+    size = up(2 * columns, SUB)
+    tails = jnp.concatenate([block[block.shape[0] - size :] for block in blocks], axis=0)
+    shape = (LANES, 3 * LANES)
+    target = lax.broadcasted_iota(jnp.int32, shape, 1)
+    target = lax.div(target, LANES) * count + lax.rem(target, count)
+    spread = lax.broadcasted_iota(jnp.int32, shape, 0) == target
+    tiled = jnp.dot(
+        tails,
+        spread.astype(jnp.float32).astype(jnp.bfloat16),
+        preferred_element_type=jnp.float32,
+    )
+    found = []
+    for step in steps:
+        for carrier in [core] if isinstance(step, int) else [core, 1 - core]:
+            i = len(found) // 2
+            chip = here ^ handled(step, carrier)
+            base = 0 if isinstance(step, int) else core * (2 * columns * rows)
+            for j in range(2):
+                first = i * size + j * columns
+                terms = [
+                    tiled[first : first + columns, term * LANES : (term + 1) * LANES]
+                    for term in range(3)
+                ]
+                start = base + j * columns * rows
+                found.append((blocks[i], start, chip * 2 + (carrier ^ j), terms))
+    return found
+
+
+def cell_differences(count, units, basis, rows, columns, c):
+    at = slice(c * CELL, (c + 1) * CELL)
     parts = rows // SUB
     depth = SUB * count
     lane = lax.broadcasted_iota(jnp.int32, (SUB, LANES), 1)
     line = lax.broadcasted_iota(jnp.int32, (SUB, LANES), 0)
     diagonal = (lane >= line * count) & (lane < (line + 1) * count)
-    me = lax.axis_index("epoch")
-    order, spread = [], []
-    for k, chip in enumerate(steps):
-        size = up(units * columns, SUB)
-        tail = blocks[k][blocks[k].shape[0] - size :].astype(jnp.float32)
-        own_lane = lax.broadcasted_iota(jnp.int32, tail.shape, 1) < count
-        terms = []
-        for term in range(3):
-            value = tail if term == 0 else pltpu.roll(tail, LANES - term * count, 1)
-            value = jnp.where(own_lane, value, 0.0)
-            step = count
-            while step < LANES:
-                value = value + pltpu.roll(value, step, 1)
-                step *= 2
-            terms.append(value)
-        for j in range(units):
-            order.append((k, j, me ^ (chip * units + j)))
-            spread.append([value[j * columns : (j + 1) * columns] for value in terms])
+    weights = [
+        jnp.concatenate(
+            [
+                jnp.where(diagonal, jnp.broadcast_to(unit[3][term][c : c + 1], (SUB, LANES)), 0.0)
+                for unit in units
+            ],
+            axis=0,
+        ).astype(jnp.bfloat16)
+        for term in range(3)
+    ]
+    planes = jnp.concatenate([basis[p * depth : (p + 1) * depth, at] for p in range(parts)], axis=1)
+    model = jnp.dot(
+        jnp.concatenate(weights, axis=1),
+        jnp.concatenate([planes] * 3, axis=0),
+        preferred_element_type=jnp.float32,
+    )
+    values = []
+    for e, (block, start, _, _) in enumerate(units):
+        first = start + c * rows
+        first = first if isinstance(first, int) else pl.multiple_of(first, rows)
+        science = block[pl.ds(first, rows), :].astype(jnp.float32)
+        planes = [model[e * SUB : (e + 1) * SUB, p * CELL : (p + 1) * CELL] for p in range(parts)]
+        values.append((science - jnp.concatenate(planes, axis=0)).astype(jnp.bfloat16))
+    return values
+
+
+def stack_kernel(count, steps, *refs):
+    blocks = refs[:-4]
+    basis, clip_mask, inv_var, out = refs[-4:]
+    epochs, rows, width = clip_mask.shape
+    columns = width // CELL
+    units = unit_terms(count, steps, blocks, rows, columns)
+    late = [cell_differences(count, units, basis, rows, columns, c) for c in range(columns)]
     for c in range(columns):
         at = slice(c * CELL, (c + 1) * CELL)
-        weights = jnp.concatenate(
-            [
-                jnp.concatenate(
-                    [
-                        jnp.where(
-                            diagonal,
-                            jnp.broadcast_to(spread[e][term][c : c + 1], (SUB, LANES)),
-                            0.0,
-                        )
-                        for e in range(epochs)
-                    ],
-                    axis=0,
-                ).astype(jnp.bfloat16)
-                for term in range(3)
-            ],
-            axis=1,
-        )
-        planes = jnp.concatenate(
-            [basis[p * depth : (p + 1) * depth, at] for p in range(parts)], axis=1
-        )
-        model[...] = jnp.dot(
-            weights, jnp.concatenate([planes] * 3, axis=0), preferred_element_type=jnp.float32
-        )
-        for p in range(parts):
+        for p in range(rows // SUB):
             top = slice(p * SUB, (p + 1) * SUB)
             values, weight_iv, base = [], [], []
-            for e in range(epochs):
-                k, j, epoch = order[e]
-                first = (j * columns + c) * rows
-                science = blocks[k][first : first + rows].astype(jnp.float32)[top]
-                difference = science - model[e * SUB : (e + 1) * SUB, p * CELL : (p + 1) * CELL]
-                values.append(difference.astype(jnp.bfloat16).astype(jnp.float32))
+            for e, (_, _, epoch, _) in enumerate(units):
+                value = late[c][e]
+                values.append(value.astype(jnp.float32)[top])
                 iv = inv_var[epoch, :, at].astype(jnp.float32)[top]
                 weight_iv.append(iv)
                 base.append(clip_mask[epoch, top, at].astype(jnp.float32) * iv)
@@ -296,7 +370,6 @@
     return pl.pallas_call(
         functools.partial(stack_kernel, count, steps),
         out_shape=jax.ShapeDtypeStruct((rows, width), jnp.float32),
-        scratch_shapes=[pltpu.VMEM((epochs * SUB, rows // SUB * CELL), jnp.float32)],
         compiler_params=pltpu.CompilerParams(vmem_limit_bytes=VMEM_LIMIT),
         cost_estimate=pl.CostEstimate(
             flops=100 * epochs * rows * width, bytes_accessed=10**6, transcendentals=0
@@ -305,25 +378,47 @@
 
 
 def exchange(block, step):
-    return lax.ppermute(block, "epoch", [(i, i ^ step) for i in range(lax.axis_size("epoch"))])
+    count = lax.axis_size("epoch")
+    apart = (step, step) if isinstance(step, int) else step
+    return lax.ppermute(block, "epoch", [(i, i ^ (2 * apart[i % 2])) for i in range(count)])
+
+
+def swap_cores(block):
+    return lax.ppermute(block, "epoch", [(i, i ^ 1) for i in range(lax.axis_size("epoch"))])
 
 
 def local(science, template, kernels, coef, grid_index, clip_mask, inv_var):
     rows, width = template.shape
     chips = lax.axis_size("epoch") // 2
     view = (chips, 2, rows, width)
-    steps = [0] + ORDER + [k for k in range(1, chips) if k not in ORDER]
-    pair_science = exchange(science, 1).reshape(view)
-    pair_coef = exchange(coef, 1)[0]
-    pair_index = exchange(grid_index, 1)[0]
-    pair = exchange(template, 1)
-    own, table = stage(science.reshape(view), coef[0], grid_index[0], nothing())
-    sent = pack(own, pair_science, table, pair_coef, pair_index, pair, steps)
-    blocks = [sent[0]] + [exchange(block, 2 * k) for block, k in zip(sent[1:], steps[1:])]
-    near = [i for i, k in enumerate(steps) if with_template(k)]
-    basis = basis_rows(
-        kernels, template, pair, [blocks[i] for i in near], [steps[i] for i in near]
-    )
+    pairs = [(k, k - 1) for k in range(chips - 1, 1, -2)]
+    pairs.sort(key=lambda step: not with_template(step[0]))
+    steps = [0] + pairs + [1]
+    pair_science = swap_cores(science).reshape(view)
+    pair_coef = swap_cores(coef)[0]
+    pair_index = swap_cores(grid_index)[0]
+    pair = swap_cores(template)
+    own, edge, table = stage(science.reshape(view), template, coef[0], grid_index[0], nothing())
+    sent = pack(steps, own, pair_science, table, pair_coef, pair_index, edge, pair)
+    arrived = [exchange(block, step) for step, block in zip(steps[1:], sent[1:])]
+    near, near_steps, swapped = [], [], {}
+    for step, block in zip(steps[1:], arrived):
+        if isinstance(step, int):
+            first = block_rows(step, rows, width // CELL)[0]
+            near.append(edge_rows(block, first, rows, width))
+            near_steps.append(step)
+        elif with_template(step[0]):
+            swapped[step] = swap_cores(block)
+            near += [block, swapped[step]]
+            near_steps.append(step)
+    basis = basis_rows(kernels, template, pair, near, near_steps)
+    blocks = [sent[0]]
+    for step, block in zip(steps[1:], arrived):
+        blocks.append(block)
+        if not isinstance(step, int):
+            if step not in swapped:
+                swapped[step] = swap_cores(pass_on(block, basis))
+            blocks.append(swapped[step])
     return stack(kernels.shape[0], steps, blocks, basis, clip_mask, inv_var)
 
 

time: 19.7 us -> 18.6 us (0.944)
  starting transfers between devices: 13.4 us -> 9.14 us
  waiting for transfers between devices: 2.56 us -> 5.76 us
    ppermute x11, starting transfers between devices: 13.4 us -> 9.14 us  [the longest x4 7.89 us: exchange(): lax.ppermute(block, 'epoch', [(i, i ^ 2 * apart[i % 2]) for i in range(co...]
    ppermute x11, waiting for transfers between devices: 2.56 us -> 5.76 us  [the longest x4 3.04 us: exchange(): lax.ppermute(block, 'epoch', [(i, i ^ 2 * apart[i % 2]) for i in range(co...]
  transfers between devices with their start and end apart: 11 -> 11, of which waited for: 4 -> 6; matrix products, arithmetic and copies ran while one was open for 0% -> 0% of each run, Pallas kernels for 6% -> 6%
where the time goes in v5:
time: 18.6 us; the launch traced here: 18.4 us
  starting transfers between devices  9.14 us (49%)
  waiting for transfers between devices  5.76 us (31%)
  Pallas kernels  2.74 us (15%)
  local copies, waits for them, and re-layouts  0.71 us (4%)
    ppermute x4, starting transfers between devices, exchange(): lax.ppermute(block, 'epoch', [(i, i ^ 2 * apart[i % 2]) for i in range(co...  7.89 us
    ppermute x4, waiting for transfers between devices, exchange(): lax.ppermute(block, 'epoch', [(i, i ^ 2 * apart[i % 2]) for i in range(co...  3.04 us
    ppermute x7, waiting for transfers between devices, swap_cores(): lax.ppermute(block, 'epoch', [(i, i ^ 1) for i in range(lax.axis_size('ep...  2.73 us
    pallas_call x1, Pallas kernels, stack(): pl.pallas_call(functools.partial(stack_kernel, count, steps), out_shape=j...  1.4 us
    ppermute x7, starting transfers between devices, swap_cores(): lax.ppermute(block, 'epoch', [(i, i ^ 1) for i in range(lax.axis_size('ep...  1.25 us
    pallas_call x1, Pallas kernels, basis_rows(): pl.pallas_call(functools.partial(basis_kernel, slot, steps), out_shape=ja...  0.93 us
    unnamed x14, local copies, waits for them, and re-layouts  0.71 us
  transfers between devices with their start and end apart: 11, of which 6 were waited for; matrix products, arithmetic and copies ran while one was open for 0% of the time, Pallas kernels for 6%

profile of v5, /device:TPU:0, one launch (start us, length us, event | category | flops | bytes accessed | tf_op | source)
XLA Modules:
  0.0 18.4 jit_solution(4215635155468250162)
XLA Ops:
  0.0 0.0 copy-start.2
  0.0 0.5 %collective-permute-start = (bf16[1,256,384]{2,1,0:T(8,128)(2,1)}, bf16[1,256,384]{2,1,0:T(8,128)(2,1)S(1)}, u32[]{:S(2)}, u32[]{:S(2)}) collective-permute-start(bf16[1,256,384]{2,1,0:T(8,128)(2,1)} %param.7), channel_id=1, source_target_pairs={{0,1},{1,0},{2,3},{3,2},{4,5},{5,4},{6,7},{7,6},{8,9},{9,8},{10,11... | collective-permute-start | bytes 589832 | tf_op jit(solution)/shard_map/ppermute | solution.py:387
  0.5 0.1 collective-permute-start.2
  0.5 0.4 %collective-permute-start.1 = (f32[1,8,16]{2,1,0:T(8,128)}, f32[1,8,16]{2,1,0:T(8,128)S(1)}, u32[]{:S(2)}, u32[]{:S(2)}) collective-permute-start(f32[1,8,16]{2,1,0:T(8,128)} %param.10), channel_id=1, source_target_pairs={{0,1},{1,0},{2,3},{3,2},{4,5},{5,4},{6,7},{7,6},{8,9},{9,8},{10,11... | collective-permute-start | bytes 1544 | tf_op jit(solution)/shard_map/ppermute | solution.py:387
  1.0 0.1 collective-permute-start.3
  1.0 0.0 copy-start.3
  1.0 0.0 copy-start.4
  1.0 0.0 copy-start.5
  1.0 0.0 copy-done.2
  1.1 0.7 %copy-done.3 = bf16[16,384]{1,0:T(8,128)(2,1)S(1)} copy-done((bf16[16,384]{1,0:T(8,128)(2,1)S(1)}, bf16[16,384]{1,0:T(8,128)(2,1)}, u32[]{:S(2)}) %copy-start.3) | copy-done | bytes 12312
  1.7 0.0 copy-done.4
  1.7 0.0 copy-done.5
  1.7 0.2 %shard_map.74 = (bf16[8,2,16,384]{3,2,1,0:T(8,128)(2,1)S(1)}, bf16[16,384]{1,0:T(8,128)(2,1)S(1)}, f32[6,128]{1,0:T(8,128)S(1)}) custom-call(bf16[8,2,16,384]{3,2,1,0:T(8,128)(2,1)S(1)} %bitcast.7, bf16[16,384]{1,0:T(8,128)(2,1)S(1)} %copy-done.3, f32[8,16]{1,0:T(8,128)S(1)} %bitcast.9, s32[2,3]{1,0:T(2,128)S(1)} %bitcast.11, f32[8,128]{1,0:T(8,128)S(1)} %shard_map.73.first), custom_call_target="tpu_custom_call" | custom-call | bytes 1000000 | tf_op jit(solution)/shard_map/pallas_call | solution.py:88
  1.9 0.0 collective-permute-done.2
  1.9 0.1 collective-permute-done.1
  2.0 0.4 %collective-permute-done.3.pair_template.pair = bf16[16,384]{1,0:T(8,128)(2,1)S(1)} collective-permute-done((bf16[16,384]{1,0:T(8,128)(2,1)}, bf16[16,384]{1,0:T(8,128)(2,1)S(1)}, u32[]{:S(2)}, u32[]{:S(2)}) %collective-permute-start.3) | collective-permute-done | bytes 12320 | tf_op jit(solution)/shard_map/ppermute | solution.py:387
  2.4 0.0 collective-permute-done
  2.4 0.2 %shard_map.75 = (bf16[104,128]{1,0:T(8,128)(2,1)S(1)}, bf16[248,128]{1,0:T(8,128)(2,1)S(1)}, bf16[248,128]{1,0:T(8,128)(2,1)S(1)}, bf16[200,128]{1,0:T(8,128)(2,1)S(1)}, bf16[152,128]{1,0:T(8,128)(2,1)S(1)}) custom-call(bf16[8,2,16,384]{3,2,1,0:T(8,128)(2,1)S(1)} %get-tuple-element.13.own, bf16[8,2,16,384]{3,2,1,0:T(8,128)(2,1)S(1)} %bitcast.8, ...), custom_call_target="tpu_custom_call" | custom-call | bytes 500000 | tf_op jit(solution)/shard_map/pallas_call | solution.py:148
  2.6 5.8 %collective-permute-start.4 = (bf16[248,128]{1,0:T(8,128)(2,1)S(1)}, bf16[248,128]{1,0:T(8,128)(2,1)S(1)}, u32[]{:S(2)}, u32[]{:S(2)}) collective-permute-start(bf16[248,128]{1,0:T(8,128)(2,1)S(1)} %get-tuple-element.17), channel_id=1, source_target_pairs={{0,14},{1,13},{2,12},{3,15},{4,10},{5,9},{6,8},{7,11},{8,6},{9,5},... | collective-permute-start | bytes 190472 | tf_op jit(solution)/shard_map/ppermute | solution.py:383
  8.4 0.0 collective-permute-start.6
  8.4 1.0 %collective-permute-start.9 = (bf16[152,128]{1,0:T(8,128)(2,1)S(1)}, bf16[152,128]{1,0:T(8,128)(2,1)S(1)}, u32[]{:S(2)}, u32[]{:S(2)}) collective-permute-start(bf16[152,128]{1,0:T(8,128)(2,1)S(1)} %get-tuple-element.20), channel_id=1, source_target_pairs={{0,2},{1,3},{2,0},{3,1},{4,6},{5,7},{6,4},{7,5},{8,10},{9,11},{10,... | collective-permute-start | bytes 116744 | tf_op jit(solution)/shard_map/ppermute | solution.py:383
  9.4 0.0 copy-start.6
  9.4 1.1 %collective-permute-start.8 = (bf16[200,128]{1,0:T(8,128)(2,1)S(1)}, bf16[200,128]{1,0:T(8,128)(2,1)S(1)}, u32[]{:S(2)}, u32[]{:S(2)}) collective-permute-start(bf16[200,128]{1,0:T(8,128)(2,1)S(1)} %get-tuple-element.19), channel_id=1, source_target_pairs={{0,10},{1,9},{2,8},{3,11},{4,14},{5,13},{6,12},{7,15},{8,2},{9,1},... | collective-permute-start | bytes 153608 | tf_op jit(solution)/shard_map/ppermute | solution.py:383
  10.5 0.8 %collective-permute-done.4.refs_0_.refs_1_ = bf16[248,128]{1,0:T(8,128)(2,1)S(1)} collective-permute-done((bf16[248,128]{1,0:T(8,128)(2,1)S(1)}, bf16[248,128]{1,0:T(8,128)(2,1)S(1)}, u32[]{:S(2)}, u32[]{:S(2)}) %collective-permute-start.4) | collective-permute-done | bytes 63520 | tf_op jit(solution)/shard_map/ppermute | solution.py:383
  11.3 0.0 collective-permute-start.5
  11.3 2.2 %collective-permute-done.6.refs_2_.refs_3_ = bf16[248,128]{1,0:T(8,128)(2,1)S(1)} collective-permute-done((bf16[248,128]{1,0:T(8,128)(2,1)S(1)}, bf16[248,128]{1,0:T(8,128)(2,1)S(1)}, u32[]{:S(2)}, u32[]{:S(2)}) %collective-permute-start.6) | collective-permute-done | bytes 63520 | tf_op jit(solution)/shard_map/ppermute | solution.py:383
  13.5 0.0 collective-permute-start.7
  13.5 0.0 collective-permute-done.9.block.refs_7_
  13.5 0.0 collective-permute-done.5.refs_1_.refs_2_
  13.5 1.2 %collective-permute-done.7.refs_3_.refs_4_ = bf16[248,128]{1,0:T(8,128)(2,1)S(1)} collective-permute-done((bf16[248,128]{1,0:T(8,128)(2,1)S(1)}, bf16[248,128]{1,0:T(8,128)(2,1)S(1)}, u32[]{:S(2)}, u32[]{:S(2)}) %collective-permute-start.7) | collective-permute-done | bytes 63520 | tf_op jit(solution)/shard_map/ppermute | solution.py:387
  14.8 0.0 copy-done.6
  14.8 0.0 copy-start
  14.8 0.9 %shard_map.77.after.refs_8_ = bf16[256,384]{1,0:T(8,128)(2,1)S(1)} custom-call(bf16[21,16,21]{2,1,0:T(8,128)(2,1)S(1)} %bitcast.13, bf16[16,384]{1,0:T(8,128)(2,1)S(1)} %copy-done.3, bf16[16,384]{1,0:T(8,128)(2,1)S(1)} %collective-permute-done.3.pair_template.pair, bf16[248,128]{1,0:T(8,128)(2,1)S(1)} %collective-permute-done.4.refs_0_.refs_1_, ...), custom_call_target="tpu_custom_call" | custom-call | flops 226492416 | bytes 600000 | tf_op jit(solution)/shard_map/pallas_call | solution.py:257
  15.7 0.0 copy-start.1
  15.7 0.0 collective-permute-done.8.block.refs_5_
  15.7 0.2 %collective-permute-start.10 = (bf16[200,128]{1,0:T(8,128)(2,1)S(1)}, bf16[200,128]{1,0:T(8,128)(2,1)S(1)}, u32[]{:S(2)}, u32[]{:S(2)}) collective-permute-start(bf16[200,128]{1,0:T(8,128)(2,1)S(1)} %shard_map.78), channel_id=1, source_target_pairs={{0,1},{1,0},{2,3},{3,2},{4,5},{5,4},{6,7},{7,6},{8,9},{9,8},{10,11... | collective-permute-start | bytes 153608 | tf_op jit(solution)/shard_map/ppermute | solution.py:387
  16.0 1.1 %collective-permute-done.10.refs_6_ = bf16[200,128]{1,0:T(8,128)(2,1)S(1)} collective-permute-done((bf16[200,128]{1,0:T(8,128)(2,1)S(1)}, bf16[200,128]{1,0:T(8,128)(2,1)S(1)}, u32[]{:S(2)}, u32[]{:S(2)}) %collective-permute-start.10) | collective-permute-done | bytes 51232 | tf_op jit(solution)/shard_map/ppermute | solution.py:387
  17.0 0.0 copy-done
  17.0 0.0 copy-done.1
  17.0 1.4 %shard_map.79 = f32[16,384]{1,0:T(8,128)} custom-call(bf16[104,128]{1,0:T(8,128)(2,1)S(1)} %get-tuple-element.16.refs_0_, bf16[248,128]{1,0:T(8,128)(2,1)S(1)} %collective-permute-done.4.refs_0_.refs_1_, bf16[248,128]{1,0:T(8,128)(2,1)S(1)} %collective-permute-done.5.refs_1_.refs_2_, bf16[248,128]{1,0:T(8,128)(2,1)S(1)} %collective-permute-done.6.refs_2_.refs_3_, ...), custom_call_target="tpu_custom_call" | custom-call | flops 9830400 | bytes 1000000 | tf_op jit(solution)/shard_map/pallas_call | solution.py:370
  (3 shorter events, 0.0 us)
Async XLA Ops:
  0.0 1.0 %copy-start.2 = (bf16[1,256,384]{2,1,0:T(8,128)(2,1)S(1)}, bf16[1,256,384]{2,1,0:T(8,128)(2,1)}, u32[]{:S(2)}) copy-start(bf16[1,256,384]{2,1,0:T(8,128)(2,1)} %param.7) | copy-start | bytes 589828
  0.0 2.4 %collective-permute-start = (bf16[1,256,384]{2,1,0:T(8,128)(2,1)}, bf16[1,256,384]{2,1,0:T(8,128)(2,1)S(1)}, u32[]{:S(2)}, u32[]{:S(2)}) collective-permute-start(bf16[1,256,384]{2,1,0:T(8,128)(2,1)} %param.7), channel_id=1, source_target_pairs={{0,1},{1,0},{2,3},{3,2},{4,5},{5,4},{6,7},{7,6},{8,9},{9,8},{10,11... | collective-permute-start | bytes 589832 | tf_op jit(solution)/shard_map/ppermute | solution.py:387
  0.5 1.5 %collective-permute-start.2 = (s32[1,2,3]{2,1,0:T(2,128)}, s32[1,2,3]{2,1,0:T(2,128)S(1)}, u32[]{:S(2)}, u32[]{:S(2)}) collective-permute-start(s32[1,2,3]{2,1,0:T(2,128)} %param.11), channel_id=1, source_target_pairs={{0,1},{1,0},{2,3},{3,2},{4,5},{5,4},{6,7},{7,6},{8,9},{9,8},{10,11... | collective-permute-start | bytes 80 | tf_op jit(solution)/shard_map/ppermute | solution.py:387
  0.5 1.5 %collective-permute-start.1 = (f32[1,8,16]{2,1,0:T(8,128)}, f32[1,8,16]{2,1,0:T(8,128)S(1)}, u32[]{:S(2)}, u32[]{:S(2)}) collective-permute-start(f32[1,8,16]{2,1,0:T(8,128)} %param.10), channel_id=1, source_target_pairs={{0,1},{1,0},{2,3},{3,2},{4,5},{5,4},{6,7},{7,6},{8,9},{9,8},{10,11... | collective-permute-start | bytes 1544 | tf_op jit(solution)/shard_map/ppermute | solution.py:387
  1.0 1.4 %collective-permute-start.3 = (bf16[16,384]{1,0:T(8,128)(2,1)}, bf16[16,384]{1,0:T(8,128)(2,1)S(1)}, u32[]{:S(2)}, u32[]{:S(2)}) collective-permute-start(bf16[16,384]{1,0:T(8,128)(2,1)} %own.1), channel_id=1, source_target_pairs={{0,1},{1,0},{2,3},{3,2},{4,5},{5,4},{6,7},{7,6},{8,9},{9,8},{10,11... | collective-permute-start | bytes 36872 | tf_op jit(solution)/shard_map/ppermute | solution.py:387
  1.0 0.7 %copy-start.3 = (bf16[16,384]{1,0:T(8,128)(2,1)S(1)}, bf16[16,384]{1,0:T(8,128)(2,1)}, u32[]{:S(2)}) copy-start(bf16[16,384]{1,0:T(8,128)(2,1)} %own.1) | copy-start | bytes 36868
  1.0 0.7 %copy-start.4 = (f32[1,8,16]{2,1,0:T(8,128)S(1)}, f32[1,8,16]{2,1,0:T(8,128)}, u32[]{:S(2)}) copy-start(f32[1,8,16]{2,1,0:T(8,128)} %param.10) | copy-start | bytes 1540
  1.0 0.7 %copy-start.5 = (s32[1,2,3]{2,1,0:T(2,128)S(1)}, s32[1,2,3]{2,1,0:T(2,128)}, u32[]{:S(2)}) copy-start(s32[1,2,3]{2,1,0:T(2,128)} %param.11) | copy-start | bytes 76
  2.6 8.7 %collective-permute-start.4 = (bf16[248,128]{1,0:T(8,128)(2,1)S(1)}, bf16[248,128]{1,0:T(8,128)(2,1)S(1)}, u32[]{:S(2)}, u32[]{:S(2)}) collective-permute-start(bf16[248,128]{1,0:T(8,128)(2,1)S(1)} %get-tuple-element.17), channel_id=1, source_target_pairs={{0,14},{1,13},{2,12},{3,15},{4,10},{5,9},{6,8},{7,11},{8,6},{9,5},... | collective-permute-start | bytes 190472 | tf_op jit(solution)/shard_map/ppermute | solution.py:383
  8.4 5.1 %collective-permute-start.6 = (bf16[248,128]{1,0:T(8,128)(2,1)S(1)}, bf16[248,128]{1,0:T(8,128)(2,1)S(1)}, u32[]{:S(2)}, u32[]{:S(2)}) collective-permute-start(bf16[248,128]{1,0:T(8,128)(2,1)S(1)} %get-tuple-element.18), channel_id=1, source_target_pairs={{0,6},{1,5},{2,4},{3,7},{4,2},{5,1},{6,0},{7,3},{8,14},{9,13},{10,... | collective-permute-start | bytes 190472 | tf_op jit(solution)/shard_map/ppermute | solution.py:383
  8.4 5.1 %collective-permute-start.9 = (bf16[152,128]{1,0:T(8,128)(2,1)S(1)}, bf16[152,128]{1,0:T(8,128)(2,1)S(1)}, u32[]{:S(2)}, u32[]{:S(2)}) collective-permute-start(bf16[152,128]{1,0:T(8,128)(2,1)S(1)} %get-tuple-element.20), channel_id=1, source_target_pairs={{0,2},{1,3},{2,0},{3,1},{4,6},{5,7},{6,4},{7,5},{8,10},{9,11},{10,... | collective-permute-start | bytes 116744 | tf_op jit(solution)/shard_map/ppermute | solution.py:383
  9.4 5.4 %copy-start.6 = (bf16[16,21,21]{2,0,1:T(8,128)(2,1)S(1)}, bf16[16,21,21]{2,0,1:T(8,128)(2,1)}, u32[]{:S(2)}) copy-start(bf16[16,21,21]{2,0,1:T(8,128)(2,1)} %param.9) | copy-start | bytes 42340
  9.4 6.3 %collective-permute-start.8 = (bf16[200,128]{1,0:T(8,128)(2,1)S(1)}, bf16[200,128]{1,0:T(8,128)(2,1)S(1)}, u32[]{:S(2)}, u32[]{:S(2)}) collective-permute-start(bf16[200,128]{1,0:T(8,128)(2,1)S(1)} %get-tuple-element.19), channel_id=1, source_target_pairs={{0,10},{1,9},{2,8},{3,11},{4,14},{5,13},{6,12},{7,15},{8,2},{9,1},... | collective-permute-start | bytes 153608 | tf_op jit(solution)/shard_map/ppermute | solution.py:383
  11.3 2.2 %collective-permute-start.5 = (bf16[248,128]{1,0:T(8,128)(2,1)S(1)}, bf16[248,128]{1,0:T(8,128)(2,1)S(1)}, u32[]{:S(2)}, u32[]{:S(2)}) collective-permute-start(bf16[248,128]{1,0:T(8,128)(2,1)S(1)} %collective-permute-done.4.refs_0_.refs_1_), channel_id=1, source_target_pairs={{0,1},{1,0},{2,3},{3,2},{4,5},{5,4},{6,7},{7,6},{8,9},{9,8},{10,11... | collective-permute-start | bytes 190472 | tf_op jit(solution)/shard_map/ppermute | solution.py:387
  13.5 1.3 %collective-permute-start.7 = (bf16[248,128]{1,0:T(8,128)(2,1)S(1)}, bf16[248,128]{1,0:T(8,128)(2,1)S(1)}, u32[]{:S(2)}, u32[]{:S(2)}) collective-permute-start(bf16[248,128]{1,0:T(8,128)(2,1)S(1)} %collective-permute-done.6.refs_2_.refs_3_), channel_id=1, source_target_pairs={{0,1},{1,0},{2,3},{3,2},{4,5},{5,4},{6,7},{7,6},{8,9},{9,8},{10,11... | collective-permute-start | bytes 190472 | tf_op jit(solution)/shard_map/ppermute | solution.py:387
  14.8 2.3 %copy-start = (s32[16,16,384]{2,1,0:T(8,128)S(1)}, s32[16,16,384]{2,1,0:T(8,128)}, u32[]{:S(2)}) copy-start(s32[16,16,384]{2,1,0:T(8,128)} %refs_9_.1) | copy-start | bytes 1179652
  15.7 1.3 %copy-start.1 = (bf16[16,16,384]{2,1,0:T(8,128)(2,1)S(1)}, bf16[16,16,384]{2,1,0:T(8,128)(2,1)}, u32[]{:S(2)}) copy-start(bf16[16,16,384]{2,1,0:T(8,128)(2,1)} %refs_10_.1) | copy-start | bytes 589828
  15.7 1.3 %collective-permute-start.10 = (bf16[200,128]{1,0:T(8,128)(2,1)S(1)}, bf16[200,128]{1,0:T(8,128)(2,1)S(1)}, u32[]{:S(2)}, u32[]{:S(2)}) collective-permute-start(bf16[200,128]{1,0:T(8,128)(2,1)S(1)} %shard_map.78), channel_id=1, source_target_pairs={{0,1},{1,0},{2,3},{3,2},{4,5},{5,4},{6,7},{7,6},{8,9},{9,8},{10,11... | collective-permute-start | bytes 153608 | tf_op jit(solution)/shard_map/ppermute | solution.py:387

commit v6 on v5

--- a/solution.py
+++ b/solution.py
@@ -417,7 +417,7 @@
         blocks.append(block)
         if not isinstance(step, int):
             if step not in swapped:
-                swapped[step] = swap_cores(pass_on(block, basis))
+                swapped[step] = swap_cores(pass_on(block, near[-1]))
             blocks.append(swapped[step])
     return stack(kernels.shape[0], steps, blocks, basis, clip_mask, inv_var)
 

time: 18.6 us -> 18.1 us (0.973)
  waiting for transfers between devices: 5.76 us -> 5.45 us
  starting transfers between devices: 9.14 us -> 8.92 us
    ppermute x7, waiting for transfers between devices: 2.73 us -> 0.66 us  [swap_cores(): lax.ppermute(block, 'epoch', [(i, i ^ 1) for i in range(lax.axis_size('ep...]
    ppermute x4, waiting for transfers between devices: 3.04 us -> 4.79 us  [exchange(): lax.ppermute(block, 'epoch', [(i, i ^ 2 * apart[i % 2]) for i in range(co...]
    ppermute x7, starting transfers between devices: 1.25 us -> 1.03 us  [swap_cores(): lax.ppermute(block, 'epoch', [(i, i ^ 1) for i in range(lax.axis_size('ep...]
where the time goes in v6:
time: 18.1 us; the launch traced here: 17.9 us
  starting transfers between devices  8.92 us (49%)
  waiting for transfers between devices  5.45 us (30%)
  Pallas kernels  2.74 us (15%)
  local copies, waits for them, and re-layouts  0.72 us (4%)
    ppermute x4, starting transfers between devices, exchange(): lax.ppermute(block, 'epoch', [(i, i ^ 2 * apart[i % 2]) for i in range(co...  7.89 us
    ppermute x4, waiting for transfers between devices, exchange(): lax.ppermute(block, 'epoch', [(i, i ^ 2 * apart[i % 2]) for i in range(co...  4.79 us
    pallas_call x1, Pallas kernels, stack(): pl.pallas_call(functools.partial(stack_kernel, count, steps), out_shape=j...  1.4 us
    ppermute x7, starting transfers between devices, swap_cores(): lax.ppermute(block, 'epoch', [(i, i ^ 1) for i in range(lax.axis_size('ep...  1.03 us
    pallas_call x1, Pallas kernels, basis_rows(): pl.pallas_call(functools.partial(basis_kernel, slot, steps), out_shape=ja...  0.93 us
    unnamed x14, local copies, waits for them, and re-layouts  0.72 us
    ppermute x7, waiting for transfers between devices, swap_cores(): lax.ppermute(block, 'epoch', [(i, i ^ 1) for i in range(lax.axis_size('ep...  0.66 us
  transfers between devices with their start and end apart: 11, of which 6 were waited for; matrix products, arithmetic and copies ran while one was open for 0% of the time, Pallas kernels for 6%

profile of v6, /device:TPU:0, one launch (start us, length us, event | category | flops | bytes accessed | tf_op | source)
XLA Modules:
  0.0 17.9 jit_solution(11386449099390151673)
XLA Ops:
  0.0 0.0 copy-start.2
  0.0 0.5 %collective-permute-start = (bf16[1,256,384]{2,1,0:T(8,128)(2,1)}, bf16[1,256,384]{2,1,0:T(8,128)(2,1)S(1)}, u32[]{:S(2)}, u32[]{:S(2)}) collective-permute-start(bf16[1,256,384]{2,1,0:T(8,128)(2,1)} %param.7), channel_id=1, source_target_pairs={{0,1},{1,0},{2,3},{3,2},{4,5},{5,4},{6,7},{7,6},{8,9},{9,8},{10,11... | collective-permute-start | bytes 589832 | tf_op jit(solution)/shard_map/ppermute | solution.py:387
  0.5 0.1 collective-permute-start.2
  0.5 0.4 %collective-permute-start.1 = (f32[1,8,16]{2,1,0:T(8,128)}, f32[1,8,16]{2,1,0:T(8,128)S(1)}, u32[]{:S(2)}, u32[]{:S(2)}) collective-permute-start(f32[1,8,16]{2,1,0:T(8,128)} %param.10), channel_id=1, source_target_pairs={{0,1},{1,0},{2,3},{3,2},{4,5},{5,4},{6,7},{7,6},{8,9},{9,8},{10,11... | collective-permute-start | bytes 1544 | tf_op jit(solution)/shard_map/ppermute | solution.py:387
  1.0 0.1 collective-permute-start.3
  1.0 0.0 copy-start.3
  1.0 0.0 copy-start.4
  1.0 0.0 copy-start.5
  1.0 0.0 copy-done.2
  1.1 0.7 %copy-done.3 = bf16[16,384]{1,0:T(8,128)(2,1)S(1)} copy-done((bf16[16,384]{1,0:T(8,128)(2,1)S(1)}, bf16[16,384]{1,0:T(8,128)(2,1)}, u32[]{:S(2)}) %copy-start.3) | copy-done | bytes 12312
  1.7 0.0 copy-done.4
  1.7 0.0 copy-done.5
  1.7 0.2 %shard_map.74 = (bf16[8,2,16,384]{3,2,1,0:T(8,128)(2,1)S(1)}, bf16[16,384]{1,0:T(8,128)(2,1)S(1)}, f32[6,128]{1,0:T(8,128)S(1)}) custom-call(bf16[8,2,16,384]{3,2,1,0:T(8,128)(2,1)S(1)} %bitcast.7, bf16[16,384]{1,0:T(8,128)(2,1)S(1)} %copy-done.3, f32[8,16]{1,0:T(8,128)S(1)} %bitcast.9, s32[2,3]{1,0:T(2,128)S(1)} %bitcast.11, f32[8,128]{1,0:T(8,128)S(1)} %shard_map.73.first), custom_call_target="tpu_custom_call" | custom-call | bytes 1000000 | tf_op jit(solution)/shard_map/pallas_call | solution.py:88
  1.9 0.0 collective-permute-done.2
  1.9 0.1 collective-permute-done.1
  2.0 0.4 %collective-permute-done.3.pair_template.pair = bf16[16,384]{1,0:T(8,128)(2,1)S(1)} collective-permute-done((bf16[16,384]{1,0:T(8,128)(2,1)}, bf16[16,384]{1,0:T(8,128)(2,1)S(1)}, u32[]{:S(2)}, u32[]{:S(2)}) %collective-permute-start.3) | collective-permute-done | bytes 12320 | tf_op jit(solution)/shard_map/ppermute | solution.py:387
  2.4 0.0 collective-permute-done
  2.4 0.2 %shard_map.75 = (bf16[104,128]{1,0:T(8,128)(2,1)S(1)}, bf16[248,128]{1,0:T(8,128)(2,1)S(1)}, bf16[248,128]{1,0:T(8,128)(2,1)S(1)}, bf16[200,128]{1,0:T(8,128)(2,1)S(1)}, bf16[152,128]{1,0:T(8,128)(2,1)S(1)}) custom-call(bf16[8,2,16,384]{3,2,1,0:T(8,128)(2,1)S(1)} %get-tuple-element.13.own, bf16[8,2,16,384]{3,2,1,0:T(8,128)(2,1)S(1)} %bitcast.8, ...), custom_call_target="tpu_custom_call" | custom-call | bytes 500000 | tf_op jit(solution)/shard_map/pallas_call | solution.py:148
  2.6 5.8 %collective-permute-start.4 = (bf16[248,128]{1,0:T(8,128)(2,1)S(1)}, bf16[248,128]{1,0:T(8,128)(2,1)S(1)}, u32[]{:S(2)}, u32[]{:S(2)}) collective-permute-start(bf16[248,128]{1,0:T(8,128)(2,1)S(1)} %get-tuple-element.17), channel_id=1, source_target_pairs={{0,14},{1,13},{2,12},{3,15},{4,10},{5,9},{6,8},{7,11},{8,6},{9,5},... | collective-permute-start | bytes 190472 | tf_op jit(solution)/shard_map/ppermute | solution.py:383
  8.4 0.0 collective-permute-start.6
  8.4 1.0 %collective-permute-start.9 = (bf16[152,128]{1,0:T(8,128)(2,1)S(1)}, bf16[152,128]{1,0:T(8,128)(2,1)S(1)}, u32[]{:S(2)}, u32[]{:S(2)}) collective-permute-start(bf16[152,128]{1,0:T(8,128)(2,1)S(1)} %get-tuple-element.20), channel_id=1, source_target_pairs={{0,2},{1,3},{2,0},{3,1},{4,6},{5,7},{6,4},{7,5},{8,10},{9,11},{10,... | collective-permute-start | bytes 116744 | tf_op jit(solution)/shard_map/ppermute | solution.py:383
  9.4 1.1 %collective-permute-start.8 = (bf16[200,128]{1,0:T(8,128)(2,1)S(1)}, bf16[200,128]{1,0:T(8,128)(2,1)S(1)}, u32[]{:S(2)}, u32[]{:S(2)}) collective-permute-start(bf16[200,128]{1,0:T(8,128)(2,1)S(1)} %get-tuple-element.19), channel_id=1, source_target_pairs={{0,10},{1,9},{2,8},{3,11},{4,14},{5,13},{6,12},{7,15},{8,2},{9,1},... | collective-permute-start | bytes 153608 | tf_op jit(solution)/shard_map/ppermute | solution.py:383
  10.5 0.8 %collective-permute-done.4.refs_0_.refs_1_ = bf16[248,128]{1,0:T(8,128)(2,1)S(1)} collective-permute-done((bf16[248,128]{1,0:T(8,128)(2,1)S(1)}, bf16[248,128]{1,0:T(8,128)(2,1)S(1)}, u32[]{:S(2)}, u32[]{:S(2)}) %collective-permute-start.4) | collective-permute-done | bytes 63520 | tf_op jit(solution)/shard_map/ppermute | solution.py:383
  11.3 0.0 collective-permute-start.5
  11.3 2.2 %collective-permute-done.6.refs_2_.refs_3_ = bf16[248,128]{1,0:T(8,128)(2,1)S(1)} collective-permute-done((bf16[248,128]{1,0:T(8,128)(2,1)S(1)}, bf16[248,128]{1,0:T(8,128)(2,1)S(1)}, u32[]{:S(2)}, u32[]{:S(2)}) %collective-permute-start.6) | collective-permute-done | bytes 63520 | tf_op jit(solution)/shard_map/ppermute | solution.py:383
  13.5 0.0 collective-permute-start.7
  13.5 0.0 collective-permute-done.9.block.refs_7_
  13.5 0.0 copy-start.6
  13.5 1.8 %collective-permute-done.8.block.refs_5_ = bf16[200,128]{1,0:T(8,128)(2,1)S(1)} collective-permute-done((bf16[200,128]{1,0:T(8,128)(2,1)S(1)}, bf16[200,128]{1,0:T(8,128)(2,1)S(1)}, u32[]{:S(2)}, u32[]{:S(2)}) %collective-permute-start.8) | collective-permute-done | bytes 51232 | tf_op jit(solution)/shard_map/ppermute | solution.py:383
  15.3 0.0 collective-permute-start.10
  15.3 0.0 collective-permute-done.5.refs_1_.refs_2_
  15.3 0.0 collective-permute-done.7.refs_3_.refs_4_
  15.3 0.0 copy-done.6
  15.3 0.0 copy-start
  15.3 0.0 copy-start.1
  15.3 0.9 %shard_map.78.refs_8_ = bf16[256,384]{1,0:T(8,128)(2,1)S(1)} custom-call(bf16[21,16,21]{2,1,0:T(8,128)(2,1)S(1)} %bitcast.13, bf16[16,384]{1,0:T(8,128)(2,1)S(1)} %copy-done.3, bf16[16,384]{1,0:T(8,128)(2,1)S(1)} %collective-permute-done.3.pair_template.pair, bf16[248,128]{1,0:T(8,128)(2,1)S(1)} %collective-permute-done.4.refs_0_.refs_1_, ...), custom_call_target="tpu_custom_call" | custom-call | flops 226492416 | bytes 600000 | tf_op jit(solution)/shard_map/pallas_call | solution.py:257
  16.3 0.2 %collective-permute-done.10.refs_6_ = bf16[200,128]{1,0:T(8,128)(2,1)S(1)} collective-permute-done((bf16[200,128]{1,0:T(8,128)(2,1)S(1)}, bf16[200,128]{1,0:T(8,128)(2,1)S(1)}, u32[]{:S(2)}, u32[]{:S(2)}) %collective-permute-start.10) | collective-permute-done | bytes 51232 | tf_op jit(solution)/shard_map/ppermute | solution.py:387
  16.5 0.0 copy-done
  16.5 0.0 copy-done.1
  16.5 1.4 %shard_map.79 = f32[16,384]{1,0:T(8,128)} custom-call(bf16[104,128]{1,0:T(8,128)(2,1)S(1)} %get-tuple-element.16.refs_0_, bf16[248,128]{1,0:T(8,128)(2,1)S(1)} %collective-permute-done.4.refs_0_.refs_1_, bf16[248,128]{1,0:T(8,128)(2,1)S(1)} %collective-permute-done.5.refs_1_.refs_2_, bf16[248,128]{1,0:T(8,128)(2,1)S(1)} %collective-permute-done.6.refs_2_.refs_3_, ...), custom_call_target="tpu_custom_call" | custom-call | flops 9830400 | bytes 1000000 | tf_op jit(solution)/shard_map/pallas_call | solution.py:370
  (3 shorter events, 0.0 us)
Async XLA Ops:
  0.0 1.0 %copy-start.2 = (bf16[1,256,384]{2,1,0:T(8,128)(2,1)S(1)}, bf16[1,256,384]{2,1,0:T(8,128)(2,1)}, u32[]{:S(2)}) copy-start(bf16[1,256,384]{2,1,0:T(8,128)(2,1)} %param.7) | copy-start | bytes 589828
  0.0 2.4 %collective-permute-start = (bf16[1,256,384]{2,1,0:T(8,128)(2,1)}, bf16[1,256,384]{2,1,0:T(8,128)(2,1)S(1)}, u32[]{:S(2)}, u32[]{:S(2)}) collective-permute-start(bf16[1,256,384]{2,1,0:T(8,128)(2,1)} %param.7), channel_id=1, source_target_pairs={{0,1},{1,0},{2,3},{3,2},{4,5},{5,4},{6,7},{7,6},{8,9},{9,8},{10,11... | collective-permute-start | bytes 589832 | tf_op jit(solution)/shard_map/ppermute | solution.py:387
  0.5 1.5 %collective-permute-start.2 = (s32[1,2,3]{2,1,0:T(2,128)}, s32[1,2,3]{2,1,0:T(2,128)S(1)}, u32[]{:S(2)}, u32[]{:S(2)}) collective-permute-start(s32[1,2,3]{2,1,0:T(2,128)} %param.11), channel_id=1, source_target_pairs={{0,1},{1,0},{2,3},{3,2},{4,5},{5,4},{6,7},{7,6},{8,9},{9,8},{10,11... | collective-permute-start | bytes 80 | tf_op jit(solution)/shard_map/ppermute | solution.py:387
  0.5 1.5 %collective-permute-start.1 = (f32[1,8,16]{2,1,0:T(8,128)}, f32[1,8,16]{2,1,0:T(8,128)S(1)}, u32[]{:S(2)}, u32[]{:S(2)}) collective-permute-start(f32[1,8,16]{2,1,0:T(8,128)} %param.10), channel_id=1, source_target_pairs={{0,1},{1,0},{2,3},{3,2},{4,5},{5,4},{6,7},{7,6},{8,9},{9,8},{10,11... | collective-permute-start | bytes 1544 | tf_op jit(solution)/shard_map/ppermute | solution.py:387
  1.0 1.4 %collective-permute-start.3 = (bf16[16,384]{1,0:T(8,128)(2,1)}, bf16[16,384]{1,0:T(8,128)(2,1)S(1)}, u32[]{:S(2)}, u32[]{:S(2)}) collective-permute-start(bf16[16,384]{1,0:T(8,128)(2,1)} %own.1), channel_id=1, source_target_pairs={{0,1},{1,0},{2,3},{3,2},{4,5},{5,4},{6,7},{7,6},{8,9},{9,8},{10,11... | collective-permute-start | bytes 36872 | tf_op jit(solution)/shard_map/ppermute | solution.py:387
  1.0 0.7 %copy-start.3 = (bf16[16,384]{1,0:T(8,128)(2,1)S(1)}, bf16[16,384]{1,0:T(8,128)(2,1)}, u32[]{:S(2)}) copy-start(bf16[16,384]{1,0:T(8,128)(2,1)} %own.1) | copy-start | bytes 36868
  1.0 0.7 %copy-start.4 = (f32[1,8,16]{2,1,0:T(8,128)S(1)}, f32[1,8,16]{2,1,0:T(8,128)}, u32[]{:S(2)}) copy-start(f32[1,8,16]{2,1,0:T(8,128)} %param.10) | copy-start | bytes 1540
  1.0 0.7 %copy-start.5 = (s32[1,2,3]{2,1,0:T(2,128)S(1)}, s32[1,2,3]{2,1,0:T(2,128)}, u32[]{:S(2)}) copy-start(s32[1,2,3]{2,1,0:T(2,128)} %param.11) | copy-start | bytes 76
  2.6 8.7 %collective-permute-start.4 = (bf16[248,128]{1,0:T(8,128)(2,1)S(1)}, bf16[248,128]{1,0:T(8,128)(2,1)S(1)}, u32[]{:S(2)}, u32[]{:S(2)}) collective-permute-start(bf16[248,128]{1,0:T(8,128)(2,1)S(1)} %get-tuple-element.17), channel_id=1, source_target_pairs={{0,14},{1,13},{2,12},{3,15},{4,10},{5,9},{6,8},{7,11},{8,6},{9,5},... | collective-permute-start | bytes 190472 | tf_op jit(solution)/shard_map/ppermute | solution.py:383
  8.4 5.1 %collective-permute-start.6 = (bf16[248,128]{1,0:T(8,128)(2,1)S(1)}, bf16[248,128]{1,0:T(8,128)(2,1)S(1)}, u32[]{:S(2)}, u32[]{:S(2)}) collective-permute-start(bf16[248,128]{1,0:T(8,128)(2,1)S(1)} %get-tuple-element.18), channel_id=1, source_target_pairs={{0,6},{1,5},{2,4},{3,7},{4,2},{5,1},{6,0},{7,3},{8,14},{9,13},{10,... | collective-permute-start | bytes 190472 | tf_op jit(solution)/shard_map/ppermute | solution.py:383
  8.4 5.1 %collective-permute-start.9 = (bf16[152,128]{1,0:T(8,128)(2,1)S(1)}, bf16[152,128]{1,0:T(8,128)(2,1)S(1)}, u32[]{:S(2)}, u32[]{:S(2)}) collective-permute-start(bf16[152,128]{1,0:T(8,128)(2,1)S(1)} %get-tuple-element.20), channel_id=1, source_target_pairs={{0,2},{1,3},{2,0},{3,1},{4,6},{5,7},{6,4},{7,5},{8,10},{9,11},{10,... | collective-permute-start | bytes 116744 | tf_op jit(solution)/shard_map/ppermute | solution.py:383
  9.4 5.9 %collective-permute-start.8 = (bf16[200,128]{1,0:T(8,128)(2,1)S(1)}, bf16[200,128]{1,0:T(8,128)(2,1)S(1)}, u32[]{:S(2)}, u32[]{:S(2)}) collective-permute-start(bf16[200,128]{1,0:T(8,128)(2,1)S(1)} %get-tuple-element.19), channel_id=1, source_target_pairs={{0,10},{1,9},{2,8},{3,11},{4,14},{5,13},{6,12},{7,15},{8,2},{9,1},... | collective-permute-start | bytes 153608 | tf_op jit(solution)/shard_map/ppermute | solution.py:383
  11.3 4.0 %collective-permute-start.5 = (bf16[248,128]{1,0:T(8,128)(2,1)S(1)}, bf16[248,128]{1,0:T(8,128)(2,1)S(1)}, u32[]{:S(2)}, u32[]{:S(2)}) collective-permute-start(bf16[248,128]{1,0:T(8,128)(2,1)S(1)} %collective-permute-done.4.refs_0_.refs_1_), channel_id=1, source_target_pairs={{0,1},{1,0},{2,3},{3,2},{4,5},{5,4},{6,7},{7,6},{8,9},{9,8},{10,11... | collective-permute-start | bytes 190472 | tf_op jit(solution)/shard_map/ppermute | solution.py:387
  13.5 1.8 %collective-permute-start.7 = (bf16[248,128]{1,0:T(8,128)(2,1)S(1)}, bf16[248,128]{1,0:T(8,128)(2,1)S(1)}, u32[]{:S(2)}, u32[]{:S(2)}) collective-permute-start(bf16[248,128]{1,0:T(8,128)(2,1)S(1)} %collective-permute-done.6.refs_2_.refs_3_), channel_id=1, source_target_pairs={{0,1},{1,0},{2,3},{3,2},{4,5},{5,4},{6,7},{7,6},{8,9},{9,8},{10,11... | collective-permute-start | bytes 190472 | tf_op jit(solution)/shard_map/ppermute | solution.py:387
  13.5 1.8 %copy-start.6 = (bf16[16,21,21]{2,0,1:T(8,128)(2,1)S(1)}, bf16[16,21,21]{2,0,1:T(8,128)(2,1)}, u32[]{:S(2)}) copy-start(bf16[16,21,21]{2,0,1:T(8,128)(2,1)} %param.9) | copy-start | bytes 42340
  15.3 1.2 %collective-permute-start.10 = (bf16[200,128]{1,0:T(8,128)(2,1)S(1)}, bf16[200,128]{1,0:T(8,128)(2,1)S(1)}, u32[]{:S(2)}, u32[]{:S(2)}) collective-permute-start(bf16[200,128]{1,0:T(8,128)(2,1)S(1)} %shard_map.77), channel_id=1, source_target_pairs={{0,1},{1,0},{2,3},{3,2},{4,5},{5,4},{6,7},{7,6},{8,9},{9,8},{10,11... | collective-permute-start | bytes 153608 | tf_op jit(solution)/shard_map/ppermute | solution.py:387
  15.3 1.2 %copy-start = (s32[16,16,384]{2,1,0:T(8,128)S(1)}, s32[16,16,384]{2,1,0:T(8,128)}, u32[]{:S(2)}) copy-start(s32[16,16,384]{2,1,0:T(8,128)} %refs_9_.1) | copy-start | bytes 1179652
  15.3 1.2 %copy-start.1 = (bf16[16,16,384]{2,1,0:T(8,128)(2,1)S(1)}, bf16[16,16,384]{2,1,0:T(8,128)(2,1)}, u32[]{:S(2)}) copy-start(bf16[16,16,384]{2,1,0:T(8,128)(2,1)} %refs_10_.1) | copy-start | bytes 589828

commit v7 on v6

--- a/solution.py
+++ b/solution.py
@@ -168,7 +168,7 @@
         functools.partial(edge_kernel, first),
         out_shape=jax.ShapeDtypeStruct((rows, width), jnp.bfloat16),
         compiler_params=pltpu.CompilerParams(vmem_limit_bytes=VMEM_LIMIT),
-        cost_estimate=pl.CostEstimate(flops=1000000000, bytes_accessed=60_000, transcendentals=0),
+        cost_estimate=pl.CostEstimate(flops=10_000_000, bytes_accessed=60_000, transcendentals=0),
     )(block)
 
 

time: 18.1 us -> 17.4 us (0.961)
  waiting for transfers between devices: 5.45 us -> 4.78 us
    ppermute x4, waiting for transfers between devices: 4.79 us -> 4.09 us  [exchange(): lax.ppermute(block, 'epoch', [(i, i ^ 2 * apart[i % 2]) for i in range(co...]
  transfers between devices with their start and end apart: 11 -> 11, of which waited for: 6 -> 7; matrix products, arithmetic and copies ran while one was open for 0% -> 0% of each run, Pallas kernels for 6% -> 7%
where the time goes in v7:
time: 17.4 us; the launch traced here: 17.3 us
  starting transfers between devices  9 us (52%)
  waiting for transfers between devices  4.78 us (27%)
  Pallas kernels  2.74 us (16%)
  local copies, waits for them, and re-layouts  0.71 us (4%)
    ppermute x4, starting transfers between devices, exchange(): lax.ppermute(block, 'epoch', [(i, i ^ 2 * apart[i % 2]) for i in range(co...  7.9 us
    ppermute x4, waiting for transfers between devices, exchange(): lax.ppermute(block, 'epoch', [(i, i ^ 2 * apart[i % 2]) for i in range(co...  4.09 us
    pallas_call x1, Pallas kernels, stack(): pl.pallas_call(functools.partial(stack_kernel, count, steps), out_shape=j...  1.4 us
    ppermute x7, starting transfers between devices, swap_cores(): lax.ppermute(block, 'epoch', [(i, i ^ 1) for i in range(lax.axis_size('ep...  1.1 us
    pallas_call x1, Pallas kernels, basis_rows(): pl.pallas_call(functools.partial(basis_kernel, slot, steps), out_shape=ja...  0.93 us
    unnamed x14, local copies, waits for them, and re-layouts  0.71 us
    ppermute x7, waiting for transfers between devices, swap_cores(): lax.ppermute(block, 'epoch', [(i, i ^ 1) for i in range(lax.axis_size('ep...  0.69 us
  transfers between devices with their start and end apart: 11, of which 7 were waited for; matrix products, arithmetic and copies ran while one was open for 0% of the time, Pallas kernels for 7%

profile of v7, /device:TPU:0, one launch (start us, length us, event | category | flops | bytes accessed | tf_op | source)
XLA Modules:
  0.0 17.3 jit_solution(9407182847539429289)
XLA Ops:
  0.0 0.0 copy-start.2
  0.0 0.5 %collective-permute-start = (bf16[1,256,384]{2,1,0:T(8,128)(2,1)}, bf16[1,256,384]{2,1,0:T(8,128)(2,1)S(1)}, u32[]{:S(2)}, u32[]{:S(2)}) collective-permute-start(bf16[1,256,384]{2,1,0:T(8,128)(2,1)} %param.7), channel_id=1, source_target_pairs={{0,1},{1,0},{2,3},{3,2},{4,5},{5,4},{6,7},{7,6},{8,9},{9,8},{10,11... | collective-permute-start | bytes 589832 | tf_op jit(solution)/shard_map/ppermute | solution.py:387
  0.5 0.1 collective-permute-start.2
  0.5 0.4 %collective-permute-start.1 = (f32[1,8,16]{2,1,0:T(8,128)}, f32[1,8,16]{2,1,0:T(8,128)S(1)}, u32[]{:S(2)}, u32[]{:S(2)}) collective-permute-start(f32[1,8,16]{2,1,0:T(8,128)} %param.10), channel_id=1, source_target_pairs={{0,1},{1,0},{2,3},{3,2},{4,5},{5,4},{6,7},{7,6},{8,9},{9,8},{10,11... | collective-permute-start | bytes 1544 | tf_op jit(solution)/shard_map/ppermute | solution.py:387
  1.0 0.1 collective-permute-start.3
  1.0 0.0 copy-start.3
  1.0 0.0 copy-start.4
  1.0 0.0 copy-start.5
  1.0 0.0 copy-done.2
  1.1 0.7 %copy-done.3 = bf16[16,384]{1,0:T(8,128)(2,1)S(1)} copy-done((bf16[16,384]{1,0:T(8,128)(2,1)S(1)}, bf16[16,384]{1,0:T(8,128)(2,1)}, u32[]{:S(2)}) %copy-start.3) | copy-done | bytes 12312
  1.7 0.0 copy-done.4
  1.7 0.0 copy-done.5
  1.7 0.2 %shard_map.74 = (bf16[8,2,16,384]{3,2,1,0:T(8,128)(2,1)S(1)}, bf16[16,384]{1,0:T(8,128)(2,1)S(1)}, f32[6,128]{1,0:T(8,128)S(1)}) custom-call(bf16[8,2,16,384]{3,2,1,0:T(8,128)(2,1)S(1)} %bitcast.7, bf16[16,384]{1,0:T(8,128)(2,1)S(1)} %copy-done.3, f32[8,16]{1,0:T(8,128)S(1)} %bitcast.9, s32[2,3]{1,0:T(2,128)S(1)} %bitcast.11, f32[8,128]{1,0:T(8,128)S(1)} %shard_map.73.first), custom_call_target="tpu_custom_call" | custom-call | bytes 1000000 | tf_op jit(solution)/shard_map/pallas_call | solution.py:88
  1.9 0.0 collective-permute-done.2
  1.9 0.1 collective-permute-done.1
  2.0 0.4 %collective-permute-done.3.pair_template.pair = bf16[16,384]{1,0:T(8,128)(2,1)S(1)} collective-permute-done((bf16[16,384]{1,0:T(8,128)(2,1)}, bf16[16,384]{1,0:T(8,128)(2,1)S(1)}, u32[]{:S(2)}, u32[]{:S(2)}) %collective-permute-start.3) | collective-permute-done | bytes 12320 | tf_op jit(solution)/shard_map/ppermute | solution.py:387
  2.4 0.0 collective-permute-done
  2.4 0.2 %shard_map.75 = (bf16[104,128]{1,0:T(8,128)(2,1)S(1)}, bf16[248,128]{1,0:T(8,128)(2,1)S(1)}, bf16[248,128]{1,0:T(8,128)(2,1)S(1)}, bf16[200,128]{1,0:T(8,128)(2,1)S(1)}, bf16[152,128]{1,0:T(8,128)(2,1)S(1)}) custom-call(bf16[8,2,16,384]{3,2,1,0:T(8,128)(2,1)S(1)} %get-tuple-element.13.own, bf16[8,2,16,384]{3,2,1,0:T(8,128)(2,1)S(1)} %bitcast.8, ...), custom_call_target="tpu_custom_call" | custom-call | bytes 500000 | tf_op jit(solution)/shard_map/pallas_call | solution.py:148
  2.6 5.8 %collective-permute-start.4 = (bf16[248,128]{1,0:T(8,128)(2,1)S(1)}, bf16[248,128]{1,0:T(8,128)(2,1)S(1)}, u32[]{:S(2)}, u32[]{:S(2)}) collective-permute-start(bf16[248,128]{1,0:T(8,128)(2,1)S(1)} %get-tuple-element.17), channel_id=1, source_target_pairs={{0,14},{1,13},{2,12},{3,15},{4,10},{5,9},{6,8},{7,11},{8,6},{9,5},... | collective-permute-start | bytes 190472 | tf_op jit(solution)/shard_map/ppermute | solution.py:383
  8.4 0.0 copy-start.6
  8.4 0.0 collective-permute-start.6
  8.4 1.7 %collective-permute-start.8 = (bf16[200,128]{1,0:T(8,128)(2,1)S(1)}, bf16[200,128]{1,0:T(8,128)(2,1)S(1)}, u32[]{:S(2)}, u32[]{:S(2)}) collective-permute-start(bf16[200,128]{1,0:T(8,128)(2,1)S(1)} %get-tuple-element.19), channel_id=1, source_target_pairs={{0,10},{1,9},{2,8},{3,11},{4,14},{5,13},{6,12},{7,15},{8,2},{9,1},... | collective-permute-start | bytes 153608 | tf_op jit(solution)/shard_map/ppermute | solution.py:383
  10.0 0.4 %collective-permute-start.9 = (bf16[152,128]{1,0:T(8,128)(2,1)S(1)}, bf16[152,128]{1,0:T(8,128)(2,1)S(1)}, u32[]{:S(2)}, u32[]{:S(2)}) collective-permute-start(bf16[152,128]{1,0:T(8,128)(2,1)S(1)} %get-tuple-element.20), channel_id=1, source_target_pairs={{0,2},{1,3},{2,0},{3,1},{4,6},{5,7},{6,4},{7,5},{8,10},{9,11},{10,... | collective-permute-start | bytes 116744 | tf_op jit(solution)/shard_map/ppermute | solution.py:383
  10.5 0.8 %collective-permute-done.4.refs_0_.refs_1_ = bf16[248,128]{1,0:T(8,128)(2,1)S(1)} collective-permute-done((bf16[248,128]{1,0:T(8,128)(2,1)S(1)}, bf16[248,128]{1,0:T(8,128)(2,1)S(1)}, u32[]{:S(2)}, u32[]{:S(2)}) %collective-permute-start.4) | collective-permute-done | bytes 63520 | tf_op jit(solution)/shard_map/ppermute | solution.py:383
  11.3 0.0 collective-permute-start.5
  11.3 2.2 %collective-permute-done.6.refs_2_.refs_3_ = bf16[248,128]{1,0:T(8,128)(2,1)S(1)} collective-permute-done((bf16[248,128]{1,0:T(8,128)(2,1)S(1)}, bf16[248,128]{1,0:T(8,128)(2,1)S(1)}, u32[]{:S(2)}, u32[]{:S(2)}) %collective-permute-start.6) | collective-permute-done | bytes 63520 | tf_op jit(solution)/shard_map/ppermute | solution.py:383
  13.5 0.0 collective-permute-start.7
  13.5 1.1 %collective-permute-done.9.block.refs_7_ = bf16[152,128]{1,0:T(8,128)(2,1)S(1)} collective-permute-done((bf16[152,128]{1,0:T(8,128)(2,1)S(1)}, bf16[152,128]{1,0:T(8,128)(2,1)S(1)}, u32[]{:S(2)}, u32[]{:S(2)}) %collective-permute-start.9) | collective-permute-done | bytes 38944 | tf_op jit(solution)/shard_map/ppermute | solution.py:383
  14.6 0.0 collective-permute-done.8.block.refs_5_
  14.6 0.1 collective-permute-start.10
  14.7 0.0 collective-permute-done.5.refs_1_.refs_2_
  14.7 0.1 collective-permute-done.7.refs_3_.refs_4_
  14.8 0.0 copy-done.6
  14.8 0.0 copy-start
  14.8 0.0 copy-start.1
  14.8 0.9 %shard_map.78.refs_8_ = bf16[256,384]{1,0:T(8,128)(2,1)S(1)} custom-call(bf16[21,16,21]{2,1,0:T(8,128)(2,1)S(1)} %bitcast.13, bf16[16,384]{1,0:T(8,128)(2,1)S(1)} %copy-done.3, bf16[16,384]{1,0:T(8,128)(2,1)S(1)} %collective-permute-done.3.pair_template.pair, bf16[248,128]{1,0:T(8,128)(2,1)S(1)} %collective-permute-done.4.refs_0_.refs_1_, ...), custom_call_target="tpu_custom_call" | custom-call | flops 226492416 | bytes 600000 | tf_op jit(solution)/shard_map/pallas_call | solution.py:257
  15.7 0.2 %collective-permute-done.10.refs_6_ = bf16[200,128]{1,0:T(8,128)(2,1)S(1)} collective-permute-done((bf16[200,128]{1,0:T(8,128)(2,1)S(1)}, bf16[200,128]{1,0:T(8,128)(2,1)S(1)}, u32[]{:S(2)}, u32[]{:S(2)}) %collective-permute-start.10) | collective-permute-done | bytes 51232 | tf_op jit(solution)/shard_map/ppermute | solution.py:387
  15.9 0.0 copy-done
  15.9 0.0 copy-done.1
  15.9 1.4 %shard_map.79 = f32[16,384]{1,0:T(8,128)} custom-call(bf16[104,128]{1,0:T(8,128)(2,1)S(1)} %get-tuple-element.16.refs_0_, bf16[248,128]{1,0:T(8,128)(2,1)S(1)} %collective-permute-done.4.refs_0_.refs_1_, bf16[248,128]{1,0:T(8,128)(2,1)S(1)} %collective-permute-done.5.refs_1_.refs_2_, bf16[248,128]{1,0:T(8,128)(2,1)S(1)} %collective-permute-done.6.refs_2_.refs_3_, ...), custom_call_target="tpu_custom_call" | custom-call | flops 9830400 | bytes 1000000 | tf_op jit(solution)/shard_map/pallas_call | solution.py:370
  (3 shorter events, 0.0 us)
Async XLA Ops:
  0.0 1.0 %copy-start.2 = (bf16[1,256,384]{2,1,0:T(8,128)(2,1)S(1)}, bf16[1,256,384]{2,1,0:T(8,128)(2,1)}, u32[]{:S(2)}) copy-start(bf16[1,256,384]{2,1,0:T(8,128)(2,1)} %param.7) | copy-start | bytes 589828
  0.0 2.4 %collective-permute-start = (bf16[1,256,384]{2,1,0:T(8,128)(2,1)}, bf16[1,256,384]{2,1,0:T(8,128)(2,1)S(1)}, u32[]{:S(2)}, u32[]{:S(2)}) collective-permute-start(bf16[1,256,384]{2,1,0:T(8,128)(2,1)} %param.7), channel_id=1, source_target_pairs={{0,1},{1,0},{2,3},{3,2},{4,5},{5,4},{6,7},{7,6},{8,9},{9,8},{10,11... | collective-permute-start | bytes 589832 | tf_op jit(solution)/shard_map/ppermute | solution.py:387
  0.5 1.5 %collective-permute-start.2 = (s32[1,2,3]{2,1,0:T(2,128)}, s32[1,2,3]{2,1,0:T(2,128)S(1)}, u32[]{:S(2)}, u32[]{:S(2)}) collective-permute-start(s32[1,2,3]{2,1,0:T(2,128)} %param.11), channel_id=1, source_target_pairs={{0,1},{1,0},{2,3},{3,2},{4,5},{5,4},{6,7},{7,6},{8,9},{9,8},{10,11... | collective-permute-start | bytes 80 | tf_op jit(solution)/shard_map/ppermute | solution.py:387
  0.5 1.5 %collective-permute-start.1 = (f32[1,8,16]{2,1,0:T(8,128)}, f32[1,8,16]{2,1,0:T(8,128)S(1)}, u32[]{:S(2)}, u32[]{:S(2)}) collective-permute-start(f32[1,8,16]{2,1,0:T(8,128)} %param.10), channel_id=1, source_target_pairs={{0,1},{1,0},{2,3},{3,2},{4,5},{5,4},{6,7},{7,6},{8,9},{9,8},{10,11... | collective-permute-start | bytes 1544 | tf_op jit(solution)/shard_map/ppermute | solution.py:387
  1.0 1.4 %collective-permute-start.3 = (bf16[16,384]{1,0:T(8,128)(2,1)}, bf16[16,384]{1,0:T(8,128)(2,1)S(1)}, u32[]{:S(2)}, u32[]{:S(2)}) collective-permute-start(bf16[16,384]{1,0:T(8,128)(2,1)} %own.1), channel_id=1, source_target_pairs={{0,1},{1,0},{2,3},{3,2},{4,5},{5,4},{6,7},{7,6},{8,9},{9,8},{10,11... | collective-permute-start | bytes 36872 | tf_op jit(solution)/shard_map/ppermute | solution.py:387
  1.0 0.7 %copy-start.3 = (bf16[16,384]{1,0:T(8,128)(2,1)S(1)}, bf16[16,384]{1,0:T(8,128)(2,1)}, u32[]{:S(2)}) copy-start(bf16[16,384]{1,0:T(8,128)(2,1)} %own.1) | copy-start | bytes 36868
  1.0 0.7 %copy-start.4 = (f32[1,8,16]{2,1,0:T(8,128)S(1)}, f32[1,8,16]{2,1,0:T(8,128)}, u32[]{:S(2)}) copy-start(f32[1,8,16]{2,1,0:T(8,128)} %param.10) | copy-start | bytes 1540
  1.0 0.7 %copy-start.5 = (s32[1,2,3]{2,1,0:T(2,128)S(1)}, s32[1,2,3]{2,1,0:T(2,128)}, u32[]{:S(2)}) copy-start(s32[1,2,3]{2,1,0:T(2,128)} %param.11) | copy-start | bytes 76
  2.6 8.7 %collective-permute-start.4 = (bf16[248,128]{1,0:T(8,128)(2,1)S(1)}, bf16[248,128]{1,0:T(8,128)(2,1)S(1)}, u32[]{:S(2)}, u32[]{:S(2)}) collective-permute-start(bf16[248,128]{1,0:T(8,128)(2,1)S(1)} %get-tuple-element.17), channel_id=1, source_target_pairs={{0,14},{1,13},{2,12},{3,15},{4,10},{5,9},{6,8},{7,11},{8,6},{9,5},... | collective-permute-start | bytes 190472 | tf_op jit(solution)/shard_map/ppermute | solution.py:383
  8.4 6.4 %copy-start.6 = (bf16[16,21,21]{2,0,1:T(8,128)(2,1)S(1)}, bf16[16,21,21]{2,0,1:T(8,128)(2,1)}, u32[]{:S(2)}) copy-start(bf16[16,21,21]{2,0,1:T(8,128)(2,1)} %param.9) | copy-start | bytes 42340
  8.4 5.1 %collective-permute-start.6 = (bf16[248,128]{1,0:T(8,128)(2,1)S(1)}, bf16[248,128]{1,0:T(8,128)(2,1)S(1)}, u32[]{:S(2)}, u32[]{:S(2)}) collective-permute-start(bf16[248,128]{1,0:T(8,128)(2,1)S(1)} %get-tuple-element.18), channel_id=1, source_target_pairs={{0,6},{1,5},{2,4},{3,7},{4,2},{5,1},{6,0},{7,3},{8,14},{9,13},{10,... | collective-permute-start | bytes 190472 | tf_op jit(solution)/shard_map/ppermute | solution.py:383
  8.4 6.2 %collective-permute-start.8 = (bf16[200,128]{1,0:T(8,128)(2,1)S(1)}, bf16[200,128]{1,0:T(8,128)(2,1)S(1)}, u32[]{:S(2)}, u32[]{:S(2)}) collective-permute-start(bf16[200,128]{1,0:T(8,128)(2,1)S(1)} %get-tuple-element.19), channel_id=1, source_target_pairs={{0,10},{1,9},{2,8},{3,11},{4,14},{5,13},{6,12},{7,15},{8,2},{9,1},... | collective-permute-start | bytes 153608 | tf_op jit(solution)/shard_map/ppermute | solution.py:383
  10.0 4.5 %collective-permute-start.9 = (bf16[152,128]{1,0:T(8,128)(2,1)S(1)}, bf16[152,128]{1,0:T(8,128)(2,1)S(1)}, u32[]{:S(2)}, u32[]{:S(2)}) collective-permute-start(bf16[152,128]{1,0:T(8,128)(2,1)S(1)} %get-tuple-element.20), channel_id=1, source_target_pairs={{0,2},{1,3},{2,0},{3,1},{4,6},{5,7},{6,4},{7,5},{8,10},{9,11},{10,... | collective-permute-start | bytes 116744 | tf_op jit(solution)/shard_map/ppermute | solution.py:383
  11.3 3.4 %collective-permute-start.5 = (bf16[248,128]{1,0:T(8,128)(2,1)S(1)}, bf16[248,128]{1,0:T(8,128)(2,1)S(1)}, u32[]{:S(2)}, u32[]{:S(2)}) collective-permute-start(bf16[248,128]{1,0:T(8,128)(2,1)S(1)} %collective-permute-done.4.refs_0_.refs_1_), channel_id=1, source_target_pairs={{0,1},{1,0},{2,3},{3,2},{4,5},{5,4},{6,7},{7,6},{8,9},{9,8},{10,11... | collective-permute-start | bytes 190472 | tf_op jit(solution)/shard_map/ppermute | solution.py:387
  13.5 1.3 %collective-permute-start.7 = (bf16[248,128]{1,0:T(8,128)(2,1)S(1)}, bf16[248,128]{1,0:T(8,128)(2,1)S(1)}, u32[]{:S(2)}, u32[]{:S(2)}) collective-permute-start(bf16[248,128]{1,0:T(8,128)(2,1)S(1)} %collective-permute-done.6.refs_2_.refs_3_), channel_id=1, source_target_pairs={{0,1},{1,0},{2,3},{3,2},{4,5},{5,4},{6,7},{7,6},{8,9},{9,8},{10,11... | collective-permute-start | bytes 190472 | tf_op jit(solution)/shard_map/ppermute | solution.py:387
  14.6 1.3 %collective-permute-start.10 = (bf16[200,128]{1,0:T(8,128)(2,1)S(1)}, bf16[200,128]{1,0:T(8,128)(2,1)S(1)}, u32[]{:S(2)}, u32[]{:S(2)}) collective-permute-start(bf16[200,128]{1,0:T(8,128)(2,1)S(1)} %shard_map.77), channel_id=1, source_target_pairs={{0,1},{1,0},{2,3},{3,2},{4,5},{5,4},{6,7},{7,6},{8,9},{9,8},{10,11... | collective-permute-start | bytes 153608 | tf_op jit(solution)/shard_map/ppermute | solution.py:387
  14.8 1.1 %copy-start = (s32[16,16,384]{2,1,0:T(8,128)S(1)}, s32[16,16,384]{2,1,0:T(8,128)}, u32[]{:S(2)}) copy-start(s32[16,16,384]{2,1,0:T(8,128)} %refs_9_.1) | copy-start | bytes 1179652
  14.8 1.1 %copy-start.1 = (bf16[16,16,384]{2,1,0:T(8,128)(2,1)S(1)}, bf16[16,16,384]{2,1,0:T(8,128)(2,1)}, u32[]{:S(2)}) copy-start(bf16[16,16,384]{2,1,0:T(8,128)(2,1)} %refs_10_.1) | copy-start | bytes 589828

commit v8 on v7

--- a/solution.py
+++ b/solution.py
@@ -60,7 +60,7 @@
     cores = 1 if isinstance(step, int) else 2
     first = cores * 2 * columns * rows
     size = up(2 * columns, SUB)
-    tail = first + (columns * rows if with_template(step if cores == 1 else step[0]) else 0)
+    tail = first + (columns * rows if with_template(step if cores == 1 else step[1]) else 0)
     return first, tail, tail + size
 
 
@@ -124,7 +124,7 @@
             mine, other = own_template[...], pair_template[...]
             near = other.astype(jnp.float32)
             if not isinstance(step, int):
-                near = jnp.where(here < to, near, mine.astype(jnp.float32))
+                near = jnp.where(here < to, mine.astype(jnp.float32), near)
             for c in range(columns):
                 at = slice(c * CELL, (c + 1) * CELL)
                 block[edge + c * rows : edge + (c + 1) * rows] = near[:, at].astype(jnp.bfloat16)
@@ -209,8 +209,8 @@
                 continue
             lines = [block[at + c * rows : at + (c + 1) * rows] for c in range(columns)]
             found.append(jnp.concatenate([line.astype(jnp.float32) for line in lines], axis=1))
-        line = found[0] if len(found) == 1 else jnp.where(odd, found[1], found[0])
-        k = step if isinstance(step, int) else step[0]
+        line = found[0] if len(found) == 1 else jnp.where(odd, found[0], found[1])
+        k = step if isinstance(step, int) else step[1]
         far = jnp.where(here ^ k == want, line, far)
     low = jnp.where(odd, near, far)
     high = jnp.where(odd, far, near)
@@ -391,8 +391,8 @@
     rows, width = template.shape
     chips = lax.axis_size("epoch") // 2
     view = (chips, 2, rows, width)
-    pairs = [(k, k - 1) for k in range(chips - 1, 1, -2)]
-    pairs.sort(key=lambda step: not with_template(step[0]))
+    pairs = [(k - 1, k) for k in range(chips - 1, 1, -2)]
+    pairs.sort(key=lambda step: not with_template(step[1]))
     steps = [0] + pairs + [1]
     pair_science = swap_cores(science).reshape(view)
     pair_coef = swap_cores(coef)[0]
@@ -407,7 +407,7 @@
             first = block_rows(step, rows, width // CELL)[0]
             near.append(edge_rows(block, first, rows, width))
             near_steps.append(step)
-        elif with_template(step[0]):
+        elif with_template(step[1]):
             swapped[step] = swap_cores(block)
             near += [block, swapped[step]]
             near_steps.append(step)

time: 17.4 us -> 17.7 us (1.017)
  starting transfers between devices: 9 us -> 9.41 us
  waiting for transfers between devices: 4.78 us -> 4.51 us
    ppermute x7, starting transfers between devices: 1.1 us -> 2.28 us  [swap_cores(): lax.ppermute(block, 'epoch', [(i, i ^ 1) for i in range(lax.axis_size('ep...]
    ppermute x4, waiting for transfers between devices: 4.09 us -> 3.3 us  [exchange(): lax.ppermute(block, 'epoch', [(i, i ^ 2 * apart[i % 2]) for i in range(co...]
    ppermute x4, starting transfers between devices: 7.9 us -> 7.13 us  [exchange(): lax.ppermute(block, 'epoch', [(i, i ^ 2 * apart[i % 2]) for i in range(co...]
    ppermute x7, waiting for transfers between devices: 0.69 us -> 1.21 us  [swap_cores(): lax.ppermute(block, 'epoch', [(i, i ^ 1) for i in range(lax.axis_size('ep...]
  transfers between devices with their start and end apart: 11 -> 11, of which waited for: 7 -> 5; matrix products, arithmetic and copies ran while one was open for 0% -> 0% of each run, Pallas kernels for 7% -> 6%
where the time goes in v8:
time: 17.7 us; the launch traced here: 17.5 us
  starting transfers between devices  9.41 us (53%)
  waiting for transfers between devices  4.51 us (25%)
  Pallas kernels  2.74 us (15%)
  local copies, waits for them, and re-layouts  0.8 us (5%)
    ppermute x4, starting transfers between devices, exchange(): lax.ppermute(block, 'epoch', [(i, i ^ 2 * apart[i % 2]) for i in range(co...  7.13 us
    ppermute x4, waiting for transfers between devices, exchange(): lax.ppermute(block, 'epoch', [(i, i ^ 2 * apart[i % 2]) for i in range(co...  3.3 us
    ppermute x7, starting transfers between devices, swap_cores(): lax.ppermute(block, 'epoch', [(i, i ^ 1) for i in range(lax.axis_size('ep...  2.28 us
    pallas_call x1, Pallas kernels, stack(): pl.pallas_call(functools.partial(stack_kernel, count, steps), out_shape=j...  1.4 us
    ppermute x7, waiting for transfers between devices, swap_cores(): lax.ppermute(block, 'epoch', [(i, i ^ 1) for i in range(lax.axis_size('ep...  1.21 us
    pallas_call x1, Pallas kernels, basis_rows(): pl.pallas_call(functools.partial(basis_kernel, slot, steps), out_shape=ja...  0.93 us
    unnamed x14, local copies, waits for them, and re-layouts  0.8 us
  transfers between devices with their start and end apart: 11, of which 5 were waited for; matrix products, arithmetic and copies ran while one was open for 0% of the time, Pallas kernels for 6%

profile of v8, /device:TPU:0, one launch (start us, length us, event | category | flops | bytes accessed | tf_op | source)
XLA Modules:
  0.0 17.5 jit_solution(5159124875133945917)
XLA Ops:
  0.0 0.0 copy-start.2
  0.0 0.5 %collective-permute-start = (bf16[1,256,384]{2,1,0:T(8,128)(2,1)}, bf16[1,256,384]{2,1,0:T(8,128)(2,1)S(1)}, u32[]{:S(2)}, u32[]{:S(2)}) collective-permute-start(bf16[1,256,384]{2,1,0:T(8,128)(2,1)} %param.7), channel_id=1, source_target_pairs={{0,1},{1,0},{2,3},{3,2},{4,5},{5,4},{6,7},{7,6},{8,9},{9,8},{10,11... | collective-permute-start | bytes 589832 | tf_op jit(solution)/shard_map/ppermute | solution.py:387
  0.5 0.1 collective-permute-start.2
  0.5 0.4 %collective-permute-start.1 = (f32[1,8,16]{2,1,0:T(8,128)}, f32[1,8,16]{2,1,0:T(8,128)S(1)}, u32[]{:S(2)}, u32[]{:S(2)}) collective-permute-start(f32[1,8,16]{2,1,0:T(8,128)} %param.10), channel_id=1, source_target_pairs={{0,1},{1,0},{2,3},{3,2},{4,5},{5,4},{6,7},{7,6},{8,9},{9,8},{10,11... | collective-permute-start | bytes 1544 | tf_op jit(solution)/shard_map/ppermute | solution.py:387
  1.0 0.1 collective-permute-start.3
  1.0 0.0 copy-start.3
  1.0 0.0 copy-start.4
  1.0 0.0 copy-start.5
  1.0 0.0 copy-done.2
  1.1 0.7 %copy-done.3 = bf16[16,384]{1,0:T(8,128)(2,1)S(1)} copy-done((bf16[16,384]{1,0:T(8,128)(2,1)S(1)}, bf16[16,384]{1,0:T(8,128)(2,1)}, u32[]{:S(2)}) %copy-start.3) | copy-done | bytes 12312
  1.7 0.0 copy-done.4
  1.7 0.0 copy-done.5
  1.7 0.2 %shard_map.74 = (bf16[8,2,16,384]{3,2,1,0:T(8,128)(2,1)S(1)}, bf16[16,384]{1,0:T(8,128)(2,1)S(1)}, f32[6,128]{1,0:T(8,128)S(1)}) custom-call(bf16[8,2,16,384]{3,2,1,0:T(8,128)(2,1)S(1)} %bitcast.7, bf16[16,384]{1,0:T(8,128)(2,1)S(1)} %copy-done.3, f32[8,16]{1,0:T(8,128)S(1)} %bitcast.9, s32[2,3]{1,0:T(2,128)S(1)} %bitcast.11, f32[8,128]{1,0:T(8,128)S(1)} %shard_map.73.first), custom_call_target="tpu_custom_call" | custom-call | bytes 1000000 | tf_op jit(solution)/shard_map/pallas_call | solution.py:88
  1.9 0.0 collective-permute-done.2
  1.9 0.1 collective-permute-done.1
  2.0 0.4 %collective-permute-done.3.pair_template.pair = bf16[16,384]{1,0:T(8,128)(2,1)S(1)} collective-permute-done((bf16[16,384]{1,0:T(8,128)(2,1)}, bf16[16,384]{1,0:T(8,128)(2,1)S(1)}, u32[]{:S(2)}, u32[]{:S(2)}) %collective-permute-start.3) | collective-permute-done | bytes 12320 | tf_op jit(solution)/shard_map/ppermute | solution.py:387
  2.4 0.0 collective-permute-done
  2.4 0.2 %shard_map.75 = (bf16[104,128]{1,0:T(8,128)(2,1)S(1)}, bf16[248,128]{1,0:T(8,128)(2,1)S(1)}, bf16[248,128]{1,0:T(8,128)(2,1)S(1)}, bf16[200,128]{1,0:T(8,128)(2,1)S(1)}, bf16[152,128]{1,0:T(8,128)(2,1)S(1)}) custom-call(bf16[8,2,16,384]{3,2,1,0:T(8,128)(2,1)S(1)} %get-tuple-element.13.own, bf16[8,2,16,384]{3,2,1,0:T(8,128)(2,1)S(1)} %bitcast.8, ...), custom_call_target="tpu_custom_call" | custom-call | bytes 500000 | tf_op jit(solution)/shard_map/pallas_call | solution.py:148
  2.6 4.8 %collective-permute-start.4 = (bf16[248,128]{1,0:T(8,128)(2,1)S(1)}, bf16[248,128]{1,0:T(8,128)(2,1)S(1)}, u32[]{:S(2)}, u32[]{:S(2)}) collective-permute-start(bf16[248,128]{1,0:T(8,128)(2,1)S(1)} %get-tuple-element.17), channel_id=1, source_target_pairs={{0,12},{1,15},{2,14},{3,13},{4,8},{5,11},{6,10},{7,9},{8,4},{9,7},... | collective-permute-start | bytes 190472 | tf_op jit(solution)/shard_map/ppermute | solution.py:383
  7.4 0.0 copy-start.6
  7.4 0.0 collective-permute-start.6
  7.4 0.6 %collective-permute-start.8 = (bf16[200,128]{1,0:T(8,128)(2,1)S(1)}, bf16[200,128]{1,0:T(8,128)(2,1)S(1)}, u32[]{:S(2)}, u32[]{:S(2)}) collective-permute-start(bf16[200,128]{1,0:T(8,128)(2,1)S(1)} %get-tuple-element.19), channel_id=1, source_target_pairs={{0,8},{1,11},{2,10},{3,9},{4,12},{5,15},{6,14},{7,13},{8,0},{9,3},... | collective-permute-start | bytes 153608 | tf_op jit(solution)/shard_map/ppermute | solution.py:383
  8.1 1.7 %collective-permute-start.9 = (bf16[152,128]{1,0:T(8,128)(2,1)S(1)}, bf16[152,128]{1,0:T(8,128)(2,1)S(1)}, u32[]{:S(2)}, u32[]{:S(2)}) collective-permute-start(bf16[152,128]{1,0:T(8,128)(2,1)S(1)} %get-tuple-element.20), channel_id=1, source_target_pairs={{0,2},{1,3},{2,0},{3,1},{4,6},{5,7},{6,4},{7,5},{8,10},{9,11},{10,... | collective-permute-start | bytes 116744 | tf_op jit(solution)/shard_map/ppermute | solution.py:383
  9.7 0.2 %collective-permute-done.4.refs_0_.refs_1_ = bf16[248,128]{1,0:T(8,128)(2,1)S(1)} collective-permute-done((bf16[248,128]{1,0:T(8,128)(2,1)S(1)}, bf16[248,128]{1,0:T(8,128)(2,1)S(1)}, u32[]{:S(2)}, u32[]{:S(2)}) %collective-permute-start.4) | collective-permute-done | bytes 63520 | tf_op jit(solution)/shard_map/ppermute | solution.py:383
  9.9 0.4 %collective-permute-start.5 = (bf16[248,128]{1,0:T(8,128)(2,1)S(1)}, bf16[248,128]{1,0:T(8,128)(2,1)S(1)}, u32[]{:S(2)}, u32[]{:S(2)}) collective-permute-start(bf16[248,128]{1,0:T(8,128)(2,1)S(1)} %collective-permute-done.4.refs_0_.refs_1_), channel_id=1, source_target_pairs={{0,1},{1,0},{2,3},{3,2},{4,5},{5,4},{6,7},{7,6},{8,9},{9,8},{10,11... | collective-permute-start | bytes 190472 | tf_op jit(solution)/shard_map/ppermute | solution.py:387
  10.3 3.1 %collective-permute-done.6.refs_2_.refs_3_ = bf16[248,128]{1,0:T(8,128)(2,1)S(1)} collective-permute-done((bf16[248,128]{1,0:T(8,128)(2,1)S(1)}, bf16[248,128]{1,0:T(8,128)(2,1)S(1)}, u32[]{:S(2)}, u32[]{:S(2)}) %collective-permute-start.6) | collective-permute-done | bytes 63520 | tf_op jit(solution)/shard_map/ppermute | solution.py:383
  13.4 0.8 %collective-permute-start.7 = (bf16[248,128]{1,0:T(8,128)(2,1)S(1)}, bf16[248,128]{1,0:T(8,128)(2,1)S(1)}, u32[]{:S(2)}, u32[]{:S(2)}) collective-permute-start(bf16[248,128]{1,0:T(8,128)(2,1)S(1)} %collective-permute-done.6.refs_2_.refs_3_), channel_id=1, source_target_pairs={{0,1},{1,0},{2,3},{3,2},{4,5},{5,4},{6,7},{7,6},{8,9},{9,8},{10,11... | collective-permute-start | bytes 190472 | tf_op jit(solution)/shard_map/ppermute | solution.py:387
  14.2 0.0 collective-permute-done.9.block.refs_7_
  14.2 0.0 collective-permute-done.8.block.refs_5_
  14.2 0.1 collective-permute-start.10
  14.3 0.0 collective-permute-done.5.refs_1_.refs_2_
  14.3 0.8 %collective-permute-done.7.refs_3_.refs_4_ = bf16[248,128]{1,0:T(8,128)(2,1)S(1)} collective-permute-done((bf16[248,128]{1,0:T(8,128)(2,1)S(1)}, bf16[248,128]{1,0:T(8,128)(2,1)S(1)}, u32[]{:S(2)}, u32[]{:S(2)}) %collective-permute-start.7) | collective-permute-done | bytes 63520 | tf_op jit(solution)/shard_map/ppermute | solution.py:387
  15.1 0.0 copy-done.6
  15.1 0.0 copy-start
  15.1 0.0 copy-start.1
  15.1 0.9 %shard_map.78.refs_8_ = bf16[256,384]{1,0:T(8,128)(2,1)S(1)} custom-call(bf16[21,16,21]{2,1,0:T(8,128)(2,1)S(1)} %bitcast.13, bf16[16,384]{1,0:T(8,128)(2,1)S(1)} %copy-done.3, bf16[16,384]{1,0:T(8,128)(2,1)S(1)} %collective-permute-done.3.pair_template.pair, bf16[248,128]{1,0:T(8,128)(2,1)S(1)} %collective-permute-done.4.refs_0_.refs_1_, ...), custom_call_target="tpu_custom_call" | custom-call | flops 226492416 | bytes 600000 | tf_op jit(solution)/shard_map/pallas_call | solution.py:257
  16.0 0.0 collective-permute-done.10.refs_6_
  16.0 0.0 copy-done
  16.1 0.0 copy-done.1
  16.1 1.4 %shard_map.79 = f32[16,384]{1,0:T(8,128)} custom-call(bf16[104,128]{1,0:T(8,128)(2,1)S(1)} %get-tuple-element.16.refs_0_, bf16[248,128]{1,0:T(8,128)(2,1)S(1)} %collective-permute-done.4.refs_0_.refs_1_, bf16[248,128]{1,0:T(8,128)(2,1)S(1)} %collective-permute-done.5.refs_1_.refs_2_, bf16[248,128]{1,0:T(8,128)(2,1)S(1)} %collective-permute-done.6.refs_2_.refs_3_, ...), custom_call_target="tpu_custom_call" | custom-call | flops 9830400 | bytes 1000000 | tf_op jit(solution)/shard_map/pallas_call | solution.py:370
  (3 shorter events, 0.0 us)
Async XLA Ops:
  0.0 1.0 %copy-start.2 = (bf16[1,256,384]{2,1,0:T(8,128)(2,1)S(1)}, bf16[1,256,384]{2,1,0:T(8,128)(2,1)}, u32[]{:S(2)}) copy-start(bf16[1,256,384]{2,1,0:T(8,128)(2,1)} %param.7) | copy-start | bytes 589828
  0.0 2.4 %collective-permute-start = (bf16[1,256,384]{2,1,0:T(8,128)(2,1)}, bf16[1,256,384]{2,1,0:T(8,128)(2,1)S(1)}, u32[]{:S(2)}, u32[]{:S(2)}) collective-permute-start(bf16[1,256,384]{2,1,0:T(8,128)(2,1)} %param.7), channel_id=1, source_target_pairs={{0,1},{1,0},{2,3},{3,2},{4,5},{5,4},{6,7},{7,6},{8,9},{9,8},{10,11... | collective-permute-start | bytes 589832 | tf_op jit(solution)/shard_map/ppermute | solution.py:387
  0.5 1.5 %collective-permute-start.2 = (s32[1,2,3]{2,1,0:T(2,128)}, s32[1,2,3]{2,1,0:T(2,128)S(1)}, u32[]{:S(2)}, u32[]{:S(2)}) collective-permute-start(s32[1,2,3]{2,1,0:T(2,128)} %param.11), channel_id=1, source_target_pairs={{0,1},{1,0},{2,3},{3,2},{4,5},{5,4},{6,7},{7,6},{8,9},{9,8},{10,11... | collective-permute-start | bytes 80 | tf_op jit(solution)/shard_map/ppermute | solution.py:387
  0.5 1.5 %collective-permute-start.1 = (f32[1,8,16]{2,1,0:T(8,128)}, f32[1,8,16]{2,1,0:T(8,128)S(1)}, u32[]{:S(2)}, u32[]{:S(2)}) collective-permute-start(f32[1,8,16]{2,1,0:T(8,128)} %param.10), channel_id=1, source_target_pairs={{0,1},{1,0},{2,3},{3,2},{4,5},{5,4},{6,7},{7,6},{8,9},{9,8},{10,11... | collective-permute-start | bytes 1544 | tf_op jit(solution)/shard_map/ppermute | solution.py:387
  1.0 1.4 %collective-permute-start.3 = (bf16[16,384]{1,0:T(8,128)(2,1)}, bf16[16,384]{1,0:T(8,128)(2,1)S(1)}, u32[]{:S(2)}, u32[]{:S(2)}) collective-permute-start(bf16[16,384]{1,0:T(8,128)(2,1)} %own.1), channel_id=1, source_target_pairs={{0,1},{1,0},{2,3},{3,2},{4,5},{5,4},{6,7},{7,6},{8,9},{9,8},{10,11... | collective-permute-start | bytes 36872 | tf_op jit(solution)/shard_map/ppermute | solution.py:387
  1.0 0.7 %copy-start.3 = (bf16[16,384]{1,0:T(8,128)(2,1)S(1)}, bf16[16,384]{1,0:T(8,128)(2,1)}, u32[]{:S(2)}) copy-start(bf16[16,384]{1,0:T(8,128)(2,1)} %own.1) | copy-start | bytes 36868
  1.0 0.7 %copy-start.4 = (f32[1,8,16]{2,1,0:T(8,128)S(1)}, f32[1,8,16]{2,1,0:T(8,128)}, u32[]{:S(2)}) copy-start(f32[1,8,16]{2,1,0:T(8,128)} %param.10) | copy-start | bytes 1540
  1.0 0.7 %copy-start.5 = (s32[1,2,3]{2,1,0:T(2,128)S(1)}, s32[1,2,3]{2,1,0:T(2,128)}, u32[]{:S(2)}) copy-start(s32[1,2,3]{2,1,0:T(2,128)} %param.11) | copy-start | bytes 76
  2.6 7.3 %collective-permute-start.4 = (bf16[248,128]{1,0:T(8,128)(2,1)S(1)}, bf16[248,128]{1,0:T(8,128)(2,1)S(1)}, u32[]{:S(2)}, u32[]{:S(2)}) collective-permute-start(bf16[248,128]{1,0:T(8,128)(2,1)S(1)} %get-tuple-element.17), channel_id=1, source_target_pairs={{0,12},{1,15},{2,14},{3,13},{4,8},{5,11},{6,10},{7,9},{8,4},{9,7},... | collective-permute-start | bytes 190472 | tf_op jit(solution)/shard_map/ppermute | solution.py:383
  7.4 7.7 %copy-start.6 = (bf16[16,21,21]{2,0,1:T(8,128)(2,1)S(1)}, bf16[16,21,21]{2,0,1:T(8,128)(2,1)}, u32[]{:S(2)}) copy-start(bf16[16,21,21]{2,0,1:T(8,128)(2,1)} %param.9) | copy-start | bytes 42340
  7.4 6.0 %collective-permute-start.6 = (bf16[248,128]{1,0:T(8,128)(2,1)S(1)}, bf16[248,128]{1,0:T(8,128)(2,1)S(1)}, u32[]{:S(2)}, u32[]{:S(2)}) collective-permute-start(bf16[248,128]{1,0:T(8,128)(2,1)S(1)} %get-tuple-element.18), channel_id=1, source_target_pairs={{0,4},{1,7},{2,6},{3,5},{4,0},{5,3},{6,2},{7,1},{8,12},{9,15},{10,... | collective-permute-start | bytes 190472 | tf_op jit(solution)/shard_map/ppermute | solution.py:383
  7.4 6.8 %collective-permute-start.8 = (bf16[200,128]{1,0:T(8,128)(2,1)S(1)}, bf16[200,128]{1,0:T(8,128)(2,1)S(1)}, u32[]{:S(2)}, u32[]{:S(2)}) collective-permute-start(bf16[200,128]{1,0:T(8,128)(2,1)S(1)} %get-tuple-element.19), channel_id=1, source_target_pairs={{0,8},{1,11},{2,10},{3,9},{4,12},{5,15},{6,14},{7,13},{8,0},{9,3},... | collective-permute-start | bytes 153608 | tf_op jit(solution)/shard_map/ppermute | solution.py:383
  8.1 6.1 %collective-permute-start.9 = (bf16[152,128]{1,0:T(8,128)(2,1)S(1)}, bf16[152,128]{1,0:T(8,128)(2,1)S(1)}, u32[]{:S(2)}, u32[]{:S(2)}) collective-permute-start(bf16[152,128]{1,0:T(8,128)(2,1)S(1)} %get-tuple-element.20), channel_id=1, source_target_pairs={{0,2},{1,3},{2,0},{3,1},{4,6},{5,7},{6,4},{7,5},{8,10},{9,11},{10,... | collective-permute-start | bytes 116744 | tf_op jit(solution)/shard_map/ppermute | solution.py:383
  9.9 4.4 %collective-permute-start.5 = (bf16[248,128]{1,0:T(8,128)(2,1)S(1)}, bf16[248,128]{1,0:T(8,128)(2,1)S(1)}, u32[]{:S(2)}, u32[]{:S(2)}) collective-permute-start(bf16[248,128]{1,0:T(8,128)(2,1)S(1)} %collective-permute-done.4.refs_0_.refs_1_), channel_id=1, source_target_pairs={{0,1},{1,0},{2,3},{3,2},{4,5},{5,4},{6,7},{7,6},{8,9},{9,8},{10,11... | collective-permute-start | bytes 190472 | tf_op jit(solution)/shard_map/ppermute | solution.py:387
  13.4 1.7 %collective-permute-start.7 = (bf16[248,128]{1,0:T(8,128)(2,1)S(1)}, bf16[248,128]{1,0:T(8,128)(2,1)S(1)}, u32[]{:S(2)}, u32[]{:S(2)}) collective-permute-start(bf16[248,128]{1,0:T(8,128)(2,1)S(1)} %collective-permute-done.6.refs_2_.refs_3_), channel_id=1, source_target_pairs={{0,1},{1,0},{2,3},{3,2},{4,5},{5,4},{6,7},{7,6},{8,9},{9,8},{10,11... | collective-permute-start | bytes 190472 | tf_op jit(solution)/shard_map/ppermute | solution.py:387
  14.2 1.8 %collective-permute-start.10 = (bf16[200,128]{1,0:T(8,128)(2,1)S(1)}, bf16[200,128]{1,0:T(8,128)(2,1)S(1)}, u32[]{:S(2)}, u32[]{:S(2)}) collective-permute-start(bf16[200,128]{1,0:T(8,128)(2,1)S(1)} %shard_map.77), channel_id=1, source_target_pairs={{0,1},{1,0},{2,3},{3,2},{4,5},{5,4},{6,7},{7,6},{8,9},{9,8},{10,11... | collective-permute-start | bytes 153608 | tf_op jit(solution)/shard_map/ppermute | solution.py:387
  15.1 1.0 %copy-start = (s32[16,16,384]{2,1,0:T(8,128)S(1)}, s32[16,16,384]{2,1,0:T(8,128)}, u32[]{:S(2)}) copy-start(s32[16,16,384]{2,1,0:T(8,128)} %refs_9_.1) | copy-start | bytes 1179652
  15.1 1.0 %copy-start.1 = (bf16[16,16,384]{2,1,0:T(8,128)(2,1)S(1)}, bf16[16,16,384]{2,1,0:T(8,128)(2,1)}, u32[]{:S(2)}) copy-start(bf16[16,16,384]{2,1,0:T(8,128)(2,1)} %refs_10_.1) | copy-start | bytes 589828
